TPU v7x, 32 devices: a whole 2x2x4 slice. The times are simulated.
32 devices in a mesh: groups: 2 (over y), seq: 16 (over z, x, core).
Axes of the slice: x: 2, y: 2, z: 4, core: 2. Of those that a mesh axis runs over, the one named last changes fastest.
Arguments:
- residual: bfloat16 [8192, 1024], P(('groups', 'seq')), parts along dimension 0, may hold values from -6 to 6
- layer_queries: bfloat16 [8192, 512], P(('groups', 'seq')), parts along dimension 0, may hold values from -200 to 200
- layer_keyvals: bfloat16 [8192, 256], P(('groups', 'seq')), parts along dimension 0, may hold values from -8 to 8
- head_window_extent: int32 [8], replicated, may hold values from 32 to 256, as said below
- block_mask: int32 [16, 4], P('seq'), may hold values 0 or 1
- first_out: bfloat16 [512, 1024], replicated, may hold values from -1 to 1
- second_query: bfloat16 [1024, 512], replicated, may hold values from -12 to 12
- second_keyval: bfloat16 [1024, 256], replicated, may hold values from -1 to 1
- second_out: bfloat16 [512, 1024], replicated, may hold values from -1 to 1
Outputs:
- layer_output: bfloat16 [8192, 1024], P(('groups', 'seq')), parts along dimension 0
There are 2 independent parts, one for each index of `groups`. A program takes and returns all parts, laid end to end along the dimension named above; an argument that names none is the same for every part. Nothing has to cross between parts.
Inputs may be any that keep to these rules, and one draw needn't show every extreme that they name: `head_window_extent`: per head; some head has exactly 256 and some exactly 32.
All inputs are finite; a program needn't handle non-finite values. No bound on the sum of `block_mask` on one device may be relied on, other than what follows from the above.
Results may differ from a plain program's by a relative error of at most 0.0065.
Values may be sent and summed in bfloat16 or wider, within the bound.
No kernel may reach another device: no remote copies, remote signals or barrier semaphores. Data moves between devices by JAX's collectives and lax.ppermute only.
A program may use at most 64 MiB of HBM per device.

v0:
```python
import jax
import jax.numpy as jnp
from jax import lax
from jax.sharding import PartitionSpec as P

QUERY_HEADS = 8
HEAD_SIZE = 64
WIN = 256


def with_halo(cells, sides, width):
    for axis, dim in sides:
        count = lax.axis_size(axis)
        ends = count - 1
        head = lax.slice_in_dim(cells, 0, width, axis=dim)
        tail = lax.slice_in_dim(cells, cells.shape[dim] - width, cells.shape[dim], axis=dim)
        cells = jnp.concatenate(
            [
                lax.ppermute(tail, axis, [(i, (i + 1) % count) for i in range(ends)]),
                cells,
                lax.ppermute(head, axis, [((i + 1) % count, i) for i in range(ends)]),
            ],
            axis=dim,
        )
    return cells


def swapped(block, axis, stride):
    count = lax.axis_size(axis)
    route = []
    for low in range(count):
        high = low | 1 << stride
        if high != low and high < count:
            route += [(low, high), (high, low)]
    return lax.ppermute(block, axis, route)


def norm_rows(hidden):
    values = hidden.astype(jnp.float32)
    scale = lax.rsqrt(jnp.mean(values * values, axis=-1, keepdims=True) + 1e-05)
    return (values * scale).astype(jnp.bfloat16)


def attend_rows(query_matrix, key_row_matrix, value_row_matrix, allowed):
    count_of_rows = query_matrix.shape[0]
    count_of_keys = key_row_matrix.shape[0]
    kv_heads = key_row_matrix.shape[1] // HEAD_SIZE
    heads_per_group = query_matrix.shape[1] // (kv_heads * HEAD_SIZE)
    query_head_rows = query_matrix.reshape(count_of_rows, kv_heads, heads_per_group, HEAD_SIZE)
    key_head_rows = key_row_matrix.reshape(count_of_keys, kv_heads, HEAD_SIZE)
    value_head_rows = value_row_matrix.reshape(count_of_keys, kv_heads, HEAD_SIZE)
    scores = jnp.einsum(
        "rkgd,jkd->kgrj", query_head_rows, key_head_rows, preferred_element_type=jnp.float32
    ) * HEAD_SIZE ** (-0.5)
    scores = jnp.where(allowed, scores, -1e30)
    row_max = jnp.max(scores, axis=-1, keepdims=True)
    weights = jnp.where(allowed, jnp.exp(scores - row_max), 0.0)
    shares = (weights / jnp.sum(weights, axis=-1, keepdims=True)).astype(jnp.bfloat16)
    mixture = jnp.einsum(
        "kgrj,jkd->rkgd", shares, value_head_rows, preferred_element_type=jnp.float32
    )
    return mixture.reshape(count_of_rows, query_matrix.shape[1]).astype(jnp.bfloat16)


def attend_groups(query_matrix, key_row_matrix, value_row_matrix, key_allowed):
    count_of_rows = query_matrix.shape[0]
    count_of_keys = key_row_matrix.shape[0]
    kv_heads = key_row_matrix.shape[1] // HEAD_SIZE
    heads_per_group = query_matrix.shape[1] // (kv_heads * HEAD_SIZE)
    query_head_rows = jnp.moveaxis(
        query_matrix.reshape(count_of_rows, kv_heads, heads_per_group, HEAD_SIZE), 2, 0
    )
    key_head_rows = key_row_matrix.reshape(count_of_keys, kv_heads, HEAD_SIZE)
    value_head_rows = value_row_matrix.reshape(count_of_keys, kv_heads, HEAD_SIZE)
    allowed = key_allowed[None, None, :]

    def one_group(q_group):
        scores = jnp.einsum(
            "rkd,jkd->krj", q_group, key_head_rows, preferred_element_type=jnp.float32
        ) * HEAD_SIZE ** (-0.5)
        scores = jnp.where(allowed, scores, -1e30)
        row_max = jnp.max(scores, axis=-1, keepdims=True)
        weights = jnp.where(allowed, jnp.exp(scores - row_max), 0.0)
        shares = (weights / jnp.sum(weights, axis=-1, keepdims=True)).astype(jnp.bfloat16)
        return jnp.einsum(
            "krj,jkd->rkd", shares, value_head_rows, preferred_element_type=jnp.float32
        ).astype(jnp.bfloat16)

    mixture = lax.map(one_group, query_head_rows)
    return jnp.moveaxis(mixture, 0, 2).reshape(count_of_rows, query_matrix.shape[1])


def shards(
    residual,
    layer_queries,
    layer_keyvals,
    head_window_extent,
    block_mask,
    first_out,
    second_query,
    second_keyval,
    second_out,
):
    local_rows = residual.shape[0]
    key_value_width = layer_keyvals.shape[1] // 2
    kv_heads = key_value_width // HEAD_SIZE
    heads_per_group = QUERY_HEADS // kv_heads
    block_rows = min(local_rows, 512)
    block_count = local_rows // block_rows
    extended = with_halo(layer_keyvals, (("seq", 0),), WIN)
    start_row = lax.axis_index("seq") * local_rows
    total_rows = lax.axis_size("seq") * local_rows
    window_extent = head_window_extent.reshape(kv_heads, heads_per_group, 1, 1)

    def window_block(block_index):
        first_row = block_index * block_rows
        query_pos = start_row + first_row + jnp.arange(block_rows, dtype=jnp.int32)
        key_pos = start_row - WIN + first_row + jnp.arange(block_rows + 2 * WIN, dtype=jnp.int32)
        inside = (key_pos >= 0) & (key_pos < total_rows)
        distance = jnp.abs(query_pos[:, None] - key_pos[None, :])
        allowed = (distance[None, None] <= window_extent) & inside[None, None, None, :]
        return attend_rows(
            layer_queries, extended[:, :key_value_width], extended[:, key_value_width:], allowed
        )

    attended = lax.map(window_block, jnp.arange(block_count, dtype=jnp.int32)).reshape(
        local_rows, -1
    )
    hidden = (
        jnp.dot(attended, first_out, preferred_element_type=jnp.float32)
        + residual.astype(jnp.float32)
    ).astype(jnp.bfloat16)
    normed = norm_rows(hidden)
    queries_two = jnp.dot(normed, second_query, preferred_element_type=jnp.float32).astype(
        jnp.bfloat16
    )
    keyvals_two = jnp.dot(normed, second_keyval, preferred_element_type=jnp.float32).astype(
        jnp.bfloat16
    )
    level_count = lax.axis_size("seq").bit_length() - 1
    levels = list(range(level_count))
    key_blocks = [keyvals_two]
    key_flags = [jnp.ones((), jnp.bool_)]
    for level in levels:
        key_blocks.append(swapped(keyvals_two, "seq", level))
        key_flags.append(block_mask[0, level] == 1)
    all_keys = jnp.concatenate(key_blocks, axis=0)
    key_allowed = jnp.repeat(jnp.stack(key_flags), local_rows)

    def butterfly_block(block_index):
        return attend_groups(
            queries_two, all_keys[:, :key_value_width], all_keys[:, key_value_width:], key_allowed
        )

    second = lax.map(butterfly_block, jnp.arange(block_count, dtype=jnp.int32)).reshape(
        local_rows, -1
    )
    output = jnp.dot(second, second_out, preferred_element_type=jnp.float32) + hidden.astype(
        jnp.float32
    )
    return output.astype(jnp.bfloat16)


def solution(mesh):
    placed = (
        P(("groups", "seq"), None),
        P(("groups", "seq"), None),
        P(("groups", "seq"), None),
        P(),
        P("seq", None),
        P(),
        P(),
        P(),
        P(),
    )
    return jax.shard_map(
        shards, mesh=mesh, in_specs=placed, out_specs=P(("groups", "seq"), None), check_vma=False
    )
```

profile of v0, /device:TPU:0, one launch (start us, length us, event | category | flops | bytes accessed | tf_op | source)
XLA Modules:
  0.0 63.5 jit_solution(9689028794966576870)
XLA Ops:
  0.0 2.5 %collective-permute-start = (bf16[256,256]{1,0:T(8,128)(2,1)}, bf16[256,256]{1,0:T(8,128)(2,1)S(1)}, u32[]{:S(2)}, u32[]{:S(2)}) collective-permute-start(bf16[256,256]{1,0:T(8,128)(2,1)} %param.13), channel_id=1, source_target_pairs={{0,1},{1,2},{2,3},{3,4},{4,5},{5,6},{6,7},{7,8},{8,9},{9,10},{10,1... | collective-permute-start | bytes 393224 | tf_op jit(solution)/shard_map/ppermute | solution.py:19
  2.5 1.3 %collective-permute-start.1 = (bf16[256,256]{1,0:T(8,128)(2,1)}, bf16[256,256]{1,0:T(8,128)(2,1)S(1)}, u32[]{:S(2)}, u32[]{:S(2)}) collective-permute-start(bf16[256,256]{1,0:T(8,128)(2,1)} %param.13), channel_id=1, source_target_pairs={{1,0},{2,1},{3,2},{4,3},{5,4},{6,5},{7,6},{8,7},{9,8},{10,9},{11,1... | collective-permute-start | bytes 393224 | tf_op jit(solution)/shard_map/ppermute | solution.py:21
  4.0 1.5 %fusion.49 = (s32[1,1]{1,0:T(1,128)}, s32[1,1]{1,0:T(1,128)}, s32[1,1]{1,0:T(1,128)}, s32[1,1]{1,0:T(1,128)}) fusion(s32[1,4]{1,0:T(1,128)} %param.15), kind=kLoop, calls=%fused_computation.63 | loop fusion | bytes 32 | tf_op jit(solution)/shard_map/slice | solution.py:146
  6.2 1.1 %copy.19 = bf16[256,512]{0,1:T(8,128)(2,1)S(1)} copy(bf16[256,512]{1,0:T(8,128)(2,1)} %param.12) | data formatting | bytes 524288 | tf_op args[1]
  10.0 0.9 %constant_dynamic-update-slice_fusion.1 = bf16[768,256]{1,0:T(8,128)(2,1)S(1)} fusion(bf16[768,256]{1,0:T(8,128)(2,1)S(1)} %constant_dynamic-update-slice_fusion.2, bf16[256,256]{1,0:T(8,128)(2,1)} %param.13), kind=kLoop, calls=%fused_computation.47 | loop fusion | bytes 262144
  11.3 6.6 %fusion.50 = (f32[2,4,256]{2,1,0:T(4,128)S(1)}, f32[2,4,256,768]{2,3,1,0:T(8,128)}) fusion(s32[2,4]{1,0:T(2,128)S(1)} %le.23, s32[256,768]{0,1:T(8,128)S(1)} %subtract_abs_fusion, pred[768]{0:T(1024)(128)(4,1)S(1)} %compare_and_fusion.1, bf16[768,2,64,1]{0,2,3,1:T(8,128)(2,1)S(1)} %bitcast.78, bf16[256,2,4,64]{0,3,2,1:T(8,128)(2,1)S(1)} %bitcast.76), kind=kOutput, calls=%fused_computation.64 | convolution fusion | flops 215483136 | bytes 7545632 | tf_op jit(solution)/shard_map/while/body/eval_jaxpr/sub | solution.py:57
  17.9 3.5 %fusion.35 = bf16[2,64,4,256]{3,1,2,0:T(8,128)(2,1)S(1)} fusion(bf16[768,2,64,1]{0,2,3,1:T(8,128)(2,1)S(1)} %bitcast.77, f32[2,4,256,768]{2,3,1,0:T(8,128)} %get-tuple-element.121, f32[2,4,256]{2,1,0:T(4,128)S(1)} %get-tuple-element.120), kind=kOutput, calls=%fused_computation.39 | convolution fusion | flops 204603392 | bytes 6758400 | tf_op jit(solution)/shard_map/while/body/eval_jaxpr/kgrj,jkd->rkgd/dot_general | solution.py:59
  22.8 3.3 %collective-permute-start.2 = (bf16[256,256]{1,0:T(8,128)(2,1)S(1)}, bf16[256,256]{1,0:T(8,128)(2,1)S(1)}, u32[]{:S(2)}, u32[]{:S(2)}) collective-permute-start(bf16[256,256]{1,0:T(8,128)(2,1)S(1)} %get-tuple-element.125), channel_id=1, source_target_pairs={{0,1},{1,0},{2,3},{3,2},{4,5},{5,4},{6,7},{7,6},{8,9},{9,8},{10,11... | collective-permute-start | bytes 393224 | tf_op jit(solution)/shard_map/ppermute | solution.py:35
  26.1 1.7 %collective-permute-start.3 = (bf16[256,256]{1,0:T(8,128)(2,1)S(1)}, bf16[256,256]{1,0:T(8,128)(2,1)S(1)}, u32[]{:S(2)}, u32[]{:S(2)}) collective-permute-start(bf16[256,256]{1,0:T(8,128)(2,1)S(1)} %get-tuple-element.125), channel_id=1, source_target_pairs={{0,2},{2,0},{1,3},{3,1},{4,6},{6,4},{5,7},{7,5},{8,10},{10,8},{9,1... | collective-permute-start | bytes 393224 | tf_op jit(solution)/shard_map/ppermute | solution.py:35
  27.8 1.6 %collective-permute-start.4 = (bf16[256,256]{1,0:T(8,128)(2,1)S(1)}, bf16[256,256]{1,0:T(8,128)(2,1)S(1)}, u32[]{:S(2)}, u32[]{:S(2)}) collective-permute-start(bf16[256,256]{1,0:T(8,128)(2,1)S(1)} %get-tuple-element.125), channel_id=1, source_target_pairs={{0,4},{4,0},{1,5},{5,1},{2,6},{6,2},{3,7},{7,3},{8,12},{12,8},{9,1... | collective-permute-start | bytes 393224 | tf_op jit(solution)/shard_map/ppermute | solution.py:35
  29.4 2.6 %collective-permute-start.5 = (bf16[256,256]{1,0:T(8,128)(2,1)S(1)}, bf16[256,256]{1,0:T(8,128)(2,1)S(1)}, u32[]{:S(2)}, u32[]{:S(2)}) collective-permute-start(bf16[256,256]{1,0:T(8,128)(2,1)S(1)} %get-tuple-element.125), channel_id=1, source_target_pairs={{0,8},{8,0},{1,9},{9,1},{2,10},{10,2},{3,11},{11,3},{4,12},{12,4},... | collective-permute-start | bytes 393224 | tf_op jit(solution)/shard_map/ppermute | solution.py:35
  32.4 0.8 %copy.21 = bf16[256,512]{0,1:T(8,128)(2,1)} copy(bf16[256,512]{1,0:T(8,128)(2,1)S(1)} %convolution_convert_fusion) | data formatting | bytes 524288 | tf_op jit(solution)/shard_map/convert_element_type | solution.py:134
  33.3 2.4 %collective-permute-done.4 = bf16[256,256]{1,0:T(8,128)(2,1)S(1)} collective-permute-done((bf16[256,256]{1,0:T(8,128)(2,1)S(1)}, bf16[256,256]{1,0:T(8,128)(2,1)S(1)}, u32[]{:S(2)}, u32[]{:S(2)}) %collective-permute-start.4) | collective-permute-done | bytes 131104 | tf_op jit(solution)/shard_map/ppermute | solution.py:35
  35.8 2.7 %collective-permute-done.5 = bf16[256,256]{1,0:T(8,128)(2,1)S(1)} collective-permute-done((bf16[256,256]{1,0:T(8,128)(2,1)S(1)}, bf16[256,256]{1,0:T(8,128)(2,1)S(1)}, u32[]{:S(2)}, u32[]{:S(2)}) %collective-permute-start.5) | collective-permute-done | bytes 131104 | tf_op jit(solution)/shard_map/ppermute | solution.py:35
  38.9 23.3 %while.14 = (s32[]{:T(128)}, bf16[4,256,2,64]{1,3,0,2:T(8,128)(2,1)S(1)}, bf16[4,256,2,64]{1,3,0,2:T(8,128)(2,1)}, bf16[1280,2,64]{0,2,1:T(8,128)(2,1)S(1)}, bf1...) while((s32[]{:T(128)}, bf16[4,256,2,64]{1,3,0,2:T(8,128)(2,1)S(1)}, ...), condition=%wide.region_6.7_spmd.clone, body=%wide.region_3.6_spmd.clone.sunk | while | flops 172393728 | bytes 6041442 | solution.py:89
  39.0 3.5 %fusion.70 = (f32[2,256]{1,0:T(2,128)S(1)}, f32[2,256,1280]{2,1,0:T(8,128)}) fusion(bf16[1280,2,64]{0,2,1:T(8,128)(2,1)S(1)} %get-tuple-element.184, pred[1280]{0:T(1024)(128)(4,1)S(1)} %broadcast_in_dim.99, bf16[4,256,2,64]{1,3,0,2:T(8,128)(2,1)} %get-tuple-element.183, s32[]{:T(128)S(6)} %copy.41), kind=kOutput, calls=%fused_computation.60.clone.1 | convolution fusion | flops 87164160 | bytes 3020804 | tf_op jit(solution)/shard_map/while/body/eval_jaxpr/while/body/eval_jaxpr/sub | solution.py:83
  42.4 2.3 %fusion.71 = bf16[4,256,2,64]{1,3,0,2:T(8,128)(2,1)S(1)} fusion(bf16[4,256,2,64]{1,3,0,2:T(8,128)(2,1)S(1)} %get-tuple-element.175, s32[]{:T(128)S(6)} %copy.41, bf16[1280,2,64]{0,2,1:T(8,128)(2,1)S(1)} %get-tuple-element.185, f32[2,256,1280]{2,1,0:T(8,128)} %get-tuple-element.165, f32[2,256]{1,0:T(2,128)S(1)} %get-tuple-element.166), kind=kOutput, calls=%fused_computation.11.clone.1 | convolution fusion | flops 85229568 | bytes 3016708 | tf_op jit(solution)/shard_map/while/body/eval_jaxpr/while/body/eval_jaxpr/krj,jkd->rkd/dot_general | solution.py:85
  44.8 3.4 %fusion.70 = (f32[2,256]{1,0:T(2,128)S(1)}, f32[2,256,1280]{2,1,0:T(8,128)}) fusion(bf16[1280,2,64]{0,2,1:T(8,128)(2,1)S(1)} %get-tuple-element.184, pred[1280]{0:T(1024)(128)(4,1)S(1)} %broadcast_in_dim.99, bf16[4,256,2,64]{1,3,0,2:T(8,128)(2,1)} %get-tuple-element.183, s32[]{:T(128)S(6)} %copy.41), kind=kOutput, calls=%fused_computation.60.clone.1 | convolution fusion | flops 87164160 | bytes 3020804 | tf_op jit(solution)/shard_map/while/body/eval_jaxpr/while/body/eval_jaxpr/sub | solution.py:83
  48.2 2.3 %fusion.71 = bf16[4,256,2,64]{1,3,0,2:T(8,128)(2,1)S(1)} fusion(bf16[4,256,2,64]{1,3,0,2:T(8,128)(2,1)S(1)} %get-tuple-element.175, s32[]{:T(128)S(6)} %copy.41, bf16[1280,2,64]{0,2,1:T(8,128)(2,1)S(1)} %get-tuple-element.185, f32[2,256,1280]{2,1,0:T(8,128)} %get-tuple-element.165, f32[2,256]{1,0:T(2,128)S(1)} %get-tuple-element.166), kind=kOutput, calls=%fused_computation.11.clone.1 | convolution fusion | flops 85229568 | bytes 3016708 | tf_op jit(solution)/shard_map/while/body/eval_jaxpr/while/body/eval_jaxpr/krj,jkd->rkd/dot_general | solution.py:85
  50.7 3.4 %fusion.70 = (f32[2,256]{1,0:T(2,128)S(1)}, f32[2,256,1280]{2,1,0:T(8,128)}) fusion(bf16[1280,2,64]{0,2,1:T(8,128)(2,1)S(1)} %get-tuple-element.184, pred[1280]{0:T(1024)(128)(4,1)S(1)} %broadcast_in_dim.99, bf16[4,256,2,64]{1,3,0,2:T(8,128)(2,1)} %get-tuple-element.183, s32[]{:T(128)S(6)} %copy.41), kind=kOutput, calls=%fused_computation.60.clone.1 | convolution fusion | flops 87164160 | bytes 3020804 | tf_op jit(solution)/shard_map/while/body/eval_jaxpr/while/body/eval_jaxpr/sub | solution.py:83
  54.1 2.3 %fusion.71 = bf16[4,256,2,64]{1,3,0,2:T(8,128)(2,1)S(1)} fusion(bf16[4,256,2,64]{1,3,0,2:T(8,128)(2,1)S(1)} %get-tuple-element.175, s32[]{:T(128)S(6)} %copy.41, bf16[1280,2,64]{0,2,1:T(8,128)(2,1)S(1)} %get-tuple-element.185, f32[2,256,1280]{2,1,0:T(8,128)} %get-tuple-element.165, f32[2,256]{1,0:T(2,128)S(1)} %get-tuple-element.166), kind=kOutput, calls=%fused_computation.11.clone.1 | convolution fusion | flops 85229568 | bytes 3016708 | tf_op jit(solution)/shard_map/while/body/eval_jaxpr/while/body/eval_jaxpr/krj,jkd->rkd/dot_general | solution.py:85
  56.5 3.4 %fusion.70 = (f32[2,256]{1,0:T(2,128)S(1)}, f32[2,256,1280]{2,1,0:T(8,128)}) fusion(bf16[1280,2,64]{0,2,1:T(8,128)(2,1)S(1)} %get-tuple-element.184, pred[1280]{0:T(1024)(128)(4,1)S(1)} %broadcast_in_dim.99, bf16[4,256,2,64]{1,3,0,2:T(8,128)(2,1)} %get-tuple-element.183, s32[]{:T(128)S(6)} %copy.41), kind=kOutput, calls=%fused_computation.60.clone.1 | convolution fusion | flops 87164160 | bytes 3020804 | tf_op jit(solution)/shard_map/while/body/eval_jaxpr/while/body/eval_jaxpr/sub | solution.py:83
  59.9 2.3 %fusion.71 = bf16[4,256,2,64]{1,3,0,2:T(8,128)(2,1)S(1)} fusion(bf16[4,256,2,64]{1,3,0,2:T(8,128)(2,1)S(1)} %get-tuple-element.175, s32[]{:T(128)S(6)} %copy.41, bf16[1280,2,64]{0,2,1:T(8,128)(2,1)S(1)} %get-tuple-element.185, f32[2,256,1280]{2,1,0:T(8,128)} %get-tuple-element.165, f32[2,256]{1,0:T(2,128)S(1)} %get-tuple-element.166), kind=kOutput, calls=%fused_computation.11.clone.1 | convolution fusion | flops 85229568 | bytes 3016708 | tf_op jit(solution)/shard_map/while/body/eval_jaxpr/while/body/eval_jaxpr/krj,jkd->rkd/dot_general | solution.py:85
  62.2 1.3 %fusion.34 = bf16[256,1024]{1,0:T(8,128)(2,1)} fusion(bf16[256,1024]{1,0:T(8,128)(2,1)S(1)} %get-tuple-element.123, bf16[256,512]{0,1:T(8,128)(2,1)S(1)} %bitcast.74, bf16[512,1024]{1,0:T(8,128)(2,1)S(1)} %copy-done.1), kind=kOutput, calls=%fused_computation.38 | convolution fusion | flops 269221888 | bytes 2359296 | tf_op jit(solution)/shard_map/dot_general | solution.py:158
  (45 shorter events, 4.0 us)
Async XLA Ops:
  0.0 21.4 %copy-start = (bf16[512,1024]{1,0:T(8,128)(2,1)S(1)}, bf16[512,1024]{1,0:T(8,128)(2,1)}, u32[]{:S(2)}) copy-start(bf16[512,1024]{1,0:T(8,128)(2,1)} %param.16) | copy-start | bytes 3145732
  0.0 9.9 %collective-permute-start = (bf16[256,256]{1,0:T(8,128)(2,1)}, bf16[256,256]{1,0:T(8,128)(2,1)S(1)}, u32[]{:S(2)}, u32[]{:S(2)}) collective-permute-start(bf16[256,256]{1,0:T(8,128)(2,1)} %param.13), channel_id=1, source_target_pairs={{0,1},{1,2},{2,3},{3,4},{4,5},{5,6},{6,7},{7,8},{8,9},{9,10},{10,1... | collective-permute-start | bytes 393224 | tf_op jit(solution)/shard_map/ppermute | solution.py:19
  2.5 8.4 %collective-permute-start.1 = (bf16[256,256]{1,0:T(8,128)(2,1)}, bf16[256,256]{1,0:T(8,128)(2,1)S(1)}, u32[]{:S(2)}, u32[]{:S(2)}) collective-permute-start(bf16[256,256]{1,0:T(8,128)(2,1)} %param.13), channel_id=1, source_target_pairs={{1,0},{2,1},{3,2},{4,3},{5,4},{6,5},{7,6},{8,7},{9,8},{10,9},{11,1... | collective-permute-start | bytes 393224 | tf_op jit(solution)/shard_map/ppermute | solution.py:21
  17.9 3.6 %copy-start.3 = (bf16[256,1024]{1,0:T(8,128)(2,1)S(1)}, bf16[256,1024]{1,0:T(8,128)(2,1)}, u32[]{:S(2)}) copy-start(bf16[256,1024]{1,0:T(8,128)(2,1)} %param.11) | copy-start | bytes 1572868
  21.4 1.0 %copy-start.4 = (bf16[1024,256]{1,0:T(8,128)(2,1)S(1)}, bf16[1024,256]{1,0:T(8,128)(2,1)}, u32[]{:S(2)}) copy-start(bf16[1024,256]{1,0:T(8,128)(2,1)} %param.18) | copy-start | bytes 1572868
  21.4 10.5 %copy-start.2 = (bf16[1024,512]{1,0:T(8,128)(2,1)S(1)}, bf16[1024,512]{1,0:T(8,128)(2,1)}, u32[]{:S(2)}) copy-start(bf16[1024,512]{1,0:T(8,128)(2,1)} %param.17) | copy-start | bytes 3145732
  22.8 10.5 %collective-permute-start.2 = (bf16[256,256]{1,0:T(8,128)(2,1)S(1)}, bf16[256,256]{1,0:T(8,128)(2,1)S(1)}, u32[]{:S(2)}, u32[]{:S(2)}) collective-permute-start(bf16[256,256]{1,0:T(8,128)(2,1)S(1)} %get-tuple-element.125), channel_id=1, source_target_pairs={{0,1},{1,0},{2,3},{3,2},{4,5},{5,4},{6,7},{7,6},{8,9},{9,8},{10,11... | collective-permute-start | bytes 393224 | tf_op jit(solution)/shard_map/ppermute | solution.py:35
  26.1 7.2 %collective-permute-start.3 = (bf16[256,256]{1,0:T(8,128)(2,1)S(1)}, bf16[256,256]{1,0:T(8,128)(2,1)S(1)}, u32[]{:S(2)}, u32[]{:S(2)}) collective-permute-start(bf16[256,256]{1,0:T(8,128)(2,1)S(1)} %get-tuple-element.125), channel_id=1, source_target_pairs={{0,2},{2,0},{1,3},{3,1},{4,6},{6,4},{5,7},{7,5},{8,10},{10,8},{9,1... | collective-permute-start | bytes 393224 | tf_op jit(solution)/shard_map/ppermute | solution.py:35
  27.8 7.9 %collective-permute-start.4 = (bf16[256,256]{1,0:T(8,128)(2,1)S(1)}, bf16[256,256]{1,0:T(8,128)(2,1)S(1)}, u32[]{:S(2)}, u32[]{:S(2)}) collective-permute-start(bf16[256,256]{1,0:T(8,128)(2,1)S(1)} %get-tuple-element.125), channel_id=1, source_target_pairs={{0,4},{4,0},{1,5},{5,1},{2,6},{6,2},{3,7},{7,3},{8,12},{12,8},{9,1... | collective-permute-start | bytes 393224 | tf_op jit(solution)/shard_map/ppermute | solution.py:35
  29.4 9.0 %collective-permute-start.5 = (bf16[256,256]{1,0:T(8,128)(2,1)S(1)}, bf16[256,256]{1,0:T(8,128)(2,1)S(1)}, u32[]{:S(2)}, u32[]{:S(2)}) collective-permute-start(bf16[256,256]{1,0:T(8,128)(2,1)S(1)} %get-tuple-element.125), channel_id=1, source_target_pairs={{0,8},{8,0},{1,9},{9,1},{2,10},{10,2},{3,11},{11,3},{4,12},{12,4},... | collective-permute-start | bytes 393224 | tf_op jit(solution)/shard_map/ppermute | solution.py:35
  38.8 23.4 %copy-start.1 = (bf16[512,1024]{1,0:T(8,128)(2,1)S(1)}, bf16[512,1024]{1,0:T(8,128)(2,1)}, u32[]{:S(2)}) copy-start(bf16[512,1024]{1,0:T(8,128)(2,1)} %param.19) | copy-start | bytes 3145732
where the time goes:
time: 64.1 us; the launch traced here: 63.5 us
  matrix products  35.7 us (56%)
  starting transfers between devices  12.9 us (20%)
  local copies, waits for them, and re-layouts  6.74 us (11%)
  waiting for transfers between devices  5.07 us (8%)
  between operations  2.76 us (4%)
    sub x4, matrix products, one_group(): weights = jnp.where(allowed, jnp.exp(scores - row_max), 0.0)  13.6 us
    dot_general x4, matrix products, one_group(): jnp.einsum('krj,jkd->rkd', shares, value_head_rows, preferred_element_typ...  9.3 us
    ppermute x4, starting transfers between devices, swapped(): return lax.ppermute(block, axis, route)  9.15 us
    sub x1, matrix products, attend_rows(): weights = jnp.where(allowed, jnp.exp(scores - row_max), 0.0)  6.61 us
    ppermute x4, waiting for transfers between devices, swapped(): return lax.ppermute(block, axis, route)  5.07 us
    dot_general x1, matrix products, attend_rows(): jnp.einsum('kgrj,jkd->rkgd', shares, value_head_rows, preferred_element_t...  3.53 us
    ppermute x1, starting transfers between devices, with_halo(): lax.ppermute(tail, axis, [(i, (i + 1) % count) for i in range(ends)])  2.49 us
    unnamed x16, local copies, waits for them, and re-layouts  2.48 us
  transfers between devices with their start and end apart: 6, of which 2 were waited for; matrix products, arithmetic and copies ran while one was open for 9% of the time, Pallas kernels for 0%

commit v1 on v0

v1 whole, which is shorter than its diff:
```python
import functools
import math

import jax
import jax.numpy as jnp
from jax import lax
from jax.experimental import pallas as pl
from jax.experimental.pallas import tpu as pltpu
from jax.sharding import PartitionSpec as P

HEAD_SIZE = 64
WIN = 256
LANES = 128
LOW = -1e30
SCALE = HEAD_SIZE**-0.5 * math.log2(math.e)


def dot(a, b):
    return jnp.dot(a, b, preferred_element_type=jnp.float32)


def dot_t(a, b):
    return lax.dot_general(a, b, (((1,), (1,)), ((), ())), preferred_element_type=jnp.float32)


def spread_keyvals(keyvals, keys_ref, values_ref, first):
    rows = keyvals.shape[0]
    kv_heads = keyvals.shape[1] // (2 * HEAD_SIZE)
    low = lax.broadcasted_iota(jnp.int32, (rows, LANES), 1) < HEAD_SIZE
    zero = jnp.zeros((rows, LANES), jnp.bfloat16)
    one = jnp.ones((rows, LANES), jnp.bfloat16)
    spot = pl.ds(first, rows)
    per_tile = LANES // HEAD_SIZE
    for g in range(kv_heads):
        tile, at = divmod(g, per_tile)
        k = keyvals[:, tile * LANES : (tile + 1) * LANES]
        v_first = kv_heads * HEAD_SIZE + tile * LANES
        v = keyvals[:, v_first : v_first + LANES]
        k_other = jnp.concatenate([k[:, HEAD_SIZE:], k[:, :HEAD_SIZE]], axis=1)
        v_other = jnp.concatenate([v[:, HEAD_SIZE:], v[:, :HEAD_SIZE]], axis=1)
        for s in range(2):
            here = low if s == 0 else jnp.logical_not(low)
            keys_ref[g, s, spot, :] = jnp.where(here, k if at == s else k_other, zero)
            values_ref[g, s, spot, :LANES] = jnp.where(here, v if at == s else v_other, zero)
            values_ref[g, s, spot, LANES:] = jnp.where(here, one, zero)


def window_kernel(
    extent_ref,
    q_ref,
    left_ref,
    own_ref,
    right_ref,
    residual_hbm,
    out_w_hbm,
    kv_w_hbm,
    hidden_ref,
    normed_ref,
    kv_ref,
    keys_ref,
    values_ref,
    attended_ref,
    residual_ref,
    out_w_ref,
    kv_w_ref,
    sems,
):
    copies = [
        pltpu.make_async_copy(src, dst, sems.at[n])
        for n, (src, dst) in enumerate(
            ((residual_hbm, residual_ref), (out_w_hbm, out_w_ref), (kv_w_hbm, kv_w_ref))
        )
    ]
    for copy in copies:
        copy.start()
    rows = q_ref.shape[0]
    step = LANES
    me = lax.axis_index("seq")
    last = lax.axis_size("seq") - 1
    spread_keyvals(left_ref[...], keys_ref, values_ref, 0)
    spread_keyvals(own_ref[...], keys_ref, values_ref, WIN)
    spread_keyvals(right_ref[...], keys_ref, values_ref, WIN + rows)
    span = step + 2 * WIN
    kv_heads = keys_ref.shape[0]
    pairs = q_ref.shape[1] // LANES
    row = lax.broadcasted_iota(jnp.int32, (step, step), 0)
    col = lax.broadcasted_iota(jnp.int32, (step, step), 1)
    gap = row - col
    for pair in range(pairs):
        g = pair * kv_heads // pairs
        for part in range(rows // step):
            first = part * step
            q = q_ref[pl.ds(first, step), pair * LANES : (pair + 1) * LANES]
            total = None
            for s in range(2):
                extent = extent_ref[2 * pair + s]
                scores = dot_t(q, keys_ref[g, s, pl.ds(first, span), :])
                tiles = []
                for t in range(span // step):
                    begin = first + t * step
                    reach = extent
                    if begin < WIN:
                        reach = jnp.where(me > 0, extent, -1)
                    elif begin >= WIN + rows:
                        reach = jnp.where(me < last, extent, -1)
                    offset = WIN - t * step
                    if offset > 0:
                        seen = gap <= reach - offset
                    elif offset < 0:
                        seen = gap >= -offset - reach
                    else:
                        seen = jnp.abs(gap) <= reach
                    tiles.append(jnp.where(seen, scores[:, t * step : (t + 1) * step], LOW))
                top = functools.reduce(jnp.maximum, tiles)
                top = jnp.max(top, axis=1, keepdims=True)
                weights = jnp.concatenate(
                    [jnp.exp2((tile - top) * SCALE).astype(jnp.bfloat16) for tile in tiles], axis=1
                )
                mix = dot(weights, values_ref[g, s, pl.ds(first, span), :])
                total = mix if total is None else total + mix
            attended_ref[pl.ds(first, step), pair * LANES : (pair + 1) * LANES] = (
                total[:, :LANES] / total[:, LANES:]
            ).astype(jnp.bfloat16)
    for copy in copies:
        copy.wait()
    hidden = (
        dot(attended_ref[...], out_w_ref[...]) + residual_ref[...].astype(jnp.float32)
    ).astype(jnp.bfloat16)
    hidden_ref[...] = hidden
    values = hidden.astype(jnp.float32)
    scale = lax.rsqrt(jnp.mean(values * values, axis=-1, keepdims=True) + 1e-05)
    normed = (values * scale).astype(jnp.bfloat16)
    normed_ref[...] = normed
    kv_ref[...] = dot(normed, kv_w_ref[...]).astype(jnp.bfloat16)


def butterfly_kernel(levels, mask_ref, *refs):
    (normed_ref, hidden_ref, q_w_ref, out_w_ref), refs = refs[:4], refs[4:]
    block_refs, refs = refs[: levels + 1], refs[levels + 1 :]
    out_ref, keys_ref, values_ref, q_ref, attended_ref = refs
    rows = normed_ref.shape[0]
    step = LANES
    q_ref[...] = dot(normed_ref[...], q_w_ref[...]).astype(jnp.bfloat16)
    for n, block in enumerate(block_refs):
        spread_keyvals(block[...], keys_ref, values_ref, n * rows)
    kv_heads = keys_ref.shape[0]
    pairs = q_ref.shape[1] // LANES
    shut = [None] + [jnp.where(mask_ref[0, level] == 1, 0.0, -LOW) for level in range(levels)]
    for pair in range(pairs):
        g = pair * kv_heads // pairs
        for part in range(rows // step):
            first = part * step
            q = q_ref[pl.ds(first, step), pair * LANES : (pair + 1) * LANES]
            total = None
            for s in range(2):
                scores = dot_t(q, keys_ref[g, s])
                top = None
                for n in range(levels + 1):
                    tiles = [
                        scores[:, n * rows + c : n * rows + c + LANES] for c in range(0, rows, LANES)
                    ]
                    one = functools.reduce(jnp.maximum, tiles)
                    if n:
                        one = one - shut[n]
                    top = one if top is None else jnp.maximum(top, one)
                top = jnp.max(top, axis=1, keepdims=True)
                weights = []
                for n in range(levels + 1):
                    base = top + shut[n] if n else top
                    weights.append(
                        jnp.exp2((scores[:, n * rows : (n + 1) * rows] - base) * SCALE).astype(
                            jnp.bfloat16
                        )
                    )
                mix = dot(jnp.concatenate(weights, axis=1), values_ref[g, s])
                total = mix if total is None else total + mix
            attended_ref[pl.ds(first, step), pair * LANES : (pair + 1) * LANES] = (
                total[:, :LANES] / total[:, LANES:]
            ).astype(jnp.bfloat16)
    out_ref[...] = (
        dot(attended_ref[...], out_w_ref[...]) + hidden_ref[...].astype(jnp.float32)
    ).astype(jnp.bfloat16)


def shards(
    residual,
    layer_queries,
    layer_keyvals,
    head_window_extent,
    block_mask,
    first_out,
    second_query,
    second_keyval,
    second_out,
):
    rows, width = residual.shape
    q_width = layer_queries.shape[1]
    kv_width = layer_keyvals.shape[1]
    kv_heads = kv_width // (2 * HEAD_SIZE)
    count = lax.axis_size("seq")
    levels = count.bit_length() - 1
    bf16 = jnp.bfloat16
    vmem = pl.BlockSpec(memory_space=pltpu.VMEM)
    smem = pl.BlockSpec(memory_space=pltpu.SMEM)
    hbm = pl.BlockSpec(memory_space=pl.ANY)

    from_left = lax.ppermute(layer_keyvals[-WIN:], "seq", [(i, i + 1) for i in range(count - 1)])
    from_right = lax.ppermute(layer_keyvals[:WIN], "seq", [(i + 1, i) for i in range(count - 1)])
    keys = rows + 2 * WIN
    hidden, normed, keyvals = pl.pallas_call(
        window_kernel,
        out_shape=[
            jax.ShapeDtypeStruct((rows, width), bf16),
            jax.ShapeDtypeStruct((rows, width), bf16),
            jax.ShapeDtypeStruct((rows, kv_width), bf16),
        ],
        in_specs=[smem, vmem, vmem, vmem, vmem, hbm, hbm, hbm],
        out_specs=[vmem] * 3,
        scratch_shapes=[
            pltpu.VMEM((kv_heads, 2, keys, LANES), bf16),
            pltpu.VMEM((kv_heads, 2, keys, 2 * LANES), bf16),
            pltpu.VMEM((rows, q_width), bf16),
            pltpu.VMEM(residual.shape, bf16),
            pltpu.VMEM(first_out.shape, bf16),
            pltpu.VMEM(second_keyval.shape, bf16),
            pltpu.SemaphoreType.DMA((3,)),
        ],
        compiler_params=pltpu.CompilerParams(vmem_limit_bytes=24 * 2**20),
        name="window",
    )(
        head_window_extent,
        layer_queries,
        from_left,
        layer_keyvals,
        from_right,
        residual,
        first_out,
        second_keyval,
    )

    others = [None] * levels
    for level in reversed(range(levels)):
        route = [(i, i ^ (1 << level)) for i in range(count)]
        others[level] = lax.ppermute(keyvals, "seq", route)
    keys = rows * (levels + 1)
    return pl.pallas_call(
        functools.partial(butterfly_kernel, levels),
        out_shape=jax.ShapeDtypeStruct((rows, width), bf16),
        in_specs=[smem] + [vmem] * (5 + levels),
        out_specs=vmem,
        scratch_shapes=[
            pltpu.VMEM((kv_heads, 2, keys, LANES), bf16),
            pltpu.VMEM((kv_heads, 2, keys, 2 * LANES), bf16),
            pltpu.VMEM((rows, q_width), bf16),
            pltpu.VMEM((rows, q_width), bf16),
        ],
        compiler_params=pltpu.CompilerParams(vmem_limit_bytes=24 * 2**20),
        name="butterfly",
    )(block_mask, normed, hidden, second_query, second_out, keyvals, *others)


def solution(mesh):
    tokens = P(("groups", "seq"), None)
    placed = (tokens, tokens, tokens, P(), P("seq", None), P(), P(), P(), P())
    return jax.shard_map(shards, mesh=mesh, in_specs=placed, out_specs=tokens, check_vma=False)
```

time: 64.1 us -> 38.7 us (0.60)
  matrix products: 35.7 us -> 0 us
  Pallas kernels: 0 us -> 10.9 us
  waiting for transfers between devices: 5.07 us -> 9.08 us
  between operations: 2.76 us -> 0.06 us
  starting transfers between devices: 12.9 us -> 11.9 us
    sub x5 -> x0, matrix products: 20.2 us -> none  [the longest x4 13.6 us: one_group(): weights = jnp.where(allowed, jnp.exp(scores - row_max), 0.0)]
    dot_general x9 -> x0, matrix products: 15.5 us -> none  [the longest x4 9.3 us: one_group(): jnp.einsum('krj,jkd->rkd', shares, value_head_rows, preferred_element_typ...]
    pallas_call x0 -> x2, Pallas kernels: none -> 10.9 us  [the longest x1 6.31 us: shards(): pl.pallas_call(functools.partial(butterfly_kernel, levels), out_shape=jax...]
    ppermute x6, waiting for transfers between devices: 5.07 us -> 9.08 us  [the longest x4 4.84 us: shards(): others[level] = lax.ppermute(keyvals, 'seq', route)]
    unnamed x16 -> x18, local copies, waits for them, and re-layouts: 2.48 us -> 6.46 us
    slice x7 -> x0, local copies, waits for them, and re-layouts: 2.21 us -> none  [the longest x1 1.47 us: shards(): key_flags.append(block_mask[0, level] == 1)]
    ppermute x6, starting transfers between devices: 12.9 us -> 11.9 us  [the longest x4 8.09 us: shards(): others[level] = lax.ppermute(keyvals, 'seq', route)]
    convert_element_type x1 -> x0, local copies, waits for them, and re-layouts: 0.84 us -> none  [shards(): jnp.dot(normed, second_query, preferred_element_type=jnp.float32)]
  transfers between devices with their start and end apart: 6 -> 6, of which waited for: 2 -> 3; matrix products, arithmetic and copies ran while one was open for 9% -> 0% of each run, Pallas kernels for 0% -> 0%
where the time goes in v1:
time: 38.7 us; the launch traced here: 38.4 us
  starting transfers between devices  11.9 us (31%)
  Pallas kernels  10.9 us (28%)
  waiting for transfers between devices  9.08 us (23%)
  local copies, waits for them, and re-layouts  6.46 us (17%)
    ppermute x4, starting transfers between devices, shards(): others[level] = lax.ppermute(keyvals, 'seq', route)  8.09 us
    unnamed x18, local copies, waits for them, and re-layouts  6.46 us
    pallas_call x1, Pallas kernels, shards(): pl.pallas_call(functools.partial(butterfly_kernel, levels), out_shape=jax...  6.31 us
    ppermute x4, waiting for transfers between devices, shards(): others[level] = lax.ppermute(keyvals, 'seq', route)  4.84 us
    pallas_call x1, Pallas kernels, shards(): pl.pallas_call(window_kernel, out_shape=[jax.ShapeDtypeStruct((rows, widt...  4.58 us
    ppermute x1, waiting for transfers between devices, shards(): lax.ppermute(layer_keyvals[:WIN], 'seq', [(i + 1, i) for i in range(count...  4.24 us
    ppermute x1, starting transfers between devices, shards(): lax.ppermute(layer_keyvals[-WIN:], 'seq', [(i, i + 1) for i in range(coun...  2.48 us
    ppermute x1, starting transfers between devices, shards(): lax.ppermute(layer_keyvals[:WIN], 'seq', [(i + 1, i) for i in range(count...  1.29 us
  transfers between devices with their start and end apart: 6, of which 3 were waited for; matrix products, arithmetic and copies ran while one was open for 0% of the time, Pallas kernels for 0%

profile of v1, /device:TPU:0, one launch (start us, length us, event | category | flops | bytes accessed | tf_op | source)
XLA Modules:
  0.0 38.4 jit_solution(13406028597258855835)
XLA Ops:
  0.0 0.0 copy-start.1
  0.0 2.5 %collective-permute-start = (bf16[256,256]{1,0:T(8,128)(2,1)}, bf16[256,256]{1,0:T(8,128)(2,1)S(1)}, u32[]{:S(2)}, u32[]{:S(2)}) collective-permute-start(bf16[256,256]{1,0:T(8,128)(2,1)} %own_ref.1), channel_id=1, source_target_pairs={{0,1},{1,2},{2,3},{3,4},{4,5},{5,6},{6,7},{7,8},{8,9},{9,10},{10,1... | collective-permute-start | bytes 393224 | tf_op jit(solution)/shard_map/ppermute | solution.py:207
  2.5 1.3 %collective-permute-start.1 = (bf16[256,256]{1,0:T(8,128)(2,1)}, bf16[256,256]{1,0:T(8,128)(2,1)S(1)}, u32[]{:S(2)}, u32[]{:S(2)}) collective-permute-start(bf16[256,256]{1,0:T(8,128)(2,1)} %own_ref.1), channel_id=1, source_target_pairs={{1,0},{2,1},{3,2},{4,3},{5,4},{6,5},{7,6},{8,7},{9,8},{10,9},{11,1... | collective-permute-start | bytes 393224 | tf_op jit(solution)/shard_map/ppermute | solution.py:208
  3.8 0.0 collective-permute-done.left_ref
  3.8 4.2 %collective-permute-done.1.right_ref = bf16[256,256]{1,0:T(8,128)(2,1)S(1)} collective-permute-done((bf16[256,256]{1,0:T(8,128)(2,1)}, bf16[256,256]{1,0:T(8,128)(2,1)S(1)}, u32[]{:S(2)}, u32[]{:S(2)}) %collective-permute-start.1) | collective-permute-done | bytes 131104 | tf_op jit(solution)/shard_map/ppermute | solution.py:208
  8.1 1.2 %copy-done.2 = bf16[512,1024]{1,0:T(8,128)(2,1)S(1)} copy-done((bf16[512,1024]{1,0:T(8,128)(2,1)S(1)}, bf16[512,1024]{1,0:T(8,128)(2,1)}, u32[]{:S(2)}) %copy-start.2) | copy-done | bytes 1048600
  9.3 1.0 %copy-done.3 = bf16[256,1024]{1,0:T(8,128)(2,1)S(1)} copy-done((bf16[256,1024]{1,0:T(8,128)(2,1)S(1)}, bf16[256,1024]{1,0:T(8,128)(2,1)}, u32[]{:S(2)}) %copy-start.3) | copy-done | bytes 524312
  10.3 1.0 %copy-done.4 = bf16[1024,256]{1,0:T(8,128)(2,1)S(1)} copy-done((bf16[1024,256]{1,0:T(8,128)(2,1)S(1)}, bf16[1024,256]{1,0:T(8,128)(2,1)}, u32[]{:S(2)}) %copy-start.4) | copy-done | bytes 524312
  11.4 0.9 %copy-done.5 = bf16[256,512]{1,0:T(8,128)(2,1)S(1)} copy-done((bf16[256,512]{1,0:T(8,128)(2,1)S(1)}, bf16[256,512]{1,0:T(8,128)(2,1)}, u32[]{:S(2)}) %copy-start.5) | copy-done | bytes 262168
  12.3 0.9 %copy-done.6 = bf16[256,256]{1,0:T(8,128)(2,1)S(1)} copy-done((bf16[256,256]{1,0:T(8,128)(2,1)S(1)}, bf16[256,256]{1,0:T(8,128)(2,1)}, u32[]{:S(2)}) %copy-start.6) | copy-done | bytes 131096
  13.2 0.7 %copy-done.7 = s32[8]{0:T(128)S(1)} copy-done((s32[8]{0:T(128)S(1)}, s32[8]{0:T(128)}, u32[]{:S(2)}) %copy-start.7) | copy-done | bytes 56
  13.9 4.6 %window.1 = (bf16[256,1024]{1,0:T(8,128)(2,1)S(1)}, bf16[256,1024]{1,0:T(8,128)(2,1)S(1)}, bf16[256,256]{1,0:T(8,128)(2,1)S(1)}) custom-call(s32[8]{0:T(128)S(1)} %copy-done.7, bf16[256,512]{1,0:T(8,128)(2,1)S(1)} %copy-done.5, bf16[256,256]{1,0:T(8,128)(2,1)S(1)} %collective-permute-done.left_ref, bf16[256,256]{1,0:T(8,128)(2,1)S(1)} %copy-done.6, ...), custom_call_target="tpu_custom_call" | custom-call | tf_op jit(solution)/shard_map/window/pallas_call | solution.py:210
  18.5 5.5 %collective-permute-start.5 = (bf16[256,256]{1,0:T(8,128)(2,1)S(1)}, bf16[256,256]{1,0:T(8,128)(2,1)S(1)}, u32[]{:S(2)}, u32[]{:S(2)}) collective-permute-start(bf16[256,256]{1,0:T(8,128)(2,1)S(1)} %get-tuple-element.10.refs_4_), channel_id=1, source_target_pairs={{0,8},{1,9},{2,10},{3,11},{4,12},{5,13},{6,14},{7,15},{8,0},{9,1},... | collective-permute-start | bytes 393224 | tf_op jit(solution)/shard_map/ppermute | solution.py:244
  23.9 1.6 %collective-permute-start.4 = (bf16[256,256]{1,0:T(8,128)(2,1)S(1)}, bf16[256,256]{1,0:T(8,128)(2,1)S(1)}, u32[]{:S(2)}, u32[]{:S(2)}) collective-permute-start(bf16[256,256]{1,0:T(8,128)(2,1)S(1)} %get-tuple-element.10.refs_4_), channel_id=1, source_target_pairs={{0,4},{1,5},{2,6},{3,7},{4,0},{5,1},{6,2},{7,3},{8,12},{9,13},{10,... | collective-permute-start | bytes 393224 | tf_op jit(solution)/shard_map/ppermute | solution.py:244
  25.5 0.6 %collective-permute-start.3 = (bf16[256,256]{1,0:T(8,128)(2,1)S(1)}, bf16[256,256]{1,0:T(8,128)(2,1)S(1)}, u32[]{:S(2)}, u32[]{:S(2)}) collective-permute-start(bf16[256,256]{1,0:T(8,128)(2,1)S(1)} %get-tuple-element.10.refs_4_), channel_id=1, source_target_pairs={{0,2},{1,3},{2,0},{3,1},{4,6},{5,7},{6,4},{7,5},{8,10},{9,11},{10,... | collective-permute-start | bytes 393224 | tf_op jit(solution)/shard_map/ppermute | solution.py:244
  26.1 0.5 %collective-permute-start.2 = (bf16[256,256]{1,0:T(8,128)(2,1)S(1)}, bf16[256,256]{1,0:T(8,128)(2,1)S(1)}, u32[]{:S(2)}, u32[]{:S(2)}) collective-permute-start(bf16[256,256]{1,0:T(8,128)(2,1)S(1)} %get-tuple-element.10.refs_4_), channel_id=1, source_target_pairs={{0,1},{1,0},{2,3},{3,2},{4,5},{5,4},{6,7},{7,6},{8,9},{9,8},{10,11... | collective-permute-start | bytes 393224 | tf_op jit(solution)/shard_map/ppermute | solution.py:244
  26.5 4.5 %collective-permute-done.5.refs_8_ = bf16[256,256]{1,0:T(8,128)(2,1)S(1)} collective-permute-done((bf16[256,256]{1,0:T(8,128)(2,1)S(1)}, bf16[256,256]{1,0:T(8,128)(2,1)S(1)}, u32[]{:S(2)}, u32[]{:S(2)}) %collective-permute-start.5) | collective-permute-done | bytes 131104 | tf_op jit(solution)/shard_map/ppermute | solution.py:244
  31.1 0.3 collective-permute-done.4.refs_7_
  31.4 0.0 collective-permute-done.3.refs_6_
  31.4 0.0 collective-permute-done.2.refs_5_
  31.4 0.0 copy-done.1
  31.4 0.0 copy-done
  31.4 0.6 %copy-done.8 = s32[1,4]{1,0:T(1,128)S(1)} copy-done((s32[1,4]{1,0:T(1,128)S(1)}, s32[1,4]{1,0:T(1,128)}, u32[]{:S(2)}) %copy-start.8) | copy-done | bytes 40
  32.0 6.3 %butterfly.1 = bf16[256,1024]{1,0:T(8,128)(2,1)} custom-call(s32[1,4]{1,0:T(1,128)S(1)} %copy-done.8, bf16[256,1024]{1,0:T(8,128)(2,1)S(1)} %get-tuple-element.8.refs_0_, bf16[256,1024]{1,0:T(8,128)(2,1)S(1)} %get-tuple-element.9.refs_1_, bf16[1024,512]{1,0:T(8,128)(2,1)S(1)} %copy-done, bf16[512,1024]{1,0:T(8,128)(2,1)S(1)} %copy-done.1, ...), custom_call_target="tpu_custom_call" | custom-call | tf_op jit(solution)/shard_map/butterfly/pallas_call | solution.py:246
  (8 shorter events, 0.0 us)
Async XLA Ops:
  0.0 31.4 %copy-start.1 = (bf16[512,1024]{1,0:T(8,128)(2,1)S(1)}, bf16[512,1024]{1,0:T(8,128)(2,1)}, u32[]{:S(2)}) copy-start(bf16[512,1024]{1,0:T(8,128)(2,1)} %refs_3_.1) | copy-start | bytes 3145732
  0.0 31.4 %copy-start = (bf16[1024,512]{1,0:T(8,128)(2,1)S(1)}, bf16[1024,512]{1,0:T(8,128)(2,1)}, u32[]{:S(2)}) copy-start(bf16[1024,512]{1,0:T(8,128)(2,1)} %refs_2_.1) | copy-start | bytes 3145732
  0.0 3.8 %collective-permute-start = (bf16[256,256]{1,0:T(8,128)(2,1)}, bf16[256,256]{1,0:T(8,128)(2,1)S(1)}, u32[]{:S(2)}, u32[]{:S(2)}) collective-permute-start(bf16[256,256]{1,0:T(8,128)(2,1)} %own_ref.1), channel_id=1, source_target_pairs={{0,1},{1,2},{2,3},{3,4},{4,5},{5,6},{6,7},{7,8},{8,9},{9,10},{10,1... | collective-permute-start | bytes 393224 | tf_op jit(solution)/shard_map/ppermute | solution.py:207
  2.5 5.6 %collective-permute-start.1 = (bf16[256,256]{1,0:T(8,128)(2,1)}, bf16[256,256]{1,0:T(8,128)(2,1)S(1)}, u32[]{:S(2)}, u32[]{:S(2)}) collective-permute-start(bf16[256,256]{1,0:T(8,128)(2,1)} %own_ref.1), channel_id=1, source_target_pairs={{1,0},{2,1},{3,2},{4,3},{5,4},{6,5},{7,6},{8,7},{9,8},{10,9},{11,1... | collective-permute-start | bytes 393224 | tf_op jit(solution)/shard_map/ppermute | solution.py:208
  8.0 1.2 %copy-start.2 = (bf16[512,1024]{1,0:T(8,128)(2,1)S(1)}, bf16[512,1024]{1,0:T(8,128)(2,1)}, u32[]{:S(2)}) copy-start(bf16[512,1024]{1,0:T(8,128)(2,1)} %out_w_hbm.1) | copy-start | bytes 3145732
  9.3 1.0 %copy-start.3 = (bf16[256,1024]{1,0:T(8,128)(2,1)S(1)}, bf16[256,1024]{1,0:T(8,128)(2,1)}, u32[]{:S(2)}) copy-start(bf16[256,1024]{1,0:T(8,128)(2,1)} %residual_hbm.1) | copy-start | bytes 1572868
  10.3 1.0 %copy-start.4 = (bf16[1024,256]{1,0:T(8,128)(2,1)S(1)}, bf16[1024,256]{1,0:T(8,128)(2,1)}, u32[]{:S(2)}) copy-start(bf16[1024,256]{1,0:T(8,128)(2,1)} %kv_w_hbm.1) | copy-start | bytes 1572868
  11.4 0.9 %copy-start.5 = (bf16[256,512]{1,0:T(8,128)(2,1)S(1)}, bf16[256,512]{1,0:T(8,128)(2,1)}, u32[]{:S(2)}) copy-start(bf16[256,512]{1,0:T(8,128)(2,1)} %q_ref.1) | copy-start | bytes 786436
  12.3 0.9 %copy-start.6 = (bf16[256,256]{1,0:T(8,128)(2,1)S(1)}, bf16[256,256]{1,0:T(8,128)(2,1)}, u32[]{:S(2)}) copy-start(bf16[256,256]{1,0:T(8,128)(2,1)} %own_ref.1) | copy-start | bytes 393220
  13.2 0.7 %copy-start.7 = (s32[8]{0:T(128)S(1)}, s32[8]{0:T(128)}, u32[]{:S(2)}) copy-start(s32[8]{0:T(128)} %extent_ref.1) | copy-start | bytes 100
  18.5 12.6 %collective-permute-start.5 = (bf16[256,256]{1,0:T(8,128)(2,1)S(1)}, bf16[256,256]{1,0:T(8,128)(2,1)S(1)}, u32[]{:S(2)}, u32[]{:S(2)}) collective-permute-start(bf16[256,256]{1,0:T(8,128)(2,1)S(1)} %get-tuple-element.10.refs_4_), channel_id=1, source_target_pairs={{0,8},{1,9},{2,10},{3,11},{4,12},{5,13},{6,14},{7,15},{8,0},{9,1},... | collective-permute-start | bytes 393224 | tf_op jit(solution)/shard_map/ppermute | solution.py:244
  23.9 7.5 %collective-permute-start.4 = (bf16[256,256]{1,0:T(8,128)(2,1)S(1)}, bf16[256,256]{1,0:T(8,128)(2,1)S(1)}, u32[]{:S(2)}, u32[]{:S(2)}) collective-permute-start(bf16[256,256]{1,0:T(8,128)(2,1)S(1)} %get-tuple-element.10.refs_4_), channel_id=1, source_target_pairs={{0,4},{1,5},{2,6},{3,7},{4,0},{5,1},{6,2},{7,3},{8,12},{9,13},{10,... | collective-permute-start | bytes 393224 | tf_op jit(solution)/shard_map/ppermute | solution.py:244
  25.5 5.9 %collective-permute-start.3 = (bf16[256,256]{1,0:T(8,128)(2,1)S(1)}, bf16[256,256]{1,0:T(8,128)(2,1)S(1)}, u32[]{:S(2)}, u32[]{:S(2)}) collective-permute-start(bf16[256,256]{1,0:T(8,128)(2,1)S(1)} %get-tuple-element.10.refs_4_), channel_id=1, source_target_pairs={{0,2},{1,3},{2,0},{3,1},{4,6},{5,7},{6,4},{7,5},{8,10},{9,11},{10,... | collective-permute-start | bytes 393224 | tf_op jit(solution)/shard_map/ppermute | solution.py:244
  26.1 5.3 %collective-permute-start.2 = (bf16[256,256]{1,0:T(8,128)(2,1)S(1)}, bf16[256,256]{1,0:T(8,128)(2,1)S(1)}, u32[]{:S(2)}, u32[]{:S(2)}) collective-permute-start(bf16[256,256]{1,0:T(8,128)(2,1)S(1)} %get-tuple-element.10.refs_4_), channel_id=1, source_target_pairs={{0,1},{1,0},{2,3},{3,2},{4,5},{5,4},{6,7},{7,6},{8,9},{9,8},{10,11... | collective-permute-start | bytes 393224 | tf_op jit(solution)/shard_map/ppermute | solution.py:244
  31.4 0.7 %copy-start.8 = (s32[1,4]{1,0:T(1,128)S(1)}, s32[1,4]{1,0:T(1,128)}, u32[]{:S(2)}) copy-start(s32[1,4]{1,0:T(1,128)} %mask_ref.1) | copy-start | bytes 52

commit v2 on v1

v2 whole, which is shorter than its diff:
```python
import functools
import math

import jax
import jax.numpy as jnp
from jax import lax
from jax.experimental import pallas as pl
from jax.experimental.pallas import tpu as pltpu
from jax.sharding import PartitionSpec as P

HEAD_SIZE = 64
WIN = 256
LANES = 128
LOW = -1e30
SCALE = HEAD_SIZE**-0.5 * math.log2(math.e)
VMEM_LIMIT = 20 * 2**20


def dot(a, b):
    return jnp.dot(a, b, preferred_element_type=jnp.float32)


def dot_t(a, b):
    return lax.dot_general(a, b, (((1,), (1,)), ((), ())), preferred_element_type=jnp.float32)


def start_copies(pairs, sems):
    copies = [pltpu.make_async_copy(src, dst, sems.at[n]) for n, (src, dst) in enumerate(pairs)]
    for copy in copies:
        copy.start()
    return copies


def spread_keyvals(keyvals, keys_ref, values_ref, first):
    rows = keyvals.shape[0]
    kv_heads = keyvals.shape[1] // (2 * HEAD_SIZE)
    low = lax.broadcasted_iota(jnp.int32, (rows, LANES), 1) < HEAD_SIZE
    zero = jnp.zeros((rows, LANES), jnp.bfloat16)
    one = jnp.ones((rows, LANES), jnp.bfloat16)
    spot = pl.ds(first, rows)
    per_tile = LANES // HEAD_SIZE
    for g in range(kv_heads):
        tile, at = divmod(g, per_tile)
        k = keyvals[:, tile * LANES : (tile + 1) * LANES]
        v_first = kv_heads * HEAD_SIZE + tile * LANES
        v = keyvals[:, v_first : v_first + LANES]
        k_other = jnp.concatenate([k[:, HEAD_SIZE:], k[:, :HEAD_SIZE]], axis=1)
        v_other = jnp.concatenate([v[:, HEAD_SIZE:], v[:, :HEAD_SIZE]], axis=1)
        for s in range(2):
            here = low if s == 0 else jnp.logical_not(low)
            keys_ref[g, s, spot, :] = jnp.where(here, k if at == s else k_other, zero)
            values_ref[g, s, spot, :LANES] = jnp.where(here, v if at == s else v_other, zero)
            values_ref[g, s, spot, LANES:] = jnp.where(here, one, zero)


def attend(q_ref, keys_ref, values_ref, ranges, mask, prior, sink):
    kv_heads = keys_ref.shape[0]
    pairs = q_ref.shape[1] // LANES
    low = lax.broadcasted_iota(jnp.int32, (LANES, LANES), 1) < HEAD_SIZE
    for pair in range(pairs):
        g = pair * kv_heads // pairs
        for part, (first, span) in enumerate(ranges):
            here = pl.ds(part * LANES, LANES)
            q = q_ref[here, pair * LANES : (pair + 1) * LANES]
            total, tops, scales = None, [], []
            for s in range(2):
                scores = dot_t(q, keys_ref[g, s, pl.ds(first, span), :])
                tiles = [scores[:, c : c + LANES] for c in range(0, span, LANES)]
                tiles, tile_tops, bases = mask(pair, s, part, tiles)
                top = jnp.max(functools.reduce(jnp.maximum, tile_tops), axis=1, keepdims=True)
                top = jnp.broadcast_to(top, (LANES, LANES))
                if prior is not None:
                    old = prior[1][2 * pair + s, here, :]
                    top = jnp.maximum(top, old)
                    scales.append(jnp.exp2((old - top) * SCALE))
                weights = jnp.concatenate(
                    [
                        jnp.exp2((tile - (top if base is None else top + base)) * SCALE).astype(
                            jnp.bfloat16
                        )
                        for tile, base in zip(tiles, bases)
                    ],
                    axis=1,
                )
                mix = dot(weights, values_ref[g, s, pl.ds(first, span), :])
                total = mix if total is None else total + mix
                tops.append(top)
            sums = [total[:, :LANES], total[:, LANES:]]
            if prior is not None:
                scale = jnp.where(low, scales[0], scales[1])
                for n in range(2):
                    sums[n] = sums[n] + prior[0][n, here, pair * LANES : (pair + 1) * LANES] * scale
            sink(pair, part, sums, tops)


def keep_state(sums_ref, tops_ref):
    def sink(pair, part, sums, tops):
        here = pl.ds(part * LANES, LANES)
        for n in range(2):
            sums_ref[n, here, pair * LANES : (pair + 1) * LANES] = sums[n]
            tops_ref[2 * pair + n, here, :] = tops[n]

    return sink


def keep_heads(attended_ref):
    def sink(pair, part, sums, tops):
        attended_ref[pl.ds(part * LANES, LANES), pair * LANES : (pair + 1) * LANES] = (
            sums[0] / sums[1]
        ).astype(jnp.bfloat16)

    return sink


def window_mask(extent_ref, places, valid):
    row = lax.broadcasted_iota(jnp.int32, (LANES, LANES), 0)
    col = lax.broadcasted_iota(jnp.int32, (LANES, LANES), 1)
    gap = row - col

    def mask(pair, s, part, tiles):
        extent = extent_ref[2 * pair + s]
        out = []
        for tile, (ahead, side) in zip(tiles, places[part]):
            reach = extent if side is None else jnp.where(valid[side], extent, -1)
            if ahead < 0:
                seen = gap <= reach + ahead
            elif ahead > 0:
                seen = gap >= ahead - reach
            else:
                seen = jnp.abs(gap) <= reach
            out.append(jnp.where(seen, tile, LOW))
        return out, out, [None] * len(out)

    return mask


def own_window_kernel(
    extent_hbm, q_hbm, own_hbm, q_ref, sums_ref, tops_ref, extent_ref, own_ref, keys_ref, values_ref, sems
):
    copies = start_copies(((own_hbm, own_ref), (q_hbm, q_ref), (extent_hbm, extent_ref)), sems)
    rows = own_ref.shape[0]
    copies[0].wait()
    spread_keyvals(own_ref[...], keys_ref, values_ref, 0)
    for copy in copies[1:]:
        copy.wait()
    ranges, places = [], []
    for first in range(0, rows, LANES):
        near = [k for k in range(0, rows, LANES) if abs(k - first) < WIN + LANES]
        ranges.append((near[0], len(near) * LANES))
        places.append([(k - first, None) for k in near])
    attend(
        q_ref,
        keys_ref,
        values_ref,
        ranges,
        window_mask(extent_ref, places, None),
        None,
        keep_state(sums_ref, tops_ref),
    )


def halo_window_kernel(
    extent_hbm,
    q_ref,
    even_ref,
    odd_ref,
    sums_ref,
    tops_ref,
    residual_hbm,
    out_w_hbm,
    kv_w_hbm,
    hidden_ref,
    normed_ref,
    kv_ref,
    extent_ref,
    keys_ref,
    values_ref,
    attended_ref,
    residual_ref,
    out_w_ref,
    kv_w_ref,
    sems,
):
    copies = start_copies(
        (
            (extent_hbm, extent_ref),
            (out_w_hbm, out_w_ref),
            (residual_hbm, residual_ref),
            (kv_w_hbm, kv_w_ref),
        ),
        sems,
    )
    rows = q_ref.shape[0]
    me = lax.axis_index("seq")
    valid = (me > 0, me < lax.axis_size("seq") - 1)
    left_is_even = lax.rem(me, 2)
    for block, after in ((even_ref, 1 - left_is_even), (odd_ref, left_is_even)):
        spread_keyvals(block[...], keys_ref, values_ref, pl.multiple_of(after * WIN, WIN))
    copies[0].wait()
    ranges, places = [], []
    for first in range(0, rows, LANES):
        left = [(k - first, 0) for k in range(-WIN, 0, LANES) if first - k < WIN + LANES]
        right = [
            (k - first, 1) for k in range(rows, rows + WIN, LANES) if k - first < WIN + LANES
        ]
        places.append(left + right)
        ranges.append((WIN - len(left) * LANES, len(left + right) * LANES))
    attend(
        q_ref,
        keys_ref,
        values_ref,
        ranges,
        window_mask(extent_ref, places, valid),
        (sums_ref, tops_ref),
        keep_heads(attended_ref),
    )
    for copy in copies[1:]:
        copy.wait()
    hidden = (
        dot(attended_ref[...], out_w_ref[...]) + residual_ref[...].astype(jnp.float32)
    ).astype(jnp.bfloat16)
    hidden_ref[...] = hidden
    values = hidden.astype(jnp.float32)
    scale = lax.rsqrt(jnp.mean(values * values, axis=-1, keepdims=True) + 1e-05)
    normed = (values * scale).astype(jnp.bfloat16)
    normed_ref[...] = normed
    kv_ref[...] = dot(normed, kv_w_ref[...]).astype(jnp.bfloat16)


def open_mask(tiles_per_block, shut):
    def mask(pair, s, part, tiles):
        tops, bases = [], []
        for n, one in enumerate(shut):
            block = tiles[n * tiles_per_block : (n + 1) * tiles_per_block]
            top = functools.reduce(jnp.maximum, block)
            tops.append(top if one is None else top - one)
            bases += [one] * tiles_per_block
        return tiles, tops, bases

    return mask


def own_butterfly_kernel(
    levels,
    mask_hbm,
    normed_ref,
    q_w_ref,
    own_ref,
    q_ref,
    sums_ref,
    tops_ref,
    shut_ref,
    mask_ref,
    keys_ref,
    values_ref,
    sems,
):
    copies = start_copies(((mask_hbm, mask_ref),), sems)
    rows = normed_ref.shape[0]
    q_ref[...] = dot(normed_ref[...], q_w_ref[...]).astype(jnp.bfloat16)
    spread_keyvals(own_ref[...], keys_ref, values_ref, 0)
    attend(
        q_ref,
        keys_ref,
        values_ref,
        [(0, rows)] * (rows // LANES),
        open_mask(rows // LANES, [None]),
        None,
        keep_state(sums_ref, tops_ref),
    )
    copies[0].wait()
    for level in range(levels):
        shut = jnp.where(mask_ref[0, level] == 1, 0.0, -LOW)
        shut_ref[level] = jnp.full(shut_ref.shape[1:], shut, jnp.float32)


def more_butterfly_kernel(levels, last, *refs):
    blocks, refs = refs[: len(levels)], refs[len(levels) :]
    (shut_ref, q_ref, sums_ref, tops_ref), refs = refs[:4], refs[4:]
    rows = q_ref.shape[0]
    if last:
        hidden_ref, out_w_ref, out_ref, keys_ref, values_ref, attended_ref = refs
        sink = keep_heads(attended_ref)
    else:
        sums_out_ref, tops_out_ref, keys_ref, values_ref = refs
        sink = keep_state(sums_out_ref, tops_out_ref)
    for n, block in enumerate(blocks):
        spread_keyvals(block[...], keys_ref, values_ref, n * rows)
    shut = [jnp.broadcast_to(shut_ref[level, :1, :], (LANES, LANES)) for level in levels]
    attend(
        q_ref,
        keys_ref,
        values_ref,
        [(0, rows * len(levels))] * (rows // LANES),
        open_mask(rows // LANES, shut),
        (sums_ref, tops_ref),
        sink,
    )
    if last:
        out_ref[...] = (
            dot(attended_ref[...], out_w_ref[...]) + hidden_ref[...].astype(jnp.float32)
        ).astype(jnp.bfloat16)


def exchange_edges(block, parity):
    groups, count = lax.axis_size("groups"), lax.axis_size("seq")
    rows = block.shape[0]
    if rows > WIN:
        first = jnp.where(lax.rem(lax.axis_index("seq"), 2) == parity, rows - WIN, 0)
        block = lax.dynamic_slice_in_dim(block, first, WIN, 0)
    route = []
    for group in range(groups):
        for i in range(count):
            other, to = group, i + 1 if i % 2 == parity else i - 1
            if not 0 <= to < count:
                other, to = (group ^ 1 if group ^ 1 < groups else group), i
            route.append((group * count + i, other * count + to))
    return lax.ppermute(block, ("groups", "seq"), route)


def shards(
    residual,
    layer_queries,
    layer_keyvals,
    head_window_extent,
    block_mask,
    first_out,
    second_query,
    second_keyval,
    second_out,
):
    rows, width = residual.shape
    q_width = layer_queries.shape[1]
    kv_width = layer_keyvals.shape[1]
    kv_heads = kv_width // (2 * HEAD_SIZE)
    heads = q_width // HEAD_SIZE
    count = lax.axis_size("seq")
    level_count = count.bit_length() - 1
    bf16, f32 = jnp.bfloat16, jnp.float32
    vmem = pl.BlockSpec(memory_space=pltpu.VMEM)
    hbm = pl.BlockSpec(memory_space=pltpu.HBM)
    state = [
        jax.ShapeDtypeStruct((2, rows, q_width), f32),
        jax.ShapeDtypeStruct((heads, rows, LANES), f32),
    ]
    queries = jax.ShapeDtypeStruct((rows, q_width), bf16)
    wide = jax.ShapeDtypeStruct((rows, width), bf16)

    def call(kernel, name, in_specs, out_shape, scratch, key_rows, extra_macs, args):
        macs = 4 * rows * heads * HEAD_SIZE * key_rows + extra_macs
        spread = [
            pltpu.VMEM((kv_heads, 2, key_rows, LANES), bf16),
            pltpu.VMEM((kv_heads, 2, key_rows, 2 * LANES), bf16),
        ]
        at = next((n for n, one in enumerate(scratch) if one is None))
        return pl.pallas_call(
            kernel,
            out_shape=out_shape,
            in_specs=in_specs,
            out_specs=jax.tree.map(lambda _: vmem, out_shape),
            scratch_shapes=scratch[:at] + spread + scratch[at + 1 :],
            compiler_params=pltpu.CompilerParams(vmem_limit_bytes=VMEM_LIMIT),
            cost_estimate=pl.CostEstimate(
                flops=16 * macs, bytes_accessed=2**21, transcendentals=rows * heads * key_rows
            ),
            name=name,
        )(*args)

    even, odd = (exchange_edges(layer_keyvals, parity) for parity in range(2))
    q_here, sums, tops = call(
        own_window_kernel,
        "own_window",
        [hbm] * 3,
        [queries] + state,
        [
            pltpu.SMEM(head_window_extent.shape, jnp.int32),
            pltpu.VMEM(layer_keyvals.shape, bf16),
            None,
            pltpu.SemaphoreType.DMA((3,)),
        ],
        rows,
        0,
        (head_window_extent, layer_queries, layer_keyvals),
    )
    hidden, normed, keyvals = call(
        halo_window_kernel,
        "halo_window",
        [hbm] + [vmem] * 5 + [hbm] * 3,
        [wide, wide, jax.ShapeDtypeStruct((rows, kv_width), bf16)],
        [
            pltpu.SMEM(head_window_extent.shape, jnp.int32),
            None,
            pltpu.VMEM((rows, q_width), bf16),
            pltpu.VMEM(residual.shape, bf16),
            pltpu.VMEM(first_out.shape, bf16),
            pltpu.VMEM(second_keyval.shape, bf16),
            pltpu.SemaphoreType.DMA((4,)),
        ],
        2 * WIN,
        rows * width * (q_width + kv_width),
        (
            head_window_extent,
            q_here,
            even,
            odd,
            sums,
            tops,
            residual,
            first_out,
            second_keyval,
        ),
    )

    others = [None] * level_count
    for level in reversed(range(level_count)):
        route = [(i, i ^ (1 << level)) for i in range(count)]
        others[level] = lax.ppermute(keyvals, "seq", route)
    queries_two, sums, tops, shut = call(
        functools.partial(own_butterfly_kernel, level_count),
        "own_butterfly",
        [hbm] + [vmem] * 3,
        [queries] + state + [jax.ShapeDtypeStruct((level_count, 8, LANES), f32)],
        [pltpu.SMEM(block_mask.shape, jnp.int32), None, pltpu.SemaphoreType.DMA((1,))],
        rows,
        rows * width * q_width,
        (block_mask, normed, second_query, keyvals),
    )
    cut = (level_count + 1) // 2
    groups = [list(reversed(range(cut))), list(reversed(range(cut, level_count)))]
    for levels in groups[:-1]:
        sums, tops = call(
            functools.partial(more_butterfly_kernel, levels, False),
            "near_butterfly",
            [vmem] * (4 + len(levels)),
            state,
            [None],
            rows * len(levels),
            0,
            (*[others[level] for level in levels], shut, queries_two, sums, tops),
        )
    levels = groups[-1]
    return call(
        functools.partial(more_butterfly_kernel, levels, True),
        "far_butterfly",
        [vmem] * (6 + len(levels)),
        wide,
        [None, pltpu.VMEM((rows, q_width), bf16)],
        rows * len(levels),
        rows * width * q_width,
        (*[others[level] for level in levels], shut, queries_two, sums, tops, hidden, second_out),
    )


def solution(mesh):
    tokens = P(("groups", "seq"), None)
    placed = (tokens, tokens, tokens, P(), P("seq", None), P(), P(), P(), P())
    return jax.shard_map(shards, mesh=mesh, in_specs=placed, out_specs=tokens, check_vma=False)
```

time: 38.7 us -> 25.2 us (0.65)
  waiting for transfers between devices: 9.08 us -> 1.59 us
  local copies, waits for them, and re-layouts: 6.46 us -> 2.54 us
  starting transfers between devices: 11.9 us -> 8.7 us
  Pallas kernels: 10.9 us -> 12.1 us
    ppermute x2, waiting for transfers between devices: 4.24 us -> 0.01 us  [exchange_edges(): return lax.ppermute(block, ('groups', 'seq'), route)]
    unnamed x18, local copies, waits for them, and re-layouts: 6.46 us -> 2.54 us
    ppermute x4, waiting for transfers between devices: 4.84 us -> 1.59 us  [shards(): others[level] = lax.ppermute(keyvals, 'seq', route)]
    ppermute x4, starting transfers between devices: 8.09 us -> 5.59 us  [shards(): others[level] = lax.ppermute(keyvals, 'seq', route)]
    pallas_call x2 -> x5, Pallas kernels: 10.9 us -> 12.1 us  [call(): pl.pallas_call(kernel, out_shape=out_shape, in_specs=in_specs, out_specs=...]
    ppermute x2, starting transfers between devices: 3.78 us -> 3.11 us  [exchange_edges(): return lax.ppermute(block, ('groups', 'seq'), route)]
  transfers between devices with their start and end apart: 6 -> 6, of which waited for: 3 -> 2; matrix products, arithmetic and copies ran while one was open for 0% -> 0% of each run, Pallas kernels for 0% -> 21%
where the time goes in v2:
time: 25.2 us; the launch traced here: 25.1 us
  Pallas kernels  12.1 us (48%)
  starting transfers between devices  8.7 us (35%)
  local copies, waits for them, and re-layouts  2.54 us (10%)
  waiting for transfers between devices  1.59 us (6%)
    pallas_call x5, Pallas kernels, call(): pl.pallas_call(kernel, out_shape=out_shape, in_specs=in_specs, out_specs=...  12.1 us
    ppermute x4, starting transfers between devices, shards(): others[level] = lax.ppermute(keyvals, 'seq', route)  5.59 us
    ppermute x2, starting transfers between devices, exchange_edges(): return lax.ppermute(block, ('groups', 'seq'), route)  3.11 us
    unnamed x18, local copies, waits for them, and re-layouts  2.54 us
    ppermute x4, waiting for transfers between devices, shards(): others[level] = lax.ppermute(keyvals, 'seq', route)  1.59 us
  transfers between devices with their start and end apart: 6, of which 2 were waited for; matrix products, arithmetic and copies ran while one was open for 0% of the time, Pallas kernels for 21%

profile of v2, /device:TPU:0, one launch (start us, length us, event | category | flops | bytes accessed | tf_op | source)
XLA Modules:
  0.0 25.1 jit_solution(2659349534360971801)
XLA Ops:
  0.0 0.5 %collective-permute-start = (bf16[256,256]{1,0:T(8,128)(2,1)}, bf16[256,256]{1,0:T(8,128)(2,1)S(1)}, u32[]{:S(2)}, u32[]{:S(2)}) collective-permute-start(bf16[256,256]{1,0:T(8,128)(2,1)} %own_hbm.1), channel_id=1, source_target_pairs={{0,1},{1,0},{2,3},{3,2},{4,5},{5,4},{6,7},{7,6},{8,9},{9,8},{10,11... | collective-permute-start | bytes 393224 | tf_op jit(solution)/shard_map/ppermute | solution.py:318
  0.5 2.6 %collective-permute-start.1 = (bf16[256,256]{1,0:T(8,128)(2,1)}, bf16[256,256]{1,0:T(8,128)(2,1)S(1)}, u32[]{:S(2)}, u32[]{:S(2)}) collective-permute-start(bf16[256,256]{1,0:T(8,128)(2,1)} %own_hbm.1), channel_id=1, source_target_pairs={{0,16},{1,2},{2,1},{3,4},{4,3},{5,6},{6,5},{7,8},{8,7},{9,10},{10,... | collective-permute-start | bytes 393224 | tf_op jit(solution)/shard_map/ppermute | solution.py:318
  3.1 0.9 %copy-done.5 = bf16[256,512]{1,0:T(8,128)(2,1)S(1)} copy-done((bf16[256,512]{1,0:T(8,128)(2,1)S(1)}, bf16[256,512]{1,0:T(8,128)(2,1)}, u32[]{:S(2)}) %copy-start.5) | copy-done | bytes 262168
  4.1 0.9 %copy-done.6 = bf16[256,256]{1,0:T(8,128)(2,1)S(1)} copy-done((bf16[256,256]{1,0:T(8,128)(2,1)S(1)}, bf16[256,256]{1,0:T(8,128)(2,1)}, u32[]{:S(2)}) %copy-start.6) | copy-done | bytes 131096
  5.0 0.7 %copy-done.7 = s32[8]{0:T(128)S(1)} copy-done((s32[8]{0:T(128)S(1)}, s32[8]{0:T(128)}, u32[]{:S(2)}) %copy-start.7) | copy-done | bytes 56
  5.6 1.7 %own_window.1 = (bf16[256,512]{1,0:T(8,128)(2,1)S(1)}, f32[2,256,512]{2,1,0:T(8,128)S(1)}, f32[8,256,128]{2,1,0:T(8,128)S(1)}) custom-call(s32[8]{0:T(128)S(1)} %copy-done.7, bf16[256,512]{1,0:T(8,128)(2,1)S(1)} %copy-done.5, bf16[256,256]{1,0:T(8,128)(2,1)S(1)} %copy-done.6), custom_call_target="tpu_custom_call" | custom-call | flops 2147483648 | bytes 2097152 | tf_op jit(solution)/shard_map/own_window/pallas_call | solution.py:356
  7.3 0.0 collective-permute-done.even_ref
  7.4 0.0 collective-permute-done.1.odd_ref
  7.4 0.0 copy-done
  7.4 0.0 copy-start.1
  7.4 3.5 %halo_window.1 = (bf16[256,1024]{1,0:T(8,128)(2,1)S(1)}, bf16[256,1024]{1,0:T(8,128)(2,1)S(1)}, bf16[256,256]{1,0:T(8,128)(2,1)S(1)}) custom-call(s32[8]{0:T(128)S(1)} %copy-done.7, bf16[256,512]{1,0:T(8,128)(2,1)S(1)} %get-tuple-element.17.q_ref, bf16[256,256]{1,0:T(8,128)(2,1)S(1)} %collective-permute-done.even_ref, ...), custom_call_target="tpu_custom_call" | custom-call | flops 7516192768 | bytes 2097152 | tf_op jit(solution)/shard_map/halo_window/pallas_call | solution.py:356
  10.9 0.0 copy-start.8
  10.9 0.4 %collective-permute-start.4 = (bf16[256,256]{1,0:T(8,128)(2,1)S(1)}, bf16[256,256]{1,0:T(8,128)(2,1)S(1)}, u32[]{:S(2)}, u32[]{:S(2)}) collective-permute-start(bf16[256,256]{1,0:T(8,128)(2,1)S(1)} %get-tuple-element.20.own_ref), channel_id=1, source_target_pairs={{0,2},{1,3},{2,0},{3,1},{4,6},{5,7},{6,4},{7,5},{8,10},{9,11},{10,... | collective-permute-start | bytes 393224 | tf_op jit(solution)/shard_map/ppermute | solution.py:417
  11.3 1.1 %collective-permute-start.5 = (bf16[256,256]{1,0:T(8,128)(2,1)S(1)}, bf16[256,256]{1,0:T(8,128)(2,1)S(1)}, u32[]{:S(2)}, u32[]{:S(2)}) collective-permute-start(bf16[256,256]{1,0:T(8,128)(2,1)S(1)} %get-tuple-element.20.own_ref), channel_id=1, source_target_pairs={{0,1},{1,0},{2,3},{3,2},{4,5},{5,4},{6,7},{7,6},{8,9},{9,8},{10,11... | collective-permute-start | bytes 393224 | tf_op jit(solution)/shard_map/ppermute | solution.py:417
  12.3 2.6 %collective-permute-start.2 = (bf16[256,256]{1,0:T(8,128)(2,1)S(1)}, bf16[256,256]{1,0:T(8,128)(2,1)S(1)}, u32[]{:S(2)}, u32[]{:S(2)}) collective-permute-start(bf16[256,256]{1,0:T(8,128)(2,1)S(1)} %get-tuple-element.20.own_ref), channel_id=1, source_target_pairs={{0,8},{1,9},{2,10},{3,11},{4,12},{5,13},{6,14},{7,15},{8,0},{9,1},... | collective-permute-start | bytes 393224 | tf_op jit(solution)/shard_map/ppermute | solution.py:417
  14.9 1.6 %collective-permute-start.3 = (bf16[256,256]{1,0:T(8,128)(2,1)S(1)}, bf16[256,256]{1,0:T(8,128)(2,1)S(1)}, u32[]{:S(2)}, u32[]{:S(2)}) collective-permute-start(bf16[256,256]{1,0:T(8,128)(2,1)S(1)} %get-tuple-element.20.own_ref), channel_id=1, source_target_pairs={{0,4},{1,5},{2,6},{3,7},{4,0},{5,1},{6,2},{7,3},{8,12},{9,13},{10,... | collective-permute-start | bytes 393224 | tf_op jit(solution)/shard_map/ppermute | solution.py:417
  16.5 1.4 %own_butterfly.1 = (bf16[256,512]{1,0:T(8,128)(2,1)S(1)}, f32[2,256,512]{2,1,0:T(8,128)S(1)}, f32[8,256,128]{2,1,0:T(8,128)S(1)}, f32[4,8,128]{2,1,0:T(8,128)S(1)}) custom-call(s32[1,4]{1,0:T(1,128)S(1)} %copy-done.8, bf16[256,1024]{1,0:T(8,128)(2,1)S(1)} %get-tuple-element.21.normed_ref, bf16[1024,512]{1,0:T(8,128)(2,1)S(1)} %copy-done.1, ...), custom_call_target="tpu_custom_call" | custom-call | flops 4294967296 | bytes 2097152 | tf_op jit(solution)/shard_map/own_butterfly/pallas_call | solution.py:356
  17.9 0.0 collective-permute-done.4.refs_0_
  17.9 0.0 collective-permute-done.5.refs_1_
  17.9 0.0 copy-start.2
  17.9 2.3 %near_butterfly.1 = (f32[2,256,512]{2,1,0:T(8,128)S(1)}, f32[8,256,128]{2,1,0:T(8,128)S(1)}) custom-call(bf16[256,256]{1,0:T(8,128)(2,1)S(1)} %collective-permute-done.4.refs_0_, bf16[256,256]{1,0:T(8,128)(2,1)S(1)} %collective-permute-done.5.refs_1_, f32[4,8,128]{2,1,0:T(8,128)S(1)} %get-tuple-element.22.refs_2_, ...), custom_call_target="tpu_custom_call" | custom-call | flops 4294967296 | bytes 2097152 | tf_op jit(solution)/shard_map/near_butterfly/pallas_call | solution.py:356
  20.2 1.4 %collective-permute-done.2.refs_0_ = bf16[256,256]{1,0:T(8,128)(2,1)S(1)} collective-permute-done((bf16[256,256]{1,0:T(8,128)(2,1)S(1)}, bf16[256,256]{1,0:T(8,128)(2,1)S(1)}, u32[]{:S(2)}, u32[]{:S(2)}) %collective-permute-start.2) | collective-permute-done | bytes 131104 | tf_op jit(solution)/shard_map/ppermute | solution.py:417
  21.6 0.2 collective-permute-done.3.refs_1_
  21.8 3.3 %far_butterfly.1 = bf16[256,1024]{1,0:T(8,128)(2,1)} custom-call(bf16[256,256]{1,0:T(8,128)(2,1)S(1)} %collective-permute-done.2.refs_0_, bf16[256,256]{1,0:T(8,128)(2,1)S(1)} %collective-permute-done.3.refs_1_, f32[4,8,128]{2,1,0:T(8,128)S(1)} %get-tuple-element.22.refs_2_, bf16[256,512]{1,0:T(8,128)(2,1)S(1)} %get-tuple-element.23.refs_3_, ...), custom_call_target="tpu_custom_call" | custom-call | flops 6442450944 | bytes 2097152 | tf_op jit(solution)/shard_map/far_butterfly/pallas_call | solution.py:356
  (11 shorter events, 0.0 us)
Async XLA Ops:
  0.0 7.4 %copy-start = (bf16[512,1024]{1,0:T(8,128)(2,1)S(1)}, bf16[512,1024]{1,0:T(8,128)(2,1)}, u32[]{:S(2)}) copy-start(bf16[512,1024]{1,0:T(8,128)(2,1)} %out_w_hbm.1) | copy-start | bytes 3145732
  0.0 7.4 %copy-start.4 = (bf16[1024,256]{1,0:T(8,128)(2,1)S(1)}, bf16[1024,256]{1,0:T(8,128)(2,1)}, u32[]{:S(2)}) copy-start(bf16[1024,256]{1,0:T(8,128)(2,1)} %kv_w_hbm.1) | copy-start | bytes 1572868
  0.0 7.4 %copy-start.3 = (bf16[256,1024]{1,0:T(8,128)(2,1)S(1)}, bf16[256,1024]{1,0:T(8,128)(2,1)}, u32[]{:S(2)}) copy-start(bf16[256,1024]{1,0:T(8,128)(2,1)} %residual_hbm.1) | copy-start | bytes 1572868
  0.0 7.3 %collective-permute-start = (bf16[256,256]{1,0:T(8,128)(2,1)}, bf16[256,256]{1,0:T(8,128)(2,1)S(1)}, u32[]{:S(2)}, u32[]{:S(2)}) collective-permute-start(bf16[256,256]{1,0:T(8,128)(2,1)} %own_hbm.1), channel_id=1, source_target_pairs={{0,1},{1,0},{2,3},{3,2},{4,5},{5,4},{6,7},{7,6},{8,9},{9,8},{10,11... | collective-permute-start | bytes 393224 | tf_op jit(solution)/shard_map/ppermute | solution.py:318
  0.5 6.8 %collective-permute-start.1 = (bf16[256,256]{1,0:T(8,128)(2,1)}, bf16[256,256]{1,0:T(8,128)(2,1)S(1)}, u32[]{:S(2)}, u32[]{:S(2)}) collective-permute-start(bf16[256,256]{1,0:T(8,128)(2,1)} %own_hbm.1), channel_id=1, source_target_pairs={{0,16},{1,2},{2,1},{3,4},{4,3},{5,6},{6,5},{7,8},{8,7},{9,10},{10,... | collective-permute-start | bytes 393224 | tf_op jit(solution)/shard_map/ppermute | solution.py:318
  3.1 0.9 %copy-start.5 = (bf16[256,512]{1,0:T(8,128)(2,1)S(1)}, bf16[256,512]{1,0:T(8,128)(2,1)}, u32[]{:S(2)}) copy-start(bf16[256,512]{1,0:T(8,128)(2,1)} %q_hbm.1) | copy-start | bytes 786436
  4.1 0.9 %copy-start.6 = (bf16[256,256]{1,0:T(8,128)(2,1)S(1)}, bf16[256,256]{1,0:T(8,128)(2,1)}, u32[]{:S(2)}) copy-start(bf16[256,256]{1,0:T(8,128)(2,1)} %own_hbm.1) | copy-start | bytes 393220
  5.0 0.7 %copy-start.7 = (s32[8]{0:T(128)S(1)}, s32[8]{0:T(128)}, u32[]{:S(2)}) copy-start(s32[8]{0:T(128)} %extent_hbm.3) | copy-start | bytes 100
  7.4 9.1 %copy-start.1 = (bf16[1024,512]{1,0:T(8,128)(2,1)S(1)}, bf16[1024,512]{1,0:T(8,128)(2,1)}, u32[]{:S(2)}) copy-start(bf16[1024,512]{1,0:T(8,128)(2,1)} %q_w_ref.1) | copy-start | bytes 3145732
  10.9 5.6 %copy-start.8 = (s32[1,4]{1,0:T(1,128)S(1)}, s32[1,4]{1,0:T(1,128)}, u32[]{:S(2)}) copy-start(s32[1,4]{1,0:T(1,128)} %mask_hbm.1) | copy-start | bytes 52
  10.9 7.0 %collective-permute-start.4 = (bf16[256,256]{1,0:T(8,128)(2,1)S(1)}, bf16[256,256]{1,0:T(8,128)(2,1)S(1)}, u32[]{:S(2)}, u32[]{:S(2)}) collective-permute-start(bf16[256,256]{1,0:T(8,128)(2,1)S(1)} %get-tuple-element.20.own_ref), channel_id=1, source_target_pairs={{0,2},{1,3},{2,0},{3,1},{4,6},{5,7},{6,4},{7,5},{8,10},{9,11},{10,... | collective-permute-start | bytes 393224 | tf_op jit(solution)/shard_map/ppermute | solution.py:417
  11.3 6.6 %collective-permute-start.5 = (bf16[256,256]{1,0:T(8,128)(2,1)S(1)}, bf16[256,256]{1,0:T(8,128)(2,1)S(1)}, u32[]{:S(2)}, u32[]{:S(2)}) collective-permute-start(bf16[256,256]{1,0:T(8,128)(2,1)S(1)} %get-tuple-element.20.own_ref), channel_id=1, source_target_pairs={{0,1},{1,0},{2,3},{3,2},{4,5},{5,4},{6,7},{7,6},{8,9},{9,8},{10,11... | collective-permute-start | bytes 393224 | tf_op jit(solution)/shard_map/ppermute | solution.py:417
  12.3 9.2 %collective-permute-start.2 = (bf16[256,256]{1,0:T(8,128)(2,1)S(1)}, bf16[256,256]{1,0:T(8,128)(2,1)S(1)}, u32[]{:S(2)}, u32[]{:S(2)}) collective-permute-start(bf16[256,256]{1,0:T(8,128)(2,1)S(1)} %get-tuple-element.20.own_ref), channel_id=1, source_target_pairs={{0,8},{1,9},{2,10},{3,11},{4,12},{5,13},{6,14},{7,15},{8,0},{9,1},... | collective-permute-start | bytes 393224 | tf_op jit(solution)/shard_map/ppermute | solution.py:417
  14.9 6.8 %collective-permute-start.3 = (bf16[256,256]{1,0:T(8,128)(2,1)S(1)}, bf16[256,256]{1,0:T(8,128)(2,1)S(1)}, u32[]{:S(2)}, u32[]{:S(2)}) collective-permute-start(bf16[256,256]{1,0:T(8,128)(2,1)S(1)} %get-tuple-element.20.own_ref), channel_id=1, source_target_pairs={{0,4},{1,5},{2,6},{3,7},{4,0},{5,1},{6,2},{7,3},{8,12},{9,13},{10,... | collective-permute-start | bytes 393224 | tf_op jit(solution)/shard_map/ppermute | solution.py:417
  17.9 3.9 %copy-start.2 = (bf16[512,1024]{1,0:T(8,128)(2,1)S(1)}, bf16[512,1024]{1,0:T(8,128)(2,1)}, u32[]{:S(2)}) copy-start(bf16[512,1024]{1,0:T(8,128)(2,1)} %refs_7_.1) | copy-start | bytes 3145732

commit v3 on v2

v3 whole, which is shorter than its diff:
```python
import functools
import math

import jax
import jax.numpy as jnp
from jax import lax
from jax.experimental import pallas as pl
from jax.experimental.pallas import tpu as pltpu
from jax.sharding import PartitionSpec as P

HEAD_SIZE = 64
WIN = 256
LANES = 128
LOW = -1e30
SCALE = HEAD_SIZE**-0.5 * math.log2(math.e)
VMEM_LIMIT = 20 * 2**20
ROWS = 256


def dot(a, b):
    return jnp.dot(a, b, preferred_element_type=jnp.float32)


def dot_t(a, b):
    return lax.dot_general(a, b, (((1,), (1,)), ((), ())), preferred_element_type=jnp.float32)


def swap_halves(tile):
    return jnp.concatenate([tile[:, HEAD_SIZE:], tile[:, :HEAD_SIZE]], axis=1)


def low_half(rows):
    return lax.broadcasted_iota(jnp.int32, (rows, LANES), 1) < HEAD_SIZE


def spread_queries(queries, kv_heads, spread_ref):
    rows, width = queries.shape
    heads = width // HEAD_SIZE
    low = low_half(rows)
    for head in range(heads):
        at, want = head % 2, head * kv_heads // heads % 2
        tile = queries[:, head // 2 * LANES : (head // 2 + 1) * LANES]
        if at != want:
            tile = swap_halves(tile)
        here = low if want == 0 else jnp.logical_not(low)
        spread_ref[head] = jnp.where(here, tile, jnp.zeros_like(tile))


def spread_values(keyvals, values_ref, first, shown=None):
    rows, width = keyvals.shape
    kv_heads = width // (2 * HEAD_SIZE)
    low = low_half(rows)
    for g in range(kv_heads):
        begin = width // 2 + g // 2 * LANES
        tile = keyvals[:, begin : begin + LANES]
        other = swap_halves(tile)
        for s in range(2):
            here = low if s == 0 else jnp.logical_not(low)
            out = jnp.where(here, tile if g % 2 == s else other, jnp.ones_like(tile))
            if shown is not None:
                out = out * shown
            values_ref[g, s, pl.ds(first, rows), :] = out


def attend(q_ref, key_refs, values_ref, parts, mask, prior, sink):
    heads = q_ref.shape[0]
    kv_heads = values_ref.shape[0]
    steps = [
        (g, s, [h for h in range(heads) if h * kv_heads // heads == g and h % 2 == s], part)
        for g in range(kv_heads)
        for s in range(2)
        for part in range(len(parts))
    ]

    def score(g, s, mine, part):
        row, rows, key, span = parts[part]
        q = jnp.concatenate([q_ref[h, pl.ds(row, rows), :] for h in mine], axis=0)
        tiles, at = [], 0
        for ref in key_refs:
            begin, end = max(key - at, 0), min(key + span - at, ref.shape[0])
            if begin < end:
                keys = ref[pl.ds(begin, end - begin), pl.ds(g // 2 * LANES, LANES)]
                scores = dot_t(q, keys)
                tiles += [scores[:, c : c + LANES] for c in range(0, end - begin, LANES)]
            at += ref.shape[0]
        return tiles

    def mix(g, s, mine, part, tiles):
        row, rows, key, span = parts[part]
        here = pl.ds(row, rows)
        weights, tops, scales = [], [], []
        for n, h in enumerate(mine):
            some = mask(h, part, [tile[n * rows : (n + 1) * rows] for tile in tiles])
            top = jnp.max(functools.reduce(jnp.maximum, some), axis=1, keepdims=True)
            top = jnp.broadcast_to(top, (rows, LANES))
            if prior is not None:
                old = prior[1][h, here, :]
                top = jnp.maximum(top, old)
                scales.append(jnp.exp2((old - top) * SCALE))
            tops.append(top)
            weights.append(
                jnp.concatenate(
                    [jnp.exp2((tile - top) * SCALE).astype(jnp.bfloat16) for tile in some], axis=1
                )
            )
        sums = dot(jnp.concatenate(weights, axis=0), values_ref[g, s, pl.ds(key, span), :])
        for n, h in enumerate(mine):
            one = sums[n * rows : (n + 1) * rows]
            if prior is not None:
                one = one + prior[0][h, here, :] * scales[n]
            sink(h, here, one, tops[n])

    tiles = score(*steps[0])
    for n, step in enumerate(steps):
        ahead = score(*steps[n + 1]) if n + 1 < len(steps) else None
        mix(*step, tiles)
        tiles = ahead


def keep_state(sums_ref, tops_ref):
    def sink(head, here, sums, top):
        sums_ref[head, here, :] = sums
        tops_ref[head, here, :] = top

    return sink


def keep_sums(sums_ref):
    def sink(head, here, sums, top):
        sums_ref[head, here, :] = sums

    return sink


def divide_pairs(sums_ref):
    heads, rows, _ = sums_ref.shape
    low = low_half(rows)
    out = []
    for head in range(0, heads, 2):
        even, odd = sums_ref[head], sums_ref[head + 1]
        total = swap_halves(jnp.where(low, odd, even))
        out.append((jnp.where(low, even, odd) / total).astype(jnp.bfloat16))
    return jnp.concatenate(out, axis=1)


def window_mask(extent_ref, places, valid):
    def mask(head, part, tiles):
        extent = extent_ref[head]
        shape = tiles[0].shape
        gap = lax.broadcasted_iota(jnp.int32, shape, 0) - lax.broadcasted_iota(jnp.int32, shape, 1)
        out = []
        for tile, (ahead, side) in zip(tiles, places[part]):
            reach = extent if side is None else jnp.where(valid[side], extent, -1)
            if ahead <= -shape[1]:
                seen = gap <= reach + ahead
            elif ahead >= shape[0]:
                seen = gap >= ahead - reach
            else:
                seen = jnp.abs(gap - ahead) <= reach
            out.append(jnp.where(seen, tile, LOW))
        return out

    return mask


def own_window_kernel(
    extent_ref, queries_ref, own_ref, q_ref, sums_ref, tops_ref, values_ref
):
    rows = own_ref.shape[0]
    kv_heads = values_ref.shape[0]
    spread_queries(queries_ref[...], kv_heads, q_ref)
    spread_values(own_ref[...], values_ref, 0)
    step = min(rows, ROWS)
    parts, places = [], []
    for row in range(0, rows, step):
        near = [k for k in range(0, rows, LANES) if row - k < WIN + LANES and k - row < WIN + step]
        parts.append((row, step, near[0], len(near) * LANES))
        places.append([(k - row, None) for k in near])
    attend(
        q_ref,
        [own_ref],
        values_ref,
        parts,
        window_mask(extent_ref, places, None),
        None,
        keep_state(sums_ref, tops_ref),
    )


def halo_window_kernel(
    extent_ref,
    q_ref,
    even_ref,
    odd_ref,
    sums_ref,
    tops_ref,
    residual_ref,
    out_w_ref,
    kv_w_ref,
    hidden_ref,
    normed_ref,
    kv_ref,
    values_ref,
    keys_ref,
    all_sums_ref,
):
    rows = q_ref.shape[1]
    key_width = even_ref.shape[1] // 2
    me = lax.axis_index("seq")
    valid = (me > 0, me < lax.axis_size("seq") - 1)
    left_is_even = lax.rem(me, 2)
    for block, after in ((even_ref, 1 - left_is_even), (odd_ref, left_is_even)):
        first = pl.multiple_of(after * WIN, WIN)
        keys_ref[pl.ds(first, WIN), :] = block[:, :key_width]
        spread_values(block[...], values_ref, first)
    step = LANES
    parts, places = [], []
    for row in range(0, rows, step):
        left = [(k - row, 0) for k in range(-WIN, 0, LANES) if row - k < WIN + LANES]
        right = [(k - row, 1) for k in range(rows, rows + WIN, LANES) if k - row < WIN + step]
        places.append(left + right)
        parts.append((row, step, WIN - len(left) * LANES, len(left + right) * LANES))
    attend(
        q_ref,
        [keys_ref],
        values_ref,
        parts,
        window_mask(extent_ref, places, valid),
        (sums_ref, tops_ref),
        keep_sums(all_sums_ref),
    )
    hidden = (
        dot(divide_pairs(all_sums_ref), out_w_ref[...]) + residual_ref[...].astype(jnp.float32)
    ).astype(jnp.bfloat16)
    hidden_ref[...] = hidden
    values = hidden.astype(jnp.float32)
    scale = lax.rsqrt(jnp.mean(values * values, axis=-1, keepdims=True) + 1e-05)
    normed = (values * scale).astype(jnp.bfloat16)
    normed_ref[...] = normed
    kv_ref[...] = dot(normed, kv_w_ref[...]).astype(jnp.bfloat16)


def all_seen(head, part, tiles):
    return tiles


def own_butterfly_kernel(
    levels,
    mask_ref,
    normed_ref,
    q_w_ref,
    own_ref,
    q_ref,
    sums_ref,
    tops_ref,
    shown_ref,
    values_ref,
):
    rows = normed_ref.shape[0]
    kv_heads = values_ref.shape[0]
    for level in range(levels):
        shown_ref[level] = jnp.full(
            shown_ref.shape[1:], jnp.where(mask_ref[0, level] == 1, 1.0, 0.0), jnp.bfloat16
        )
    spread_queries(
        dot(normed_ref[...], q_w_ref[...]).astype(jnp.bfloat16), kv_heads, q_ref
    )
    spread_values(own_ref[...], values_ref, 0)
    step = min(rows, ROWS)
    attend(
        q_ref,
        [own_ref],
        values_ref,
        [(row, step, 0, rows) for row in range(0, rows, step)],
        all_seen,
        None,
        keep_state(sums_ref, tops_ref),
    )


def more_butterfly_kernel(levels, last, *refs):
    blocks, refs = refs[: len(levels)], refs[len(levels) :]
    (shown_ref, own_ref, q_ref, sums_ref, tops_ref), refs = refs[:5], refs[5:]
    rows = q_ref.shape[1]
    if last:
        hidden_ref, out_w_ref, out_ref, values_ref, keys_ref, all_sums_ref = refs
        sink = keep_sums(all_sums_ref)
    else:
        sums_out_ref, tops_out_ref, values_ref, keys_ref = refs
        sink = keep_state(sums_out_ref, tops_out_ref)
    key_width = own_ref.shape[1] // 2
    for n, (level, block) in enumerate(zip(levels, blocks)):
        spot = pl.ds(n * rows, rows)
        shown = shown_ref[level, :1, :]
        for c in range(0, key_width, LANES):
            keys = block[:, c : c + LANES]
            here = jnp.broadcast_to(shown, keys.shape) > 0
            keys_ref[spot, c : c + LANES] = jnp.where(here, keys, own_ref[:, c : c + LANES])
        spread_values(block[...], values_ref, n * rows, shown)
    step = min(rows, ROWS)
    attend(
        q_ref,
        [keys_ref],
        values_ref,
        [(row, step, 0, rows * len(levels)) for row in range(0, rows, step)],
        all_seen,
        (sums_ref, tops_ref),
        sink,
    )
    if last:
        out_ref[...] = (
            dot(divide_pairs(all_sums_ref), out_w_ref[...]) + hidden_ref[...].astype(jnp.float32)
        ).astype(jnp.bfloat16)


def exchange_edges(block, parity):
    groups, count = lax.axis_size("groups"), lax.axis_size("seq")
    rows = block.shape[0]
    if rows > WIN:
        first = jnp.where(lax.rem(lax.axis_index("seq"), 2) == parity, rows - WIN, 0)
        block = lax.dynamic_slice_in_dim(block, first, WIN, 0)
    route = []
    for group in range(groups):
        for i in range(count):
            other, to = group, i + 1 if i % 2 == parity else i - 1
            if not 0 <= to < count:
                other, to = (group ^ 1 if group ^ 1 < groups else group), i
            route.append((group * count + i, other * count + to))
    return lax.ppermute(block, ("groups", "seq"), route)


def shards(
    residual,
    layer_queries,
    layer_keyvals,
    head_window_extent,
    block_mask,
    first_out,
    second_query,
    second_keyval,
    second_out,
):
    rows, width = residual.shape
    q_width = layer_queries.shape[1]
    kv_width = layer_keyvals.shape[1]
    kv_heads = kv_width // (2 * HEAD_SIZE)
    heads = q_width // HEAD_SIZE
    count = lax.axis_size("seq")
    level_count = count.bit_length() - 1
    bf16, f32 = jnp.bfloat16, jnp.float32
    vmem = pl.BlockSpec(memory_space=pltpu.VMEM)
    smem = pl.BlockSpec(memory_space=pltpu.SMEM)
    state = [jax.ShapeDtypeStruct((heads, rows, LANES), f32)] * 2
    queries = jax.ShapeDtypeStruct((heads, rows, LANES), bf16)
    wide = jax.ShapeDtypeStruct((rows, width), bf16)
    all_sums = pltpu.VMEM((heads, rows, LANES), f32)

    def call(kernel, name, in_specs, out_shape, scratch, key_rows, extra_macs, args):
        macs = 4 * rows * heads * HEAD_SIZE * key_rows + extra_macs
        values = pltpu.VMEM((kv_heads, 2, key_rows, LANES), bf16)
        return pl.pallas_call(
            kernel,
            out_shape=out_shape,
            in_specs=in_specs,
            out_specs=jax.tree.map(lambda _: vmem, out_shape),
            scratch_shapes=[values] + scratch,
            compiler_params=pltpu.CompilerParams(vmem_limit_bytes=VMEM_LIMIT),
            cost_estimate=pl.CostEstimate(
                flops=16 * macs, bytes_accessed=2**21, transcendentals=rows * heads * key_rows
            ),
            name=name,
        )(*args)

    even, odd = (exchange_edges(layer_keyvals, parity) for parity in range(2))
    q_here, sums, tops = call(
        own_window_kernel,
        "own_window",
        [smem, vmem, vmem],
        [queries] + state,
        [],
        rows,
        0,
        (head_window_extent, layer_queries, layer_keyvals),
    )
    hidden, normed, keyvals = call(
        halo_window_kernel,
        "halo_window",
        [smem] + [vmem] * 8,
        [wide, wide, jax.ShapeDtypeStruct((rows, kv_width), bf16)],
        [pltpu.VMEM((2 * WIN, kv_width // 2), bf16), all_sums],
        2 * WIN,
        rows * width * (q_width + kv_width),
        (
            head_window_extent,
            q_here,
            even,
            odd,
            sums,
            tops,
            residual,
            first_out,
            second_keyval,
        ),
    )

    others = [None] * level_count
    for level in reversed(range(level_count)):
        route = [(i, i ^ (1 << level)) for i in range(count)]
        others[level] = lax.ppermute(keyvals, "seq", route)
    queries_two, sums, tops, shown = call(
        functools.partial(own_butterfly_kernel, level_count),
        "own_butterfly",
        [smem] + [vmem] * 3,
        [queries] + state + [jax.ShapeDtypeStruct((level_count, 16, LANES), bf16)],
        [],
        rows,
        rows * width * q_width,
        (block_mask, normed, second_query, keyvals),
    )
    cut = (level_count + 1) // 2
    groups = [list(reversed(range(cut))), list(reversed(range(cut, level_count)))]


    def key_block(levels):
        return pltpu.VMEM((rows * len(levels), kv_width // 2), bf16)

    for levels in groups[:-1]:
        sums, tops = call(
            functools.partial(more_butterfly_kernel, levels, False),
            "near_butterfly",
            [vmem] * (5 + len(levels)),
            state,
            [key_block(levels)],
            rows * len(levels),
            0,
            (*[others[level] for level in levels], shown, keyvals, queries_two, sums, tops),
        )
    levels = groups[-1]
    return call(
        functools.partial(more_butterfly_kernel, levels, True),
        "far_butterfly",
        [vmem] * (7 + len(levels)),
        wide,
        [key_block(levels), all_sums],
        rows * len(levels),
        rows * width * q_width,
        (*[others[level] for level in levels], shown, keyvals, queries_two, sums, tops, hidden, second_out),
    )


def solution(mesh):
    tokens = P(("groups", "seq"), None)
    placed = (tokens, tokens, tokens, P(), P("seq", None), P(), P(), P(), P())
    return jax.shard_map(shards, mesh=mesh, in_specs=placed, out_specs=tokens, check_vma=False)
```

time: 25.2 us -> 24.5 us (0.972)
  Pallas kernels: 12.1 us -> 11.2 us
    pallas_call x5, Pallas kernels: 12.1 us -> 11.2 us  [call(): pl.pallas_call(kernel, out_shape=out_shape, in_specs=in_specs, out_specs=...]
where the time goes in v3:
time: 24.5 us; the launch traced here: 24.4 us
  Pallas kernels  11.2 us (46%)
  starting transfers between devices  8.71 us (36%)
  local copies, waits for them, and re-layouts  2.54 us (10%)
  waiting for transfers between devices  1.77 us (7%)
    pallas_call x5, Pallas kernels, call(): pl.pallas_call(kernel, out_shape=out_shape, in_specs=in_specs, out_specs=...  11.2 us
    ppermute x4, starting transfers between devices, shards(): others[level] = lax.ppermute(keyvals, 'seq', route)  5.6 us
    ppermute x2, starting transfers between devices, exchange_edges(): return lax.ppermute(block, ('groups', 'seq'), route)  3.11 us
    unnamed x18, local copies, waits for them, and re-layouts  2.54 us
    ppermute x4, waiting for transfers between devices, shards(): others[level] = lax.ppermute(keyvals, 'seq', route)  1.77 us
  transfers between devices with their start and end apart: 6, of which 2 were waited for; matrix products, arithmetic and copies ran while one was open for 0% of the time, Pallas kernels for 21%

profile of v3, /device:TPU:0, one launch (start us, length us, event | category | flops | bytes accessed | tf_op | source)
XLA Modules:
  0.0 24.4 jit_solution(14206482863413790110)
XLA Ops:
  0.0 0.5 %collective-permute-start = (bf16[256,256]{1,0:T(8,128)(2,1)}, bf16[256,256]{1,0:T(8,128)(2,1)S(1)}, u32[]{:S(2)}, u32[]{:S(2)}) collective-permute-start(bf16[256,256]{1,0:T(8,128)(2,1)} %own_ref.1), channel_id=1, source_target_pairs={{0,1},{1,0},{2,3},{3,2},{4,5},{5,4},{6,7},{7,6},{8,9},{9,8},{10,11... | collective-permute-start | bytes 393224 | tf_op jit(solution)/shard_map/ppermute | solution.py:329
  0.5 2.6 %collective-permute-start.1 = (bf16[256,256]{1,0:T(8,128)(2,1)}, bf16[256,256]{1,0:T(8,128)(2,1)S(1)}, u32[]{:S(2)}, u32[]{:S(2)}) collective-permute-start(bf16[256,256]{1,0:T(8,128)(2,1)} %own_ref.1), channel_id=1, source_target_pairs={{0,16},{1,2},{2,1},{3,4},{4,3},{5,6},{6,5},{7,8},{8,7},{9,10},{10,... | collective-permute-start | bytes 393224 | tf_op jit(solution)/shard_map/ppermute | solution.py:329
  3.1 0.9 %copy-done.5 = bf16[256,512]{1,0:T(8,128)(2,1)S(1)} copy-done((bf16[256,512]{1,0:T(8,128)(2,1)S(1)}, bf16[256,512]{1,0:T(8,128)(2,1)}, u32[]{:S(2)}) %copy-start.5) | copy-done | bytes 262168
  4.1 0.9 %copy-done.6 = bf16[256,256]{1,0:T(8,128)(2,1)S(1)} copy-done((bf16[256,256]{1,0:T(8,128)(2,1)S(1)}, bf16[256,256]{1,0:T(8,128)(2,1)}, u32[]{:S(2)}) %copy-start.6) | copy-done | bytes 131096
  5.0 0.7 %copy-done.7 = s32[8]{0:T(128)S(1)} copy-done((s32[8]{0:T(128)S(1)}, s32[8]{0:T(128)}, u32[]{:S(2)}) %copy-start.7) | copy-done | bytes 56
  5.6 1.8 %own_window.1 = (bf16[8,256,128]{2,1,0:T(8,128)(2,1)S(1)}, f32[8,256,128]{2,1,0:T(8,128)S(1)}, f32[8,256,128]{2,1,0:T(8,128)S(1)}) custom-call(s32[8]{0:T(128)S(1)} %copy-done.7, bf16[256,512]{1,0:T(8,128)(2,1)S(1)} %copy-done.5, bf16[256,256]{1,0:T(8,128)(2,1)S(1)} %copy-done.6), custom_call_target="tpu_custom_call" | custom-call | flops 2147483648 | bytes 2097152 | tf_op jit(solution)/shard_map/own_window/pallas_call | solution.py:361
  7.4 0.0 collective-permute-done.even_ref
  7.4 0.0 collective-permute-done.1.odd_ref
  7.5 0.0 copy-done
  7.5 0.0 copy-start.1
  7.5 3.2 %halo_window.1 = (bf16[256,1024]{1,0:T(8,128)(2,1)S(1)}, bf16[256,1024]{1,0:T(8,128)(2,1)S(1)}, bf16[256,256]{1,0:T(8,128)(2,1)S(1)}) custom-call(s32[8]{0:T(128)S(1)} %copy-done.7, bf16[8,256,128]{2,1,0:T(8,128)(2,1)S(1)} %get-tuple-element.17.q_ref, bf16[256,256]{1,0:T(8,128)(2,1)S(1)} %collective-permute-done.even_ref, ...), custom_call_target="tpu_custom_call" | custom-call | flops 7516192768 | bytes 2097152 | tf_op jit(solution)/shard_map/halo_window/pallas_call | solution.py:361
  10.7 0.0 copy-start.8
  10.7 0.3 %collective-permute-start.4 = (bf16[256,256]{1,0:T(8,128)(2,1)S(1)}, bf16[256,256]{1,0:T(8,128)(2,1)S(1)}, u32[]{:S(2)}, u32[]{:S(2)}) collective-permute-start(bf16[256,256]{1,0:T(8,128)(2,1)S(1)} %get-tuple-element.20.own_ref.refs_3_), channel_id=1, source_target_pairs={{0,2},{1,3},{2,0},{3,1},{4,6},{5,7},{6,4},{7,5},{8,10},{9,11},{10,... | collective-permute-start | bytes 393224 | tf_op jit(solution)/shard_map/ppermute | solution.py:409
  11.0 1.1 %collective-permute-start.5 = (bf16[256,256]{1,0:T(8,128)(2,1)S(1)}, bf16[256,256]{1,0:T(8,128)(2,1)S(1)}, u32[]{:S(2)}, u32[]{:S(2)}) collective-permute-start(bf16[256,256]{1,0:T(8,128)(2,1)S(1)} %get-tuple-element.20.own_ref.refs_3_), channel_id=1, source_target_pairs={{0,1},{1,0},{2,3},{3,2},{4,5},{5,4},{6,7},{7,6},{8,9},{9,8},{10,11... | collective-permute-start | bytes 393224 | tf_op jit(solution)/shard_map/ppermute | solution.py:409
  12.1 2.6 %collective-permute-start.2 = (bf16[256,256]{1,0:T(8,128)(2,1)S(1)}, bf16[256,256]{1,0:T(8,128)(2,1)S(1)}, u32[]{:S(2)}, u32[]{:S(2)}) collective-permute-start(bf16[256,256]{1,0:T(8,128)(2,1)S(1)} %get-tuple-element.20.own_ref.refs_3_), channel_id=1, source_target_pairs={{0,8},{1,9},{2,10},{3,11},{4,12},{5,13},{6,14},{7,15},{8,0},{9,1},... | collective-permute-start | bytes 393224 | tf_op jit(solution)/shard_map/ppermute | solution.py:409
  14.7 1.6 %collective-permute-start.3 = (bf16[256,256]{1,0:T(8,128)(2,1)S(1)}, bf16[256,256]{1,0:T(8,128)(2,1)S(1)}, u32[]{:S(2)}, u32[]{:S(2)}) collective-permute-start(bf16[256,256]{1,0:T(8,128)(2,1)S(1)} %get-tuple-element.20.own_ref.refs_3_), channel_id=1, source_target_pairs={{0,4},{1,5},{2,6},{3,7},{4,0},{5,1},{6,2},{7,3},{8,12},{9,13},{10,... | collective-permute-start | bytes 393224 | tf_op jit(solution)/shard_map/ppermute | solution.py:409
  16.3 1.8 %own_butterfly.1 = (bf16[8,256,128]{2,1,0:T(8,128)(2,1)S(1)}, f32[8,256,128]{2,1,0:T(8,128)S(1)}, f32[8,256,128]{2,1,0:T(8,128)S(1)}, bf16[4,16,128]{2,1,0:T(8,128)(2,1)S(1)}) custom-call(s32[1,4]{1,0:T(1,128)S(1)} %copy-done.8, bf16[256,1024]{1,0:T(8,128)(2,1)S(1)} %get-tuple-element.21.normed_ref, bf16[1024,512]{1,0:T(8,128)(2,1)S(1)} %copy-done.1, ...), custom_call_target="tpu_custom_call" | custom-call | flops 4294967296 | bytes 2097152 | tf_op jit(solution)/shard_map/own_butterfly/pallas_call | solution.py:361
  18.1 0.0 collective-permute-done.4.refs_0_
  18.1 0.0 collective-permute-done.5.refs_1_
  18.1 0.0 copy-start.2
  18.1 1.6 %near_butterfly.1 = (f32[8,256,128]{2,1,0:T(8,128)S(1)}, f32[8,256,128]{2,1,0:T(8,128)S(1)}) custom-call(bf16[256,256]{1,0:T(8,128)(2,1)S(1)} %collective-permute-done.4.refs_0_, bf16[256,256]{1,0:T(8,128)(2,1)S(1)} %collective-permute-done.5.refs_1_, bf16[4,16,128]{2,1,0:T(8,128)(2,1)S(1)} %get-tuple-element.22.refs_2_, ...), custom_call_target="tpu_custom_call" | custom-call | flops 4294967296 | bytes 2097152 | tf_op jit(solution)/shard_map/near_butterfly/pallas_call | solution.py:361
  19.8 1.6 %collective-permute-done.2.refs_0_ = bf16[256,256]{1,0:T(8,128)(2,1)S(1)} collective-permute-done((bf16[256,256]{1,0:T(8,128)(2,1)S(1)}, bf16[256,256]{1,0:T(8,128)(2,1)S(1)}, u32[]{:S(2)}, u32[]{:S(2)}) %collective-permute-start.2) | collective-permute-done | bytes 131104 | tf_op jit(solution)/shard_map/ppermute | solution.py:409
  21.3 0.2 collective-permute-done.3.refs_1_
  21.5 2.9 %far_butterfly.1 = bf16[256,1024]{1,0:T(8,128)(2,1)} custom-call(bf16[256,256]{1,0:T(8,128)(2,1)S(1)} %collective-permute-done.2.refs_0_, bf16[256,256]{1,0:T(8,128)(2,1)S(1)} %collective-permute-done.3.refs_1_, bf16[4,16,128]{2,1,0:T(8,128)(2,1)S(1)} %get-tuple-element.22.refs_2_, bf16[256,256]{1,0:T(8,128)(2,1)S(1)} %get-tuple-element.20.own_ref.refs_3_, ...), custom_call_target="tpu_custom_call" | custom-call | flops 6442450944 | bytes 2097152 | tf_op jit(solution)/shard_map/far_butterfly/pallas_call | solution.py:361
  (11 shorter events, 0.0 us)
Async XLA Ops:
  0.0 7.5 %copy-start = (bf16[512,1024]{1,0:T(8,128)(2,1)S(1)}, bf16[512,1024]{1,0:T(8,128)(2,1)}, u32[]{:S(2)}) copy-start(bf16[512,1024]{1,0:T(8,128)(2,1)} %out_w_ref.1) | copy-start | bytes 3145732
  0.0 7.5 %copy-start.4 = (bf16[1024,256]{1,0:T(8,128)(2,1)S(1)}, bf16[1024,256]{1,0:T(8,128)(2,1)}, u32[]{:S(2)}) copy-start(bf16[1024,256]{1,0:T(8,128)(2,1)} %kv_w_ref.1) | copy-start | bytes 1572868
  0.0 7.5 %copy-start.3 = (bf16[256,1024]{1,0:T(8,128)(2,1)S(1)}, bf16[256,1024]{1,0:T(8,128)(2,1)}, u32[]{:S(2)}) copy-start(bf16[256,1024]{1,0:T(8,128)(2,1)} %residual_ref.1) | copy-start | bytes 1572868
  0.0 7.4 %collective-permute-start = (bf16[256,256]{1,0:T(8,128)(2,1)}, bf16[256,256]{1,0:T(8,128)(2,1)S(1)}, u32[]{:S(2)}, u32[]{:S(2)}) collective-permute-start(bf16[256,256]{1,0:T(8,128)(2,1)} %own_ref.1), channel_id=1, source_target_pairs={{0,1},{1,0},{2,3},{3,2},{4,5},{5,4},{6,7},{7,6},{8,9},{9,8},{10,11... | collective-permute-start | bytes 393224 | tf_op jit(solution)/shard_map/ppermute | solution.py:329
  0.5 6.9 %collective-permute-start.1 = (bf16[256,256]{1,0:T(8,128)(2,1)}, bf16[256,256]{1,0:T(8,128)(2,1)S(1)}, u32[]{:S(2)}, u32[]{:S(2)}) collective-permute-start(bf16[256,256]{1,0:T(8,128)(2,1)} %own_ref.1), channel_id=1, source_target_pairs={{0,16},{1,2},{2,1},{3,4},{4,3},{5,6},{6,5},{7,8},{8,7},{9,10},{10,... | collective-permute-start | bytes 393224 | tf_op jit(solution)/shard_map/ppermute | solution.py:329
  3.1 0.9 %copy-start.5 = (bf16[256,512]{1,0:T(8,128)(2,1)S(1)}, bf16[256,512]{1,0:T(8,128)(2,1)}, u32[]{:S(2)}) copy-start(bf16[256,512]{1,0:T(8,128)(2,1)} %queries_ref.1) | copy-start | bytes 786436
  4.1 0.9 %copy-start.6 = (bf16[256,256]{1,0:T(8,128)(2,1)S(1)}, bf16[256,256]{1,0:T(8,128)(2,1)}, u32[]{:S(2)}) copy-start(bf16[256,256]{1,0:T(8,128)(2,1)} %own_ref.1) | copy-start | bytes 393220
  5.0 0.7 %copy-start.7 = (s32[8]{0:T(128)S(1)}, s32[8]{0:T(128)}, u32[]{:S(2)}) copy-start(s32[8]{0:T(128)} %extent_ref.3) | copy-start | bytes 100
  7.5 8.8 %copy-start.1 = (bf16[1024,512]{1,0:T(8,128)(2,1)S(1)}, bf16[1024,512]{1,0:T(8,128)(2,1)}, u32[]{:S(2)}) copy-start(bf16[1024,512]{1,0:T(8,128)(2,1)} %q_w_ref.1) | copy-start | bytes 3145732
  10.7 5.6 %copy-start.8 = (s32[1,4]{1,0:T(1,128)S(1)}, s32[1,4]{1,0:T(1,128)}, u32[]{:S(2)}) copy-start(s32[1,4]{1,0:T(1,128)} %mask_ref.1) | copy-start | bytes 52
  10.7 7.4 %collective-permute-start.4 = (bf16[256,256]{1,0:T(8,128)(2,1)S(1)}, bf16[256,256]{1,0:T(8,128)(2,1)S(1)}, u32[]{:S(2)}, u32[]{:S(2)}) collective-permute-start(bf16[256,256]{1,0:T(8,128)(2,1)S(1)} %get-tuple-element.20.own_ref.refs_3_), channel_id=1, source_target_pairs={{0,2},{1,3},{2,0},{3,1},{4,6},{5,7},{6,4},{7,5},{8,10},{9,11},{10,... | collective-permute-start | bytes 393224 | tf_op jit(solution)/shard_map/ppermute | solution.py:409
  11.0 7.2 %collective-permute-start.5 = (bf16[256,256]{1,0:T(8,128)(2,1)S(1)}, bf16[256,256]{1,0:T(8,128)(2,1)S(1)}, u32[]{:S(2)}, u32[]{:S(2)}) collective-permute-start(bf16[256,256]{1,0:T(8,128)(2,1)S(1)} %get-tuple-element.20.own_ref.refs_3_), channel_id=1, source_target_pairs={{0,1},{1,0},{2,3},{3,2},{4,5},{5,4},{6,7},{7,6},{8,9},{9,8},{10,11... | collective-permute-start | bytes 393224 | tf_op jit(solution)/shard_map/ppermute | solution.py:409
  12.1 9.2 %collective-permute-start.2 = (bf16[256,256]{1,0:T(8,128)(2,1)S(1)}, bf16[256,256]{1,0:T(8,128)(2,1)S(1)}, u32[]{:S(2)}, u32[]{:S(2)}) collective-permute-start(bf16[256,256]{1,0:T(8,128)(2,1)S(1)} %get-tuple-element.20.own_ref.refs_3_), channel_id=1, source_target_pairs={{0,8},{1,9},{2,10},{3,11},{4,12},{5,13},{6,14},{7,15},{8,0},{9,1},... | collective-permute-start | bytes 393224 | tf_op jit(solution)/shard_map/ppermute | solution.py:409
  14.7 6.8 %collective-permute-start.3 = (bf16[256,256]{1,0:T(8,128)(2,1)S(1)}, bf16[256,256]{1,0:T(8,128)(2,1)S(1)}, u32[]{:S(2)}, u32[]{:S(2)}) collective-permute-start(bf16[256,256]{1,0:T(8,128)(2,1)S(1)} %get-tuple-element.20.own_ref.refs_3_), channel_id=1, source_target_pairs={{0,4},{1,5},{2,6},{3,7},{4,0},{5,1},{6,2},{7,3},{8,12},{9,13},{10,... | collective-permute-start | bytes 393224 | tf_op jit(solution)/shard_map/ppermute | solution.py:409
  18.1 3.4 %copy-start.2 = (bf16[512,1024]{1,0:T(8,128)(2,1)S(1)}, bf16[512,1024]{1,0:T(8,128)(2,1)}, u32[]{:S(2)}) copy-start(bf16[512,1024]{1,0:T(8,128)(2,1)} %refs_8_.1) | copy-start | bytes 3145732

commit v4 on v3

--- a/solution.py
+++ b/solution.py
@@ -31,6 +31,12 @@
 
 def low_half(rows):
     return lax.broadcasted_iota(jnp.int32, (rows, LANES), 1) < HEAD_SIZE
+
+
+def splat(row, index, shape):
+    lane = lax.broadcasted_iota(jnp.int32, row.shape, 1)
+    one = jnp.sum(jnp.where(lane == index, row.astype(jnp.float32), 0.0), axis=1, keepdims=True)
+    return jnp.broadcast_to(one, shape)
 
 
 def spread_queries(queries, kv_heads, spread_ref):
@@ -143,9 +149,9 @@
     return jnp.concatenate(out, axis=1)
 
 
-def window_mask(extent_ref, places, valid):
+def window_mask(extents_ref, places, valid):
     def mask(head, part, tiles):
-        extent = extent_ref[head]
+        extent = extents_ref[head, :1, :]
         shape = tiles[0].shape
         gap = lax.broadcasted_iota(jnp.int32, shape, 0) - lax.broadcasted_iota(jnp.int32, shape, 1)
         out = []
@@ -164,9 +170,12 @@
 
 
 def own_window_kernel(
-    extent_ref, queries_ref, own_ref, q_ref, sums_ref, tops_ref, values_ref
+    extent_ref, queries_ref, own_ref, extents_ref, q_ref, sums_ref, tops_ref, values_ref
 ):
     rows = own_ref.shape[0]
+    for head in range(extents_ref.shape[0]):
+        one = splat(extent_ref[...], head, extents_ref.shape[1:])
+        extents_ref[head] = one.astype(jnp.int32)
     kv_heads = values_ref.shape[0]
     spread_queries(queries_ref[...], kv_heads, q_ref)
     spread_values(own_ref[...], values_ref, 0)
@@ -181,14 +190,14 @@
         [own_ref],
         values_ref,
         parts,
-        window_mask(extent_ref, places, None),
+        window_mask(extents_ref, places, None),
         None,
         keep_state(sums_ref, tops_ref),
     )
 
 
 def halo_window_kernel(
-    extent_ref,
+    extents_ref,
     q_ref,
     even_ref,
     odd_ref,
@@ -225,7 +234,7 @@
         [keys_ref],
         values_ref,
         parts,
-        window_mask(extent_ref, places, valid),
+        window_mask(extents_ref, places, valid),
         (sums_ref, tops_ref),
         keep_sums(all_sums_ref),
     )
@@ -259,9 +268,8 @@
     rows = normed_ref.shape[0]
     kv_heads = values_ref.shape[0]
     for level in range(levels):
-        shown_ref[level] = jnp.full(
-            shown_ref.shape[1:], jnp.where(mask_ref[0, level] == 1, 1.0, 0.0), jnp.bfloat16
-        )
+        one = splat(mask_ref[...], level, shown_ref.shape[1:])
+        shown_ref[level] = jnp.where(one == 1.0, 1.0, 0.0).astype(jnp.bfloat16)
     spread_queries(
         dot(normed_ref[...], q_w_ref[...]).astype(jnp.bfloat16), kv_heads, q_ref
     )
@@ -349,7 +357,6 @@
     level_count = count.bit_length() - 1
     bf16, f32 = jnp.bfloat16, jnp.float32
     vmem = pl.BlockSpec(memory_space=pltpu.VMEM)
-    smem = pl.BlockSpec(memory_space=pltpu.SMEM)
     state = [jax.ShapeDtypeStruct((heads, rows, LANES), f32)] * 2
     queries = jax.ShapeDtypeStruct((heads, rows, LANES), bf16)
     wide = jax.ShapeDtypeStruct((rows, width), bf16)
@@ -372,26 +379,26 @@
         )(*args)
 
     even, odd = (exchange_edges(layer_keyvals, parity) for parity in range(2))
-    q_here, sums, tops = call(
+    extents, q_here, sums, tops = call(
         own_window_kernel,
         "own_window",
-        [smem, vmem, vmem],
-        [queries] + state,
+        [vmem] * 3,
+        [jax.ShapeDtypeStruct((heads, 8, LANES), jnp.int32), queries] + state,
         [],
         rows,
         0,
-        (head_window_extent, layer_queries, layer_keyvals),
+        (head_window_extent.reshape(1, heads), layer_queries, layer_keyvals),
     )
     hidden, normed, keyvals = call(
         halo_window_kernel,
         "halo_window",
-        [smem] + [vmem] * 8,
+        [vmem] * 9,
         [wide, wide, jax.ShapeDtypeStruct((rows, kv_width), bf16)],
         [pltpu.VMEM((2 * WIN, kv_width // 2), bf16), all_sums],
         2 * WIN,
         rows * width * (q_width + kv_width),
         (
-            head_window_extent,
+            extents,
             q_here,
             even,
             odd,
@@ -410,15 +417,15 @@
     queries_two, sums, tops, shown = call(
         functools.partial(own_butterfly_kernel, level_count),
         "own_butterfly",
-        [smem] + [vmem] * 3,
+        [vmem] * 4,
         [queries] + state + [jax.ShapeDtypeStruct((level_count, 16, LANES), bf16)],
         [],
         rows,
         rows * width * q_width,
         (block_mask, normed, second_query, keyvals),
     )
-    cut = (level_count + 1) // 2
-    groups = [list(reversed(range(cut))), list(reversed(range(cut, level_count)))]
+    far = level_count - 1
+    groups = [list(reversed(range(far))), [far]]
 
 
     def key_block(levels):

time: 24.5 us -> 24.1 us (0.984)
  waiting for transfers between devices: 1.77 us -> 3.5 us
  Pallas kernels: 11.2 us -> 9.79 us
  local copies, waits for them, and re-layouts: 2.54 us -> 1.96 us
    ppermute x4, waiting for transfers between devices: 1.77 us -> 3.49 us  [shards(): others[level] = lax.ppermute(keyvals, 'seq', route)]
    pallas_call x5, Pallas kernels: 11.2 us -> 9.79 us  [call(): pl.pallas_call(kernel, out_shape=out_shape, in_specs=in_specs, out_specs=...]
    unnamed x18, local copies, waits for them, and re-layouts: 2.54 us -> 1.96 us
where the time goes in v4:
time: 24.1 us; the launch traced here: 24 us
  Pallas kernels  9.79 us (41%)
  starting transfers between devices  8.62 us (36%)
  waiting for transfers between devices  3.5 us (15%)
  local copies, waits for them, and re-layouts  1.96 us (8%)
    pallas_call x5, Pallas kernels, call(): pl.pallas_call(kernel, out_shape=out_shape, in_specs=in_specs, out_specs=...  9.79 us
    ppermute x4, starting transfers between devices, shards(): others[level] = lax.ppermute(keyvals, 'seq', route)  5.59 us
    ppermute x4, waiting for transfers between devices, shards(): others[level] = lax.ppermute(keyvals, 'seq', route)  3.49 us
    ppermute x2, starting transfers between devices, exchange_edges(): return lax.ppermute(block, ('groups', 'seq'), route)  3.03 us
    unnamed x18, local copies, waits for them, and re-layouts  1.96 us
  transfers between devices with their start and end apart: 6, of which 2 were waited for; matrix products, arithmetic and copies ran while one was open for 0% of the time, Pallas kernels for 21%

profile of v4, /device:TPU:0, one launch (start us, length us, event | category | flops | bytes accessed | tf_op | source)
XLA Modules:
  0.0 24.0 jit_solution(13949986307756091973)
XLA Ops:
  0.0 0.5 %collective-permute-start = (bf16[256,256]{1,0:T(8,128)(2,1)}, bf16[256,256]{1,0:T(8,128)(2,1)S(1)}, u32[]{:S(2)}, u32[]{:S(2)}) collective-permute-start(bf16[256,256]{1,0:T(8,128)(2,1)} %own_ref.1), channel_id=1, source_target_pairs={{0,1},{1,0},{2,3},{3,2},{4,5},{5,4},{6,7},{7,6},{8,9},{9,8},{10,11... | collective-permute-start | bytes 393224 | tf_op jit(solution)/shard_map/ppermute | solution.py:337
  0.5 2.6 %collective-permute-start.1 = (bf16[256,256]{1,0:T(8,128)(2,1)}, bf16[256,256]{1,0:T(8,128)(2,1)S(1)}, u32[]{:S(2)}, u32[]{:S(2)}) collective-permute-start(bf16[256,256]{1,0:T(8,128)(2,1)} %own_ref.1), channel_id=1, source_target_pairs={{0,16},{1,2},{2,1},{3,4},{4,3},{5,6},{6,5},{7,8},{8,7},{9,10},{10,... | collective-permute-start | bytes 393224 | tf_op jit(solution)/shard_map/ppermute | solution.py:337
  3.0 0.0 copy-done.7
  3.0 0.9 %copy-done.5 = bf16[256,512]{1,0:T(8,128)(2,1)S(1)} copy-done((bf16[256,512]{1,0:T(8,128)(2,1)S(1)}, bf16[256,512]{1,0:T(8,128)(2,1)}, u32[]{:S(2)}) %copy-start.5) | copy-done | bytes 262168
  4.0 0.9 %copy-done.6 = bf16[256,256]{1,0:T(8,128)(2,1)S(1)} copy-done((bf16[256,256]{1,0:T(8,128)(2,1)S(1)}, bf16[256,256]{1,0:T(8,128)(2,1)}, u32[]{:S(2)}) %copy-start.6) | copy-done | bytes 131096
  4.9 1.4 %own_window.1 = (s32[8,8,128]{2,1,0:T(8,128)S(1)}, bf16[8,256,128]{2,1,0:T(8,128)(2,1)S(1)}, f32[8,256,128]{2,1,0:T(8,128)S(1)}, f32[8,256,128]{2,1,0:T(8,128)S(1)}) custom-call(s32[1,8]{1,0:T(1,128)S(1)} %bitcast.1, bf16[256,512]{1,0:T(8,128)(2,1)S(1)} %copy-done.5, bf16[256,256]{1,0:T(8,128)(2,1)S(1)} %copy-done.6), custom_call_target="tpu_custom_call" | custom-call | flops 2147483648 | bytes 2097152 | tf_op jit(solution)/shard_map/own_window/pallas_call | solution.py:368
  6.3 0.0 collective-permute-done.even_ref
  6.3 0.0 collective-permute-done.1.odd_ref
  6.4 0.1 copy-done.4
  6.5 2.6 %halo_window.1 = (bf16[256,1024]{1,0:T(8,128)(2,1)S(1)}, bf16[256,1024]{1,0:T(8,128)(2,1)S(1)}, bf16[256,256]{1,0:T(8,128)(2,1)S(1)}) custom-call(s32[8,8,128]{2,1,0:T(8,128)S(1)} %get-tuple-element.18.extents_ref, bf16[8,256,128]{2,1,0:T(8,128)(2,1)S(1)} %get-tuple-element.19.q_ref, bf16[256,256]{1,0:T(8,128)(2,1)S(1)} %collective-permute-done.even_ref, ...), custom_call_target="tpu_custom_call" | custom-call | flops 7516192768 | bytes 2097152 | tf_op jit(solution)/shard_map/halo_window/pallas_call | solution.py:368
  9.1 0.0 copy-start.8
  9.1 2.3 %collective-permute-start.3 = (bf16[256,256]{1,0:T(8,128)(2,1)S(1)}, bf16[256,256]{1,0:T(8,128)(2,1)S(1)}, u32[]{:S(2)}, u32[]{:S(2)}) collective-permute-start(bf16[256,256]{1,0:T(8,128)(2,1)S(1)} %get-tuple-element.22.own_ref.refs_4_.refs_2_), channel_id=1, source_target_pairs={{0,4},{1,5},{2,6},{3,7},{4,0},{5,1},{6,2},{7,3},{8,12},{9,13},{10,... | collective-permute-start | bytes 393224 | tf_op jit(solution)/shard_map/ppermute | solution.py:416
  11.4 0.7 %collective-permute-start.4 = (bf16[256,256]{1,0:T(8,128)(2,1)S(1)}, bf16[256,256]{1,0:T(8,128)(2,1)S(1)}, u32[]{:S(2)}, u32[]{:S(2)}) collective-permute-start(bf16[256,256]{1,0:T(8,128)(2,1)S(1)} %get-tuple-element.22.own_ref.refs_4_.refs_2_), channel_id=1, source_target_pairs={{0,2},{1,3},{2,0},{3,1},{4,6},{5,7},{6,4},{7,5},{8,10},{9,11},{10,... | collective-permute-start | bytes 393224 | tf_op jit(solution)/shard_map/ppermute | solution.py:416
  12.1 0.6 %collective-permute-start.5 = (bf16[256,256]{1,0:T(8,128)(2,1)S(1)}, bf16[256,256]{1,0:T(8,128)(2,1)S(1)}, u32[]{:S(2)}, u32[]{:S(2)}) collective-permute-start(bf16[256,256]{1,0:T(8,128)(2,1)S(1)} %get-tuple-element.22.own_ref.refs_4_.refs_2_), channel_id=1, source_target_pairs={{0,1},{1,0},{2,3},{3,2},{4,5},{5,4},{6,7},{7,6},{8,9},{9,8},{10,11... | collective-permute-start | bytes 393224 | tf_op jit(solution)/shard_map/ppermute | solution.py:416
  12.7 2.0 %collective-permute-start.2 = (bf16[256,256]{1,0:T(8,128)(2,1)S(1)}, bf16[256,256]{1,0:T(8,128)(2,1)S(1)}, u32[]{:S(2)}, u32[]{:S(2)}) collective-permute-start(bf16[256,256]{1,0:T(8,128)(2,1)S(1)} %get-tuple-element.22.own_ref.refs_4_.refs_2_), channel_id=1, source_target_pairs={{0,8},{1,9},{2,10},{3,11},{4,12},{5,13},{6,14},{7,15},{8,0},{9,1},... | collective-permute-start | bytes 393224 | tf_op jit(solution)/shard_map/ppermute | solution.py:416
  14.7 0.0 copy-done.8
  14.7 1.3 %own_butterfly.1 = (bf16[8,256,128]{2,1,0:T(8,128)(2,1)S(1)}, f32[8,256,128]{2,1,0:T(8,128)S(1)}, f32[8,256,128]{2,1,0:T(8,128)S(1)}, bf16[4,16,128]{2,1,0:T(8,128)(2,1)S(1)}) custom-call(s32[1,4]{1,0:T(1,128)S(1)} %copy-done.8, bf16[256,1024]{1,0:T(8,128)(2,1)S(1)} %get-tuple-element.23.normed_ref, bf16[1024,512]{1,0:T(8,128)(2,1)S(1)} %copy-done.1, ...), custom_call_target="tpu_custom_call" | custom-call | flops 4294967296 | bytes 2097152 | tf_op jit(solution)/shard_map/own_butterfly/pallas_call | solution.py:368
  16.0 0.0 collective-permute-done.3.refs_0_
  16.0 1.4 %collective-permute-done.4.refs_1_ = bf16[256,256]{1,0:T(8,128)(2,1)S(1)} collective-permute-done((bf16[256,256]{1,0:T(8,128)(2,1)S(1)}, bf16[256,256]{1,0:T(8,128)(2,1)S(1)}, u32[]{:S(2)}, u32[]{:S(2)}) %collective-permute-start.4) | collective-permute-done | bytes 131104 | tf_op jit(solution)/shard_map/ppermute | solution.py:416
  17.4 0.0 collective-permute-done.5.refs_2_
  17.4 2.3 %near_butterfly.1 = (f32[8,256,128]{2,1,0:T(8,128)S(1)}, f32[8,256,128]{2,1,0:T(8,128)S(1)}) custom-call(bf16[256,256]{1,0:T(8,128)(2,1)S(1)} %collective-permute-done.3.refs_0_, bf16[256,256]{1,0:T(8,128)(2,1)S(1)} %collective-permute-done.4.refs_1_, bf16[256,256]{1,0:T(8,128)(2,1)S(1)} %collective-permute-done.5.refs_2_, ...), custom_call_target="tpu_custom_call" | custom-call | flops 6442450944 | bytes 2097152 | tf_op jit(solution)/shard_map/near_butterfly/pallas_call | solution.py:368
  19.7 2.1 %collective-permute-done.2.refs_0_ = bf16[256,256]{1,0:T(8,128)(2,1)S(1)} collective-permute-done((bf16[256,256]{1,0:T(8,128)(2,1)S(1)}, bf16[256,256]{1,0:T(8,128)(2,1)S(1)}, u32[]{:S(2)}, u32[]{:S(2)}) %collective-permute-start.2) | collective-permute-done | bytes 131104 | tf_op jit(solution)/shard_map/ppermute | solution.py:416
  21.8 0.0 copy-done.2
  21.8 2.2 %far_butterfly.1 = bf16[256,1024]{1,0:T(8,128)(2,1)} custom-call(bf16[256,256]{1,0:T(8,128)(2,1)S(1)} %collective-permute-done.2.refs_0_, bf16[4,16,128]{2,1,0:T(8,128)(2,1)S(1)} %get-tuple-element.24.refs_3_.refs_1_, bf16[256,256]{1,0:T(8,128)(2,1)S(1)} %get-tuple-element.22.own_ref.refs_4_.refs_2_, ...), custom_call_target="tpu_custom_call" | custom-call | flops 4294967296 | bytes 2097152 | tf_op jit(solution)/shard_map/far_butterfly/pallas_call | solution.py:368
  (11 shorter events, 0.0 us)
Async XLA Ops:
  0.0 3.0 %copy-start.7 = (s32[8]{0:T(128)S(1)}, s32[8]{0:T(128)}, u32[]{:S(2)}) copy-start(s32[8]{0:T(128)} %param.12) | copy-start | bytes 100
  0.0 6.3 %collective-permute-start = (bf16[256,256]{1,0:T(8,128)(2,1)}, bf16[256,256]{1,0:T(8,128)(2,1)S(1)}, u32[]{:S(2)}, u32[]{:S(2)}) collective-permute-start(bf16[256,256]{1,0:T(8,128)(2,1)} %own_ref.1), channel_id=1, source_target_pairs={{0,1},{1,0},{2,3},{3,2},{4,5},{5,4},{6,7},{7,6},{8,9},{9,8},{10,11... | collective-permute-start | bytes 393224 | tf_op jit(solution)/shard_map/ppermute | solution.py:337
  0.5 5.9 %collective-permute-start.1 = (bf16[256,256]{1,0:T(8,128)(2,1)}, bf16[256,256]{1,0:T(8,128)(2,1)S(1)}, u32[]{:S(2)}, u32[]{:S(2)}) collective-permute-start(bf16[256,256]{1,0:T(8,128)(2,1)} %own_ref.1), channel_id=1, source_target_pairs={{0,16},{1,2},{2,1},{3,4},{4,3},{5,6},{6,5},{7,8},{8,7},{9,10},{10,... | collective-permute-start | bytes 393224 | tf_op jit(solution)/shard_map/ppermute | solution.py:337
  3.0 1.0 %copy-start.5 = (bf16[256,512]{1,0:T(8,128)(2,1)S(1)}, bf16[256,512]{1,0:T(8,128)(2,1)}, u32[]{:S(2)}) copy-start(bf16[256,512]{1,0:T(8,128)(2,1)} %queries_ref.1) | copy-start | bytes 786436
  4.0 0.9 %copy-start.6 = (bf16[256,256]{1,0:T(8,128)(2,1)S(1)}, bf16[256,256]{1,0:T(8,128)(2,1)}, u32[]{:S(2)}) copy-start(bf16[256,256]{1,0:T(8,128)(2,1)} %own_ref.1) | copy-start | bytes 393220
  4.9 1.5 %copy-start = (bf16[512,1024]{1,0:T(8,128)(2,1)S(1)}, bf16[512,1024]{1,0:T(8,128)(2,1)}, u32[]{:S(2)}) copy-start(bf16[512,1024]{1,0:T(8,128)(2,1)} %out_w_ref.1) | copy-start | bytes 3145732
  4.9 1.5 %copy-start.3 = (bf16[256,1024]{1,0:T(8,128)(2,1)S(1)}, bf16[256,1024]{1,0:T(8,128)(2,1)}, u32[]{:S(2)}) copy-start(bf16[256,1024]{1,0:T(8,128)(2,1)} %residual_ref.1) | copy-start | bytes 1572868
  4.9 1.6 %copy-start.4 = (bf16[1024,256]{1,0:T(8,128)(2,1)S(1)}, bf16[1024,256]{1,0:T(8,128)(2,1)}, u32[]{:S(2)}) copy-start(bf16[1024,256]{1,0:T(8,128)(2,1)} %kv_w_ref.1) | copy-start | bytes 1572868
  6.5 8.2 %copy-start.1 = (bf16[1024,512]{1,0:T(8,128)(2,1)S(1)}, bf16[1024,512]{1,0:T(8,128)(2,1)}, u32[]{:S(2)}) copy-start(bf16[1024,512]{1,0:T(8,128)(2,1)} %q_w_ref.1) | copy-start | bytes 3145732
  9.1 5.6 %copy-start.8 = (s32[1,4]{1,0:T(1,128)S(1)}, s32[1,4]{1,0:T(1,128)}, u32[]{:S(2)}) copy-start(s32[1,4]{1,0:T(1,128)} %mask_ref.1) | copy-start | bytes 52
  9.1 6.9 %collective-permute-start.3 = (bf16[256,256]{1,0:T(8,128)(2,1)S(1)}, bf16[256,256]{1,0:T(8,128)(2,1)S(1)}, u32[]{:S(2)}, u32[]{:S(2)}) collective-permute-start(bf16[256,256]{1,0:T(8,128)(2,1)S(1)} %get-tuple-element.22.own_ref.refs_4_.refs_2_), channel_id=1, source_target_pairs={{0,4},{1,5},{2,6},{3,7},{4,0},{5,1},{6,2},{7,3},{8,12},{9,13},{10,... | collective-permute-start | bytes 393224 | tf_op jit(solution)/shard_map/ppermute | solution.py:416
  11.4 6.0 %collective-permute-start.4 = (bf16[256,256]{1,0:T(8,128)(2,1)S(1)}, bf16[256,256]{1,0:T(8,128)(2,1)S(1)}, u32[]{:S(2)}, u32[]{:S(2)}) collective-permute-start(bf16[256,256]{1,0:T(8,128)(2,1)S(1)} %get-tuple-element.22.own_ref.refs_4_.refs_2_), channel_id=1, source_target_pairs={{0,2},{1,3},{2,0},{3,1},{4,6},{5,7},{6,4},{7,5},{8,10},{9,11},{10,... | collective-permute-start | bytes 393224 | tf_op jit(solution)/shard_map/ppermute | solution.py:416
  12.1 5.3 %collective-permute-start.5 = (bf16[256,256]{1,0:T(8,128)(2,1)S(1)}, bf16[256,256]{1,0:T(8,128)(2,1)S(1)}, u32[]{:S(2)}, u32[]{:S(2)}) collective-permute-start(bf16[256,256]{1,0:T(8,128)(2,1)S(1)} %get-tuple-element.22.own_ref.refs_4_.refs_2_), channel_id=1, source_target_pairs={{0,1},{1,0},{2,3},{3,2},{4,5},{5,4},{6,7},{7,6},{8,9},{9,8},{10,11... | collective-permute-start | bytes 393224 | tf_op jit(solution)/shard_map/ppermute | solution.py:416
  12.7 9.1 %collective-permute-start.2 = (bf16[256,256]{1,0:T(8,128)(2,1)S(1)}, bf16[256,256]{1,0:T(8,128)(2,1)S(1)}, u32[]{:S(2)}, u32[]{:S(2)}) collective-permute-start(bf16[256,256]{1,0:T(8,128)(2,1)S(1)} %get-tuple-element.22.own_ref.refs_4_.refs_2_), channel_id=1, source_target_pairs={{0,8},{1,9},{2,10},{3,11},{4,12},{5,13},{6,14},{7,15},{8,0},{9,1},... | collective-permute-start | bytes 393224 | tf_op jit(solution)/shard_map/ppermute | solution.py:416
  17.4 4.4 %copy-start.2 = (bf16[512,1024]{1,0:T(8,128)(2,1)S(1)}, bf16[512,1024]{1,0:T(8,128)(2,1)}, u32[]{:S(2)}) copy-start(bf16[512,1024]{1,0:T(8,128)(2,1)} %refs_7_.1) | copy-start | bytes 3145732

commit v5 on v4

--- a/solution.py
+++ b/solution.py
@@ -155,8 +155,8 @@
         shape = tiles[0].shape
         gap = lax.broadcasted_iota(jnp.int32, shape, 0) - lax.broadcasted_iota(jnp.int32, shape, 1)
         out = []
-        for tile, (ahead, side) in zip(tiles, places[part]):
-            reach = extent if side is None else jnp.where(valid[side], extent, -1)
+        for tile, (ahead, outer) in zip(tiles, places[part]):
+            reach = jnp.where(valid, extent, -1) if outer else extent
             if ahead <= -shape[1]:
                 seen = gap <= reach + ahead
             elif ahead >= shape[0]:
@@ -169,37 +169,55 @@
     return mask
 
 
+def window_parts(rows, begin, end):
+    parts, places = [], []
+    for row in range(0, rows, LANES):
+        near = [k for k in range(begin, end, LANES) if -WIN - LANES < k - row < WIN + LANES]
+        near = near or [begin]
+        parts.append((row, LANES, near[0] - begin, len(near) * LANES))
+        places.append([(k - row, not 0 <= k < rows) for k in near])
+    return parts, places
+
+
+def on_side(parity, run):
+    me, last = lax.axis_index("seq"), lax.axis_size("seq") - 1
+    is_right = lax.rem(me, 2) == parity
+    pl.when(is_right)(lambda: run(True, me < last))
+    pl.when(jnp.logical_not(is_right))(lambda: run(False, me > 0))
+
+
 def own_window_kernel(
-    extent_ref, queries_ref, own_ref, extents_ref, q_ref, sums_ref, tops_ref, values_ref
+    extent_ref, queries_ref, own_ref, even_ref, extents_ref, q_ref, sums_ref, tops_ref, values_ref
 ):
     rows = own_ref.shape[0]
     for head in range(extents_ref.shape[0]):
         one = splat(extent_ref[...], head, extents_ref.shape[1:])
         extents_ref[head] = one.astype(jnp.int32)
-    kv_heads = values_ref.shape[0]
-    spread_queries(queries_ref[...], kv_heads, q_ref)
-    spread_values(own_ref[...], values_ref, 0)
-    step = min(rows, ROWS)
-    parts, places = [], []
-    for row in range(0, rows, step):
-        near = [k for k in range(0, rows, LANES) if row - k < WIN + LANES and k - row < WIN + step]
-        parts.append((row, step, near[0], len(near) * LANES))
-        places.append([(k - row, None) for k in near])
-    attend(
-        q_ref,
-        [own_ref],
-        values_ref,
-        parts,
-        window_mask(extents_ref, places, None),
-        None,
-        keep_state(sums_ref, tops_ref),
-    )
+    spread_queries(queries_ref[...], values_ref.shape[0], q_ref)
+
+    def run(right, valid):
+        begin, refs = (0, [own_ref, even_ref]) if right else (-WIN, [even_ref, own_ref])
+        at = 0
+        for ref in refs:
+            spread_values(ref[...], values_ref, at)
+            at += ref.shape[0]
+        parts, places = window_parts(rows, begin, begin + at)
+        attend(
+            q_ref,
+            refs,
+            values_ref,
+            parts,
+            window_mask(extents_ref, places, valid),
+            None,
+            keep_state(sums_ref, tops_ref),
+        )
+
+    on_side(0, run)
 
 
 def halo_window_kernel(
     extents_ref,
     q_ref,
-    even_ref,
     odd_ref,
     sums_ref,
     tops_ref,
@@ -210,34 +228,25 @@
     normed_ref,
     kv_ref,
     values_ref,
-    keys_ref,
     all_sums_ref,
 ):
     rows = q_ref.shape[1]
-    key_width = even_ref.shape[1] // 2
-    me = lax.axis_index("seq")
-    valid = (me > 0, me < lax.axis_size("seq") - 1)
-    left_is_even = lax.rem(me, 2)
-    for block, after in ((even_ref, 1 - left_is_even), (odd_ref, left_is_even)):
-        first = pl.multiple_of(after * WIN, WIN)
-        keys_ref[pl.ds(first, WIN), :] = block[:, :key_width]
-        spread_values(block[...], values_ref, first)
-    step = LANES
-    parts, places = [], []
-    for row in range(0, rows, step):
-        left = [(k - row, 0) for k in range(-WIN, 0, LANES) if row - k < WIN + LANES]
-        right = [(k - row, 1) for k in range(rows, rows + WIN, LANES) if k - row < WIN + step]
-        places.append(left + right)
-        parts.append((row, step, WIN - len(left) * LANES, len(left + right) * LANES))
-    attend(
-        q_ref,
-        [keys_ref],
-        values_ref,
-        parts,
-        window_mask(extents_ref, places, valid),
-        (sums_ref, tops_ref),
-        keep_sums(all_sums_ref),
-    )
+    spread_values(odd_ref[...], values_ref, 0)
+
+    def run(right, valid):
+        begin = rows if right else -WIN
+        parts, places = window_parts(rows, begin, begin + WIN)
+        attend(
+            q_ref,
+            [odd_ref],
+            values_ref,
+            parts,
+            window_mask(extents_ref, places, valid),
+            (sums_ref, tops_ref),
+            keep_sums(all_sums_ref),
+        )
+
+    on_side(1, run)
     hidden = (
         dot(divide_pairs(all_sums_ref), out_w_ref[...]) + residual_ref[...].astype(jnp.float32)
     ).astype(jnp.bfloat16)
@@ -253,33 +262,39 @@
     return tiles
 
 
-def own_butterfly_kernel(
-    levels,
-    mask_ref,
-    normed_ref,
-    q_w_ref,
-    own_ref,
-    q_ref,
-    sums_ref,
-    tops_ref,
-    shown_ref,
-    values_ref,
-):
+def place_blocks(levels, blocks, own_ref, shown_ref, keys_ref, values_ref, first):
+    rows = own_ref.shape[0]
+    for n, (level, block) in enumerate(zip(levels, blocks)):
+        shown = shown_ref[level, :1, :]
+        for c in range(0, own_ref.shape[1] // 2, LANES):
+            keys = block[:, c : c + LANES]
+            here = jnp.broadcast_to(shown, keys.shape) > 0
+            keys_ref[pl.ds(n * rows, rows), c : c + LANES] = jnp.where(
+                here, keys, own_ref[:, c : c + LANES]
+            )
+        spread_values(block[...], values_ref, first + n * rows, shown)
+
+
+def own_butterfly_kernel(levels, *refs):
+    blocks, refs = refs[: len(levels)], refs[len(levels) :]
+    (mask_ref, normed_ref, q_w_ref, own_ref), refs = refs[:4], refs[4:]
+    q_ref, sums_ref, tops_ref, shown_ref, values_ref, keys_ref = refs
     rows = normed_ref.shape[0]
     kv_heads = values_ref.shape[0]
-    for level in range(levels):
+    for level in range(shown_ref.shape[0]):
         one = splat(mask_ref[...], level, shown_ref.shape[1:])
         shown_ref[level] = jnp.where(one == 1.0, 1.0, 0.0).astype(jnp.bfloat16)
     spread_queries(
         dot(normed_ref[...], q_w_ref[...]).astype(jnp.bfloat16), kv_heads, q_ref
     )
     spread_values(own_ref[...], values_ref, 0)
+    place_blocks(levels, blocks, own_ref, shown_ref, keys_ref, values_ref, rows)
     step = min(rows, ROWS)
     attend(
         q_ref,
-        [own_ref],
+        [own_ref, keys_ref],
         values_ref,
-        [(row, step, 0, rows) for row in range(0, rows, step)],
+        [(row, step, 0, rows * (1 + len(levels))) for row in range(0, rows, step)],
         all_seen,
         None,
         keep_state(sums_ref, tops_ref),
@@ -296,15 +311,7 @@
     else:
         sums_out_ref, tops_out_ref, values_ref, keys_ref = refs
         sink = keep_state(sums_out_ref, tops_out_ref)
-    key_width = own_ref.shape[1] // 2
-    for n, (level, block) in enumerate(zip(levels, blocks)):
-        spot = pl.ds(n * rows, rows)
-        shown = shown_ref[level, :1, :]
-        for c in range(0, key_width, LANES):
-            keys = block[:, c : c + LANES]
-            here = jnp.broadcast_to(shown, keys.shape) > 0
-            keys_ref[spot, c : c + LANES] = jnp.where(here, keys, own_ref[:, c : c + LANES])
-        spread_values(block[...], values_ref, n * rows, shown)
+    place_blocks(levels, blocks, own_ref, shown_ref, keys_ref, values_ref, 0)
     step = min(rows, ROWS)
     attend(
         q_ref,
@@ -382,25 +389,24 @@
     extents, q_here, sums, tops = call(
         own_window_kernel,
         "own_window",
-        [vmem] * 3,
+        [vmem] * 4,
         [jax.ShapeDtypeStruct((heads, 8, LANES), jnp.int32), queries] + state,
         [],
-        rows,
+        rows + WIN,
         0,
-        (head_window_extent.reshape(1, heads), layer_queries, layer_keyvals),
+        (head_window_extent.reshape(1, heads), layer_queries, layer_keyvals, even),
     )
     hidden, normed, keyvals = call(
         halo_window_kernel,
         "halo_window",
-        [vmem] * 9,
+        [vmem] * 8,
         [wide, wide, jax.ShapeDtypeStruct((rows, kv_width), bf16)],
-        [pltpu.VMEM((2 * WIN, kv_width // 2), bf16), all_sums],
-        2 * WIN,
+        [all_sums],
+        WIN,
         rows * width * (q_width + kv_width),
         (
             extents,
             q_here,
-            even,
             odd,
             sums,
             tops,
@@ -414,23 +420,22 @@
     for level in reversed(range(level_count)):
         route = [(i, i ^ (1 << level)) for i in range(count)]
         others[level] = lax.ppermute(keyvals, "seq", route)
+    groups = [[0], [], list(reversed(range(1, level_count)))]
+    first, groups = groups[0], [levels for levels in groups[1:] if levels]
+
+    def key_block(levels):
+        return pltpu.VMEM((rows * max(len(levels), 1), kv_width // 2), bf16)
+
     queries_two, sums, tops, shown = call(
-        functools.partial(own_butterfly_kernel, level_count),
+        functools.partial(own_butterfly_kernel, first),
         "own_butterfly",
-        [vmem] * 4,
+        [vmem] * (4 + len(first)),
         [queries] + state + [jax.ShapeDtypeStruct((level_count, 16, LANES), bf16)],
-        [],
-        rows,
+        [key_block(first)],
+        rows * (1 + len(first)),
         rows * width * q_width,
-        (block_mask, normed, second_query, keyvals),
-    )
-    far = level_count - 1
-    groups = [list(reversed(range(far))), [far]]
-
-
-    def key_block(levels):
-        return pltpu.VMEM((rows * len(levels), kv_width // 2), bf16)
-
+        (*[others[level] for level in first], block_mask, normed, second_query, keyvals),
+    )
     for levels in groups[:-1]:
         sums, tops = call(
             functools.partial(more_butterfly_kernel, levels, False),

time: 24.1 us -> 23.5 us (0.975)
  waiting for transfers between devices: 3.5 us -> 2.8 us
  starting transfers between devices: 8.62 us -> 9.04 us
  Pallas kernels: 9.79 us -> 9.47 us
    ppermute x4, waiting for transfers between devices: 3.49 us -> 2.79 us  [shards(): others[level] = lax.ppermute(keyvals, 'seq', route)]
    ppermute x4, starting transfers between devices: 5.59 us -> 6.01 us  [shards(): others[level] = lax.ppermute(keyvals, 'seq', route)]
    pallas_call x5 -> x4, Pallas kernels: 9.79 us -> 9.47 us  [call(): pl.pallas_call(kernel, out_shape=out_shape, in_specs=in_specs, out_specs=...]
  transfers between devices with their start and end apart: 6 -> 6, of which waited for: 2 -> 2; matrix products, arithmetic and copies ran while one was open for 0% -> 0% of each run, Pallas kernels for 21% -> 16%
where the time goes in v5:
time: 23.5 us; the launch traced here: 23.3 us
  Pallas kernels  9.47 us (40%)
  starting transfers between devices  9.04 us (38%)
  waiting for transfers between devices  2.8 us (12%)
  local copies, waits for them, and re-layouts  1.89 us (8%)
    pallas_call x4, Pallas kernels, call(): pl.pallas_call(kernel, out_shape=out_shape, in_specs=in_specs, out_specs=...  9.47 us
    ppermute x4, starting transfers between devices, shards(): others[level] = lax.ppermute(keyvals, 'seq', route)  6.01 us
    ppermute x2, starting transfers between devices, exchange_edges(): return lax.ppermute(block, ('groups', 'seq'), route)  3.03 us
    ppermute x4, waiting for transfers between devices, shards(): others[level] = lax.ppermute(keyvals, 'seq', route)  2.79 us
    unnamed x18, local copies, waits for them, and re-layouts  1.89 us
  transfers between devices with their start and end apart: 6, of which 2 were waited for; matrix products, arithmetic and copies ran while one was open for 0% of the time, Pallas kernels for 16%

profile of v5, /device:TPU:0, one launch (start us, length us, event | category | flops | bytes accessed | tf_op | source)
XLA Modules:
  0.0 23.3 jit_solution(300645743208400104)
XLA Ops:
  0.0 0.5 %collective-permute-start = (bf16[256,256]{1,0:T(8,128)(2,1)}, bf16[256,256]{1,0:T(8,128)(2,1)S(1)}, u32[]{:S(2)}, u32[]{:S(2)}) collective-permute-start(bf16[256,256]{1,0:T(8,128)(2,1)} %own_ref.1), channel_id=1, source_target_pairs={{0,1},{1,0},{2,3},{3,2},{4,5},{5,4},{6,7},{7,6},{8,9},{9,8},{10,11... | collective-permute-start | bytes 393224 | tf_op jit(solution)/shard_map/ppermute | solution.py:344
  0.5 2.6 %collective-permute-start.1 = (bf16[256,256]{1,0:T(8,128)(2,1)}, bf16[256,256]{1,0:T(8,128)(2,1)S(1)}, u32[]{:S(2)}, u32[]{:S(2)}) collective-permute-start(bf16[256,256]{1,0:T(8,128)(2,1)} %own_ref.1), channel_id=1, source_target_pairs={{0,16},{1,2},{2,1},{3,4},{4,3},{5,6},{6,5},{7,8},{8,7},{9,10},{10,... | collective-permute-start | bytes 393224 | tf_op jit(solution)/shard_map/ppermute | solution.py:344
  3.0 0.0 collective-permute-done.even_ref
  3.0 0.0 copy-done.7
  3.0 0.9 %copy-done.5 = bf16[256,512]{1,0:T(8,128)(2,1)S(1)} copy-done((bf16[256,512]{1,0:T(8,128)(2,1)S(1)}, bf16[256,512]{1,0:T(8,128)(2,1)}, u32[]{:S(2)}) %copy-start.5) | copy-done | bytes 262168
  4.0 0.9 %copy-done.6 = bf16[256,256]{1,0:T(8,128)(2,1)S(1)} copy-done((bf16[256,256]{1,0:T(8,128)(2,1)S(1)}, bf16[256,256]{1,0:T(8,128)(2,1)}, u32[]{:S(2)}) %copy-start.6) | copy-done | bytes 131096
  4.9 1.8 %own_window.1 = (s32[8,8,128]{2,1,0:T(8,128)S(1)}, bf16[8,256,128]{2,1,0:T(8,128)(2,1)S(1)}, f32[8,256,128]{2,1,0:T(8,128)S(1)}, f32[8,256,128]{2,1,0:T(8,128)S(1)}) custom-call(s32[1,8]{1,0:T(1,128)S(1)} %bitcast.1, bf16[256,512]{1,0:T(8,128)(2,1)S(1)} %copy-done.5, bf16[256,256]{1,0:T(8,128)(2,1)S(1)} %copy-done.6, ...), custom_call_target="tpu_custom_call" | custom-call | flops 4294967296 | bytes 2097152 | tf_op jit(solution)/shard_map/own_window/pallas_call | solution.py:375
  6.7 0.0 collective-permute-done.1.odd_ref
  6.8 0.0 copy-done
  6.8 0.0 copy-done.3
  6.8 0.0 copy-start.1
  6.8 2.2 %halo_window.1 = (bf16[256,1024]{1,0:T(8,128)(2,1)S(1)}, bf16[256,1024]{1,0:T(8,128)(2,1)S(1)}, bf16[256,256]{1,0:T(8,128)(2,1)S(1)}) custom-call(s32[8,8,128]{2,1,0:T(8,128)S(1)} %get-tuple-element.16.extents_ref, bf16[8,256,128]{2,1,0:T(8,128)(2,1)S(1)} %get-tuple-element.17.q_ref, bf16[256,256]{1,0:T(8,128)(2,1)S(1)} %collective-permute-done.1.odd_ref, ...), custom_call_target="tpu_custom_call" | custom-call | flops 5368709120 | bytes 2097152 | tf_op jit(solution)/shard_map/halo_window/pallas_call | solution.py:375
  9.0 0.0 copy-start.8
  9.0 0.3 %collective-permute-start.5 = (bf16[256,256]{1,0:T(8,128)(2,1)S(1)}, bf16[256,256]{1,0:T(8,128)(2,1)S(1)}, u32[]{:S(2)}, u32[]{:S(2)}) collective-permute-start(bf16[256,256]{1,0:T(8,128)(2,1)S(1)} %get-tuple-element.20.refs_4_), channel_id=1, source_target_pairs={{0,1},{1,0},{2,3},{3,2},{4,5},{5,4},{6,7},{7,6},{8,9},{9,8},{10,11... | collective-permute-start | bytes 393224 | tf_op jit(solution)/shard_map/ppermute | solution.py:422
  9.3 3.7 %collective-permute-start.2 = (bf16[256,256]{1,0:T(8,128)(2,1)S(1)}, bf16[256,256]{1,0:T(8,128)(2,1)S(1)}, u32[]{:S(2)}, u32[]{:S(2)}) collective-permute-start(bf16[256,256]{1,0:T(8,128)(2,1)S(1)} %get-tuple-element.20.refs_4_), channel_id=1, source_target_pairs={{0,8},{1,9},{2,10},{3,11},{4,12},{5,13},{6,14},{7,15},{8,0},{9,1},... | collective-permute-start | bytes 393224 | tf_op jit(solution)/shard_map/ppermute | solution.py:422
  13.0 1.6 %collective-permute-start.3 = (bf16[256,256]{1,0:T(8,128)(2,1)S(1)}, bf16[256,256]{1,0:T(8,128)(2,1)S(1)}, u32[]{:S(2)}, u32[]{:S(2)}) collective-permute-start(bf16[256,256]{1,0:T(8,128)(2,1)S(1)} %get-tuple-element.20.refs_4_), channel_id=1, source_target_pairs={{0,4},{1,5},{2,6},{3,7},{4,0},{5,1},{6,2},{7,3},{8,12},{9,13},{10,... | collective-permute-start | bytes 393224 | tf_op jit(solution)/shard_map/ppermute | solution.py:422
  14.5 0.5 %collective-permute-start.4 = (bf16[256,256]{1,0:T(8,128)(2,1)S(1)}, bf16[256,256]{1,0:T(8,128)(2,1)S(1)}, u32[]{:S(2)}, u32[]{:S(2)}) collective-permute-start(bf16[256,256]{1,0:T(8,128)(2,1)S(1)} %get-tuple-element.20.refs_4_), channel_id=1, source_target_pairs={{0,2},{1,3},{2,0},{3,1},{4,6},{5,7},{6,4},{7,5},{8,10},{9,11},{10,... | collective-permute-start | bytes 393224 | tf_op jit(solution)/shard_map/ppermute | solution.py:422
  15.0 0.0 collective-permute-done.5.refs_0_
  15.0 0.0 copy-start.2
  15.1 1.9 %own_butterfly.1 = (bf16[8,256,128]{2,1,0:T(8,128)(2,1)S(1)}, f32[8,256,128]{2,1,0:T(8,128)S(1)}, f32[8,256,128]{2,1,0:T(8,128)S(1)}, bf16[4,16,128]{2,1,0:T(8,128)(2,1)S(1)}) custom-call(bf16[256,256]{1,0:T(8,128)(2,1)S(1)} %collective-permute-done.5.refs_0_, s32[1,4]{1,0:T(1,128)S(1)} %copy-done.8, bf16[256,1024]{1,0:T(8,128)(2,1)S(1)} %get-tuple-element.21.refs_2_, ...), custom_call_target="tpu_custom_call" | custom-call | flops 6442450944 | bytes 2097152 | tf_op jit(solution)/shard_map/own_butterfly/pallas_call | solution.py:375
  17.0 2.6 %collective-permute-done.2.refs_0_ = bf16[256,256]{1,0:T(8,128)(2,1)S(1)} collective-permute-done((bf16[256,256]{1,0:T(8,128)(2,1)S(1)}, bf16[256,256]{1,0:T(8,128)(2,1)S(1)}, u32[]{:S(2)}, u32[]{:S(2)}) %collective-permute-start.2) | collective-permute-done | bytes 131104 | tf_op jit(solution)/shard_map/ppermute | solution.py:422
  19.6 0.2 collective-permute-done.3.refs_1_
  19.8 0.0 collective-permute-done.4.refs_2_
  19.8 3.5 %far_butterfly.1 = bf16[256,1024]{1,0:T(8,128)(2,1)} custom-call(bf16[256,256]{1,0:T(8,128)(2,1)S(1)} %collective-permute-done.2.refs_0_, bf16[256,256]{1,0:T(8,128)(2,1)S(1)} %collective-permute-done.3.refs_1_, bf16[256,256]{1,0:T(8,128)(2,1)S(1)} %collective-permute-done.4.refs_2_, bf16[4,16,128]{2,1,0:T(8,128)(2,1)S(1)} %get-tuple-element.22.refs_3_, ...), custom_call_target="tpu_custom_call" | custom-call | flops 8589934592 | bytes 2097152 | tf_op jit(solution)/shard_map/far_butterfly/pallas_call | solution.py:375
  (10 shorter events, 0.0 us)
Async XLA Ops:
  0.0 3.0 %copy-start.7 = (s32[8]{0:T(128)S(1)}, s32[8]{0:T(128)}, u32[]{:S(2)}) copy-start(s32[8]{0:T(128)} %param.12) | copy-start | bytes 100
  0.0 3.0 %collective-permute-start = (bf16[256,256]{1,0:T(8,128)(2,1)}, bf16[256,256]{1,0:T(8,128)(2,1)S(1)}, u32[]{:S(2)}, u32[]{:S(2)}) collective-permute-start(bf16[256,256]{1,0:T(8,128)(2,1)} %own_ref.1), channel_id=1, source_target_pairs={{0,1},{1,0},{2,3},{3,2},{4,5},{5,4},{6,7},{7,6},{8,9},{9,8},{10,11... | collective-permute-start | bytes 393224 | tf_op jit(solution)/shard_map/ppermute | solution.py:344
  0.5 6.3 %collective-permute-start.1 = (bf16[256,256]{1,0:T(8,128)(2,1)}, bf16[256,256]{1,0:T(8,128)(2,1)S(1)}, u32[]{:S(2)}, u32[]{:S(2)}) collective-permute-start(bf16[256,256]{1,0:T(8,128)(2,1)} %own_ref.1), channel_id=1, source_target_pairs={{0,16},{1,2},{2,1},{3,4},{4,3},{5,6},{6,5},{7,8},{8,7},{9,10},{10,... | collective-permute-start | bytes 393224 | tf_op jit(solution)/shard_map/ppermute | solution.py:344
  3.0 1.0 %copy-start.5 = (bf16[256,512]{1,0:T(8,128)(2,1)S(1)}, bf16[256,512]{1,0:T(8,128)(2,1)}, u32[]{:S(2)}) copy-start(bf16[256,512]{1,0:T(8,128)(2,1)} %queries_ref.1) | copy-start | bytes 786436
  4.0 0.9 %copy-start.6 = (bf16[256,256]{1,0:T(8,128)(2,1)S(1)}, bf16[256,256]{1,0:T(8,128)(2,1)}, u32[]{:S(2)}) copy-start(bf16[256,256]{1,0:T(8,128)(2,1)} %own_ref.1) | copy-start | bytes 393220
  4.9 1.9 %copy-start = (bf16[512,1024]{1,0:T(8,128)(2,1)S(1)}, bf16[512,1024]{1,0:T(8,128)(2,1)}, u32[]{:S(2)}) copy-start(bf16[512,1024]{1,0:T(8,128)(2,1)} %out_w_ref.1) | copy-start | bytes 3145732
  4.9 1.9 %copy-start.3 = (bf16[256,1024]{1,0:T(8,128)(2,1)S(1)}, bf16[256,1024]{1,0:T(8,128)(2,1)}, u32[]{:S(2)}) copy-start(bf16[256,1024]{1,0:T(8,128)(2,1)} %residual_ref.1) | copy-start | bytes 1572868
  4.9 1.9 %copy-start.4 = (bf16[1024,256]{1,0:T(8,128)(2,1)S(1)}, bf16[1024,256]{1,0:T(8,128)(2,1)}, u32[]{:S(2)}) copy-start(bf16[1024,256]{1,0:T(8,128)(2,1)} %kv_w_ref.1) | copy-start | bytes 1572868
  6.8 8.3 %copy-start.1 = (bf16[1024,512]{1,0:T(8,128)(2,1)S(1)}, bf16[1024,512]{1,0:T(8,128)(2,1)}, u32[]{:S(2)}) copy-start(bf16[1024,512]{1,0:T(8,128)(2,1)} %refs_3_.1) | copy-start | bytes 3145732
  9.0 6.0 %copy-start.8 = (s32[1,4]{1,0:T(1,128)S(1)}, s32[1,4]{1,0:T(1,128)}, u32[]{:S(2)}) copy-start(s32[1,4]{1,0:T(1,128)} %refs_1_.1) | copy-start | bytes 52
  9.0 6.0 %collective-permute-start.5 = (bf16[256,256]{1,0:T(8,128)(2,1)S(1)}, bf16[256,256]{1,0:T(8,128)(2,1)S(1)}, u32[]{:S(2)}, u32[]{:S(2)}) collective-permute-start(bf16[256,256]{1,0:T(8,128)(2,1)S(1)} %get-tuple-element.20.refs_4_), channel_id=1, source_target_pairs={{0,1},{1,0},{2,3},{3,2},{4,5},{5,4},{6,7},{7,6},{8,9},{9,8},{10,11... | collective-permute-start | bytes 393224 | tf_op jit(solution)/shard_map/ppermute | solution.py:422
  9.3 10.3 %collective-permute-start.2 = (bf16[256,256]{1,0:T(8,128)(2,1)S(1)}, bf16[256,256]{1,0:T(8,128)(2,1)S(1)}, u32[]{:S(2)}, u32[]{:S(2)}) collective-permute-start(bf16[256,256]{1,0:T(8,128)(2,1)S(1)} %get-tuple-element.20.refs_4_), channel_id=1, source_target_pairs={{0,8},{1,9},{2,10},{3,11},{4,12},{5,13},{6,14},{7,15},{8,0},{9,1},... | collective-permute-start | bytes 393224 | tf_op jit(solution)/shard_map/ppermute | solution.py:422
  13.0 6.8 %collective-permute-start.3 = (bf16[256,256]{1,0:T(8,128)(2,1)S(1)}, bf16[256,256]{1,0:T(8,128)(2,1)S(1)}, u32[]{:S(2)}, u32[]{:S(2)}) collective-permute-start(bf16[256,256]{1,0:T(8,128)(2,1)S(1)} %get-tuple-element.20.refs_4_), channel_id=1, source_target_pairs={{0,4},{1,5},{2,6},{3,7},{4,0},{5,1},{6,2},{7,3},{8,12},{9,13},{10,... | collective-permute-start | bytes 393224 | tf_op jit(solution)/shard_map/ppermute | solution.py:422
  14.5 5.3 %collective-permute-start.4 = (bf16[256,256]{1,0:T(8,128)(2,1)S(1)}, bf16[256,256]{1,0:T(8,128)(2,1)S(1)}, u32[]{:S(2)}, u32[]{:S(2)}) collective-permute-start(bf16[256,256]{1,0:T(8,128)(2,1)S(1)} %get-tuple-element.20.refs_4_), channel_id=1, source_target_pairs={{0,2},{1,3},{2,0},{3,1},{4,6},{5,7},{6,4},{7,5},{8,10},{9,11},{10,... | collective-permute-start | bytes 393224 | tf_op jit(solution)/shard_map/ppermute | solution.py:422
  15.0 4.8 %copy-start.2 = (bf16[512,1024]{1,0:T(8,128)(2,1)S(1)}, bf16[512,1024]{1,0:T(8,128)(2,1)}, u32[]{:S(2)}) copy-start(bf16[512,1024]{1,0:T(8,128)(2,1)} %refs_9_.1) | copy-start | bytes 3145732

commit v6 on v5

--- a/solution.py
+++ b/solution.py
@@ -15,22 +15,21 @@
 SCALE = HEAD_SIZE**-0.5 * math.log2(math.e)
 VMEM_LIMIT = 20 * 2**20
 ROWS = 256
+STEP = 512
+LAST_STEP = 1024
+TOTALS = 16
 
 
 def dot(a, b):
     return jnp.dot(a, b, preferred_element_type=jnp.float32)
 
 
+def dot_first(a, b):
+    return lax.dot_general(a, b, (((0,), (0,)), ((), ())), preferred_element_type=jnp.float32)
+
+
 def dot_t(a, b):
     return lax.dot_general(a, b, (((1,), (1,)), ((), ())), preferred_element_type=jnp.float32)
-
-
-def swap_halves(tile):
-    return jnp.concatenate([tile[:, HEAD_SIZE:], tile[:, :HEAD_SIZE]], axis=1)
-
-
-def low_half(rows):
-    return lax.broadcasted_iota(jnp.int32, (rows, LANES), 1) < HEAD_SIZE
 
 
 def splat(row, index, shape):
@@ -42,129 +41,116 @@
 def spread_queries(queries, kv_heads, spread_ref):
     rows, width = queries.shape
     heads = width // HEAD_SIZE
-    low = low_half(rows)
+    low = lax.broadcasted_iota(jnp.int32, (rows, LANES), 1) < HEAD_SIZE
     for head in range(heads):
         at, want = head % 2, head * kv_heads // heads % 2
         tile = queries[:, head // 2 * LANES : (head // 2 + 1) * LANES]
         if at != want:
-            tile = swap_halves(tile)
+            tile = jnp.concatenate([tile[:, HEAD_SIZE:], tile[:, :HEAD_SIZE]], axis=1)
         here = low if want == 0 else jnp.logical_not(low)
         spread_ref[head] = jnp.where(here, tile, jnp.zeros_like(tile))
 
 
 def spread_values(keyvals, values_ref, first, shown=None):
     rows, width = keyvals.shape
-    kv_heads = width // (2 * HEAD_SIZE)
-    low = low_half(rows)
+    kv_heads = values_ref.shape[0]
+    for begin in range(0, width // 2, LANES):
+        tile = jnp.transpose(keyvals[:, width // 2 + begin : width // 2 + begin + LANES])
+        if shown is not None:
+            tile = tile * shown
+        for g in range(begin // HEAD_SIZE, min((begin + LANES) // HEAD_SIZE, kv_heads)):
+            at = g * HEAD_SIZE - begin
+            values_ref[g, :HEAD_SIZE, pl.ds(first, rows)] = tile[at : at + HEAD_SIZE]
+    one = jnp.ones((TOTALS, rows), jnp.bfloat16)
     for g in range(kv_heads):
-        begin = width // 2 + g // 2 * LANES
-        tile = keyvals[:, begin : begin + LANES]
-        other = swap_halves(tile)
-        for s in range(2):
-            here = low if s == 0 else jnp.logical_not(low)
-            out = jnp.where(here, tile if g % 2 == s else other, jnp.ones_like(tile))
-            if shown is not None:
-                out = out * shown
-            values_ref[g, s, pl.ds(first, rows), :] = out
-
-
-def attend(q_ref, key_refs, values_ref, parts, mask, prior, sink):
+        values_ref[g, HEAD_SIZE:, pl.ds(first, rows)] = one if shown is None else one * shown
+
+
+def attend(q_ref, key_refs, values_ref, parts, mask, prior, sink, columns=STEP):
     heads = q_ref.shape[0]
     kv_heads = values_ref.shape[0]
-    steps = [
-        (g, s, [h for h in range(heads) if h * kv_heads // heads == g and h % 2 == s], part)
-        for g in range(kv_heads)
-        for s in range(2)
-        for part in range(len(parts))
-    ]
-
-    def score(g, s, mine, part):
+    group = heads // kv_heads
+    steps = []
+    for part, (row, rows, key, span) in enumerate(parts):
+        many = max(columns // rows, 1)
+        for head in range(0, heads, group):
+            for h in range(head, head + group, many):
+                steps.append((part, list(range(h, min(h + many, head + group)))))
+
+    def score(part, mine):
         row, rows, key, span = parts[part]
         q = jnp.concatenate([q_ref[h, pl.ds(row, rows), :] for h in mine], axis=0)
-        tiles, at = [], 0
+        lanes = pl.ds(mine[0] // group // 2 * LANES, LANES)
+        scores, at = [], 0
         for ref in key_refs:
             begin, end = max(key - at, 0), min(key + span - at, ref.shape[0])
             if begin < end:
-                keys = ref[pl.ds(begin, end - begin), pl.ds(g // 2 * LANES, LANES)]
-                scores = dot_t(q, keys)
-                tiles += [scores[:, c : c + LANES] for c in range(0, end - begin, LANES)]
+                scores.append(dot_t(ref[pl.ds(begin, end - begin), lanes], q))
             at += ref.shape[0]
-        return tiles
-
-    def mix(g, s, mine, part, tiles):
+        return jnp.concatenate(scores, axis=0)
+
+    def mix(part, mine, scores):
         row, rows, key, span = parts[part]
         here = pl.ds(row, rows)
         weights, tops, scales = [], [], []
         for n, h in enumerate(mine):
-            some = mask(h, part, [tile[n * rows : (n + 1) * rows] for tile in tiles])
-            top = jnp.max(functools.reduce(jnp.maximum, some), axis=1, keepdims=True)
-            top = jnp.broadcast_to(top, (rows, LANES))
+            some = mask(h, part, scores[:, n * rows : (n + 1) * rows])
+            top = jnp.max(some, axis=0, keepdims=True)
             if prior is not None:
-                old = prior[1][h, here, :]
+                old = prior[1][h, :1, here]
                 top = jnp.maximum(top, old)
                 scales.append(jnp.exp2((old - top) * SCALE))
             tops.append(top)
-            weights.append(
-                jnp.concatenate(
-                    [jnp.exp2((tile - top) * SCALE).astype(jnp.bfloat16) for tile in some], axis=1
-                )
-            )
-        sums = dot(jnp.concatenate(weights, axis=0), values_ref[g, s, pl.ds(key, span), :])
+            weights.append(jnp.exp2((some - top) * SCALE).astype(jnp.bfloat16))
+        sums = dot(
+            values_ref[mine[0] // group, :, pl.ds(key, span)], jnp.concatenate(weights, axis=1)
+        )
         for n, h in enumerate(mine):
-            one = sums[n * rows : (n + 1) * rows]
+            one = sums[:, n * rows : (n + 1) * rows]
             if prior is not None:
-                one = one + prior[0][h, here, :] * scales[n]
+                one = one + prior[0][h, :, here] * scales[n]
             sink(h, here, one, tops[n])
 
-    tiles = score(*steps[0])
+    scores = score(*steps[0])
     for n, step in enumerate(steps):
         ahead = score(*steps[n + 1]) if n + 1 < len(steps) else None
-        mix(*step, tiles)
-        tiles = ahead
+        mix(*step, scores)
+        scores = ahead
 
 
 def keep_state(sums_ref, tops_ref):
     def sink(head, here, sums, top):
-        sums_ref[head, here, :] = sums
-        tops_ref[head, here, :] = top
+        sums_ref[head, :, here] = sums
+        tops_ref[head, :, here] = jnp.broadcast_to(top, (tops_ref.shape[1], here.size))
 
     return sink
 
 
-def keep_sums(sums_ref):
+def keep_heads(attended_ref):
     def sink(head, here, sums, top):
-        sums_ref[head, here, :] = sums
+        attended_ref[head * HEAD_SIZE : (head + 1) * HEAD_SIZE, here] = (
+            sums[:HEAD_SIZE] / sums[HEAD_SIZE : HEAD_SIZE + 1]
+        ).astype(jnp.bfloat16)
 
     return sink
 
 
-def divide_pairs(sums_ref):
-    heads, rows, _ = sums_ref.shape
-    low = low_half(rows)
-    out = []
-    for head in range(0, heads, 2):
-        even, odd = sums_ref[head], sums_ref[head + 1]
-        total = swap_halves(jnp.where(low, odd, even))
-        out.append((jnp.where(low, even, odd) / total).astype(jnp.bfloat16))
-    return jnp.concatenate(out, axis=1)
-
-
 def window_mask(extents_ref, places, valid):
-    def mask(head, part, tiles):
+    def mask(head, part, scores):
         extent = extents_ref[head, :1, :]
-        shape = tiles[0].shape
-        gap = lax.broadcasted_iota(jnp.int32, shape, 0) - lax.broadcasted_iota(jnp.int32, shape, 1)
+        shape = (LANES, scores.shape[1])
+        gap = lax.broadcasted_iota(jnp.int32, shape, 1) - lax.broadcasted_iota(jnp.int32, shape, 0)
         out = []
-        for tile, (ahead, outer) in zip(tiles, places[part]):
+        for n, (ahead, outer) in enumerate(places[part]):
             reach = jnp.where(valid, extent, -1) if outer else extent
-            if ahead <= -shape[1]:
+            if ahead <= -LANES:
                 seen = gap <= reach + ahead
-            elif ahead >= shape[0]:
+            elif ahead >= LANES:
                 seen = gap >= ahead - reach
             else:
                 seen = jnp.abs(gap - ahead) <= reach
-            out.append(jnp.where(seen, tile, LOW))
-        return out
+            out.append(jnp.where(seen, scores[n * LANES : (n + 1) * LANES], LOW))
+        return jnp.concatenate(out, axis=0)
 
     return mask
 
@@ -228,7 +214,7 @@
     normed_ref,
     kv_ref,
     values_ref,
-    all_sums_ref,
+    attended_ref,
 ):
     rows = q_ref.shape[1]
     spread_values(odd_ref[...], values_ref, 0)
@@ -243,12 +229,12 @@
             parts,
             window_mask(extents_ref, places, valid),
             (sums_ref, tops_ref),
-            keep_sums(all_sums_ref),
+            keep_heads(attended_ref),
         )
 
     on_side(1, run)
     hidden = (
-        dot(divide_pairs(all_sums_ref), out_w_ref[...]) + residual_ref[...].astype(jnp.float32)
+        dot_first(attended_ref[...], out_w_ref[...]) + residual_ref[...].astype(jnp.float32)
     ).astype(jnp.bfloat16)
     hidden_ref[...] = hidden
     values = hidden.astype(jnp.float32)
@@ -258,21 +244,22 @@
     kv_ref[...] = dot(normed, kv_w_ref[...]).astype(jnp.bfloat16)
 
 
-def all_seen(head, part, tiles):
-    return tiles
+def all_seen(head, part, scores):
+    return scores
 
 
 def place_blocks(levels, blocks, own_ref, shown_ref, keys_ref, values_ref, first):
     rows = own_ref.shape[0]
     for n, (level, block) in enumerate(zip(levels, blocks)):
         shown = shown_ref[level, :1, :]
+        wide = jnp.concatenate([shown] * (rows // LANES), axis=1)
         for c in range(0, own_ref.shape[1] // 2, LANES):
             keys = block[:, c : c + LANES]
             here = jnp.broadcast_to(shown, keys.shape) > 0
             keys_ref[pl.ds(n * rows, rows), c : c + LANES] = jnp.where(
                 here, keys, own_ref[:, c : c + LANES]
             )
-        spread_values(block[...], values_ref, first + n * rows, shown)
+        spread_values(block[...], values_ref, first + n * rows, wide)
 
 
 def own_butterfly_kernel(levels, *refs):
@@ -306,8 +293,8 @@
     (shown_ref, own_ref, q_ref, sums_ref, tops_ref), refs = refs[:5], refs[5:]
     rows = q_ref.shape[1]
     if last:
-        hidden_ref, out_w_ref, out_ref, values_ref, keys_ref, all_sums_ref = refs
-        sink = keep_sums(all_sums_ref)
+        hidden_ref, out_w_ref, out_ref, values_ref, keys_ref, attended_ref = refs
+        sink = keep_heads(attended_ref)
     else:
         sums_out_ref, tops_out_ref, values_ref, keys_ref = refs
         sink = keep_state(sums_out_ref, tops_out_ref)
@@ -321,10 +308,11 @@
         all_seen,
         (sums_ref, tops_ref),
         sink,
+        LAST_STEP,
     )
     if last:
         out_ref[...] = (
-            dot(divide_pairs(all_sums_ref), out_w_ref[...]) + hidden_ref[...].astype(jnp.float32)
+            dot_first(attended_ref[...], out_w_ref[...]) + hidden_ref[...].astype(jnp.float32)
         ).astype(jnp.bfloat16)
 
 
@@ -364,14 +352,17 @@
     level_count = count.bit_length() - 1
     bf16, f32 = jnp.bfloat16, jnp.float32
     vmem = pl.BlockSpec(memory_space=pltpu.VMEM)
-    state = [jax.ShapeDtypeStruct((heads, rows, LANES), f32)] * 2
+    state = [
+        jax.ShapeDtypeStruct((heads, HEAD_SIZE + TOTALS, rows), f32),
+        jax.ShapeDtypeStruct((heads, 8, rows), f32),
+    ]
     queries = jax.ShapeDtypeStruct((heads, rows, LANES), bf16)
     wide = jax.ShapeDtypeStruct((rows, width), bf16)
-    all_sums = pltpu.VMEM((heads, rows, LANES), f32)
+    attended = pltpu.VMEM((q_width, rows), bf16)
 
     def call(kernel, name, in_specs, out_shape, scratch, key_rows, extra_macs, args):
         macs = 4 * rows * heads * HEAD_SIZE * key_rows + extra_macs
-        values = pltpu.VMEM((kv_heads, 2, key_rows, LANES), bf16)
+        values = pltpu.VMEM((kv_heads, HEAD_SIZE + TOTALS, key_rows), bf16)
         return pl.pallas_call(
             kernel,
             out_shape=out_shape,
@@ -401,7 +392,7 @@
         "halo_window",
         [vmem] * 8,
         [wide, wide, jax.ShapeDtypeStruct((rows, kv_width), bf16)],
-        [all_sums],
+        [attended],
         WIN,
         rows * width * (q_width + kv_width),
         (
@@ -453,7 +444,7 @@
         "far_butterfly",
         [vmem] * (7 + len(levels)),
         wide,
-        [key_block(levels), all_sums],
+        [key_block(levels), attended],
         rows * len(levels),
         rows * width * q_width,
         (*[others[level] for level in levels], shown, keyvals, queries_two, sums, tops, hidden, second_out),

time: 23.5 us -> 23.2 us (0.987)
  Pallas kernels: 9.47 us -> 9.12 us
    pallas_call x4, Pallas kernels: 9.47 us -> 9.12 us  [call(): pl.pallas_call(kernel, out_shape=out_shape, in_specs=in_specs, out_specs=...]
where the time goes in v6:
time: 23.2 us; the launch traced here: 23.1 us
  Pallas kernels  9.12 us (39%)
  starting transfers between devices  9.05 us (39%)
  waiting for transfers between devices  2.92 us (13%)
  local copies, waits for them, and re-layouts  1.89 us (8%)
    pallas_call x4, Pallas kernels, call(): pl.pallas_call(kernel, out_shape=out_shape, in_specs=in_specs, out_specs=...  9.12 us
    ppermute x4, starting transfers between devices, shards(): others[level] = lax.ppermute(keyvals, 'seq', route)  6.03 us
    ppermute x2, starting transfers between devices, exchange_edges(): return lax.ppermute(block, ('groups', 'seq'), route)  3.03 us
    ppermute x4, waiting for transfers between devices, shards(): others[level] = lax.ppermute(keyvals, 'seq', route)  2.91 us
    unnamed x18, local copies, waits for them, and re-layouts  1.89 us
  transfers between devices with their start and end apart: 6, of which 2 were waited for; matrix products, arithmetic and copies ran while one was open for 0% of the time, Pallas kernels for 16%

profile of v6, /device:TPU:0, one launch (start us, length us, event | category | flops | bytes accessed | tf_op | source)
XLA Modules:
  0.0 23.1 jit_solution(5436942459577135665)
XLA Ops:
  0.0 0.5 %collective-permute-start = (bf16[256,256]{1,0:T(8,128)(2,1)}, bf16[256,256]{1,0:T(8,128)(2,1)S(1)}, u32[]{:S(2)}, u32[]{:S(2)}) collective-permute-start(bf16[256,256]{1,0:T(8,128)(2,1)} %own_ref.1), channel_id=1, source_target_pairs={{0,1},{1,0},{2,3},{3,2},{4,5},{5,4},{6,7},{7,6},{8,9},{9,8},{10,11... | collective-permute-start | bytes 393224 | tf_op jit(solution)/shard_map/ppermute | solution.py:332
  0.5 2.6 %collective-permute-start.1 = (bf16[256,256]{1,0:T(8,128)(2,1)}, bf16[256,256]{1,0:T(8,128)(2,1)S(1)}, u32[]{:S(2)}, u32[]{:S(2)}) collective-permute-start(bf16[256,256]{1,0:T(8,128)(2,1)} %own_ref.1), channel_id=1, source_target_pairs={{0,16},{1,2},{2,1},{3,4},{4,3},{5,6},{6,5},{7,8},{8,7},{9,10},{10,... | collective-permute-start | bytes 393224 | tf_op jit(solution)/shard_map/ppermute | solution.py:332
  3.0 0.0 collective-permute-done.even_ref
  3.0 0.0 copy-done.7
  3.0 0.9 %copy-done.5 = bf16[256,512]{1,0:T(8,128)(2,1)S(1)} copy-done((bf16[256,512]{1,0:T(8,128)(2,1)S(1)}, bf16[256,512]{1,0:T(8,128)(2,1)}, u32[]{:S(2)}) %copy-start.5) | copy-done | bytes 262168
  4.0 0.9 %copy-done.6 = bf16[256,256]{1,0:T(8,128)(2,1)S(1)} copy-done((bf16[256,256]{1,0:T(8,128)(2,1)S(1)}, bf16[256,256]{1,0:T(8,128)(2,1)}, u32[]{:S(2)}) %copy-start.6) | copy-done | bytes 131096
  4.9 1.7 %own_window.1 = (s32[8,8,128]{2,1,0:T(8,128)S(1)}, bf16[8,256,128]{2,1,0:T(8,128)(2,1)S(1)}, f32[8,80,256]{2,1,0:T(8,128)S(1)}, f32[8,8,256]{2,1,0:T(8,128)S(1)}) custom-call(s32[1,8]{1,0:T(1,128)S(1)} %bitcast.1, bf16[256,512]{1,0:T(8,128)(2,1)S(1)} %copy-done.5, bf16[256,256]{1,0:T(8,128)(2,1)S(1)} %copy-done.6, ...), custom_call_target="tpu_custom_call" | custom-call | flops 4294967296 | bytes 2097152 | tf_op jit(solution)/shard_map/own_window/pallas_call | solution.py:366
  6.6 0.0 collective-permute-done.1.odd_ref
  6.6 0.0 copy-start.1
  6.6 2.1 %halo_window.1 = (bf16[256,1024]{1,0:T(8,128)(2,1)S(1)}, bf16[256,1024]{1,0:T(8,128)(2,1)S(1)}, bf16[256,256]{1,0:T(8,128)(2,1)S(1)}) custom-call(s32[8,8,128]{2,1,0:T(8,128)S(1)} %get-tuple-element.16.extents_ref, bf16[8,256,128]{2,1,0:T(8,128)(2,1)S(1)} %get-tuple-element.17.q_ref, bf16[256,256]{1,0:T(8,128)(2,1)S(1)} %collective-permute-done.1.odd_ref, ...), custom_call_target="tpu_custom_call" | custom-call | flops 5368709120 | bytes 2097152 | tf_op jit(solution)/shard_map/halo_window/pallas_call | solution.py:366
  8.7 0.0 copy-start.8
  8.7 0.3 %collective-permute-start.5 = (bf16[256,256]{1,0:T(8,128)(2,1)S(1)}, bf16[256,256]{1,0:T(8,128)(2,1)S(1)}, u32[]{:S(2)}, u32[]{:S(2)}) collective-permute-start(bf16[256,256]{1,0:T(8,128)(2,1)S(1)} %get-tuple-element.20.refs_4_), channel_id=1, source_target_pairs={{0,1},{1,0},{2,3},{3,2},{4,5},{5,4},{6,7},{7,6},{8,9},{9,8},{10,11... | collective-permute-start | bytes 393224 | tf_op jit(solution)/shard_map/ppermute | solution.py:413
  9.0 3.8 %collective-permute-start.2 = (bf16[256,256]{1,0:T(8,128)(2,1)S(1)}, bf16[256,256]{1,0:T(8,128)(2,1)S(1)}, u32[]{:S(2)}, u32[]{:S(2)}) collective-permute-start(bf16[256,256]{1,0:T(8,128)(2,1)S(1)} %get-tuple-element.20.refs_4_), channel_id=1, source_target_pairs={{0,8},{1,9},{2,10},{3,11},{4,12},{5,13},{6,14},{7,15},{8,0},{9,1},... | collective-permute-start | bytes 393224 | tf_op jit(solution)/shard_map/ppermute | solution.py:413
  12.8 1.6 %collective-permute-start.3 = (bf16[256,256]{1,0:T(8,128)(2,1)S(1)}, bf16[256,256]{1,0:T(8,128)(2,1)S(1)}, u32[]{:S(2)}, u32[]{:S(2)}) collective-permute-start(bf16[256,256]{1,0:T(8,128)(2,1)S(1)} %get-tuple-element.20.refs_4_), channel_id=1, source_target_pairs={{0,4},{1,5},{2,6},{3,7},{4,0},{5,1},{6,2},{7,3},{8,12},{9,13},{10,... | collective-permute-start | bytes 393224 | tf_op jit(solution)/shard_map/ppermute | solution.py:413
  14.4 0.3 %collective-permute-start.4 = (bf16[256,256]{1,0:T(8,128)(2,1)S(1)}, bf16[256,256]{1,0:T(8,128)(2,1)S(1)}, u32[]{:S(2)}, u32[]{:S(2)}) collective-permute-start(bf16[256,256]{1,0:T(8,128)(2,1)S(1)} %get-tuple-element.20.refs_4_), channel_id=1, source_target_pairs={{0,2},{1,3},{2,0},{3,1},{4,6},{5,7},{6,4},{7,5},{8,10},{9,11},{10,... | collective-permute-start | bytes 393224 | tf_op jit(solution)/shard_map/ppermute | solution.py:413
  14.8 0.0 collective-permute-done.5.refs_0_
  14.8 0.0 copy-done.1
  14.8 0.0 copy-start.2
  14.8 2.0 %own_butterfly.1 = (bf16[8,256,128]{2,1,0:T(8,128)(2,1)S(1)}, f32[8,80,256]{2,1,0:T(8,128)S(1)}, f32[8,8,256]{2,1,0:T(8,128)S(1)}, bf16[4,16,128]{2,1,0:T(8,128)(2,1)S(1)}) custom-call(bf16[256,256]{1,0:T(8,128)(2,1)S(1)} %collective-permute-done.5.refs_0_, s32[1,4]{1,0:T(1,128)S(1)} %copy-done.8, bf16[256,1024]{1,0:T(8,128)(2,1)S(1)} %get-tuple-element.21.refs_2_, ...), custom_call_target="tpu_custom_call" | custom-call | flops 6442450944 | bytes 2097152 | tf_op jit(solution)/shard_map/own_butterfly/pallas_call | solution.py:366
  16.7 2.7 %collective-permute-done.2.refs_0_ = bf16[256,256]{1,0:T(8,128)(2,1)S(1)} collective-permute-done((bf16[256,256]{1,0:T(8,128)(2,1)S(1)}, bf16[256,256]{1,0:T(8,128)(2,1)S(1)}, u32[]{:S(2)}, u32[]{:S(2)}) %collective-permute-start.2) | collective-permute-done | bytes 131104 | tf_op jit(solution)/shard_map/ppermute | solution.py:413
  19.5 0.2 collective-permute-done.3.refs_1_
  19.7 0.0 collective-permute-done.4.refs_2_
  19.7 0.0 copy-done.2
  19.7 3.4 %far_butterfly.1 = bf16[256,1024]{1,0:T(8,128)(2,1)} custom-call(bf16[256,256]{1,0:T(8,128)(2,1)S(1)} %collective-permute-done.2.refs_0_, bf16[256,256]{1,0:T(8,128)(2,1)S(1)} %collective-permute-done.3.refs_1_, bf16[256,256]{1,0:T(8,128)(2,1)S(1)} %collective-permute-done.4.refs_2_, bf16[4,16,128]{2,1,0:T(8,128)(2,1)S(1)} %get-tuple-element.22.refs_3_, ...), custom_call_target="tpu_custom_call" | custom-call | flops 8589934592 | bytes 2097152 | tf_op jit(solution)/shard_map/far_butterfly/pallas_call | solution.py:366
  (10 shorter events, 0.0 us)
Async XLA Ops:
  0.0 3.0 %copy-start.7 = (s32[8]{0:T(128)S(1)}, s32[8]{0:T(128)}, u32[]{:S(2)}) copy-start(s32[8]{0:T(128)} %param.12) | copy-start | bytes 100
  0.0 3.0 %collective-permute-start = (bf16[256,256]{1,0:T(8,128)(2,1)}, bf16[256,256]{1,0:T(8,128)(2,1)S(1)}, u32[]{:S(2)}, u32[]{:S(2)}) collective-permute-start(bf16[256,256]{1,0:T(8,128)(2,1)} %own_ref.1), channel_id=1, source_target_pairs={{0,1},{1,0},{2,3},{3,2},{4,5},{5,4},{6,7},{7,6},{8,9},{9,8},{10,11... | collective-permute-start | bytes 393224 | tf_op jit(solution)/shard_map/ppermute | solution.py:332
  0.5 6.1 %collective-permute-start.1 = (bf16[256,256]{1,0:T(8,128)(2,1)}, bf16[256,256]{1,0:T(8,128)(2,1)S(1)}, u32[]{:S(2)}, u32[]{:S(2)}) collective-permute-start(bf16[256,256]{1,0:T(8,128)(2,1)} %own_ref.1), channel_id=1, source_target_pairs={{0,16},{1,2},{2,1},{3,4},{4,3},{5,6},{6,5},{7,8},{8,7},{9,10},{10,... | collective-permute-start | bytes 393224 | tf_op jit(solution)/shard_map/ppermute | solution.py:332
  3.0 1.0 %copy-start.5 = (bf16[256,512]{1,0:T(8,128)(2,1)S(1)}, bf16[256,512]{1,0:T(8,128)(2,1)}, u32[]{:S(2)}) copy-start(bf16[256,512]{1,0:T(8,128)(2,1)} %queries_ref.1) | copy-start | bytes 786436
  4.0 0.9 %copy-start.6 = (bf16[256,256]{1,0:T(8,128)(2,1)S(1)}, bf16[256,256]{1,0:T(8,128)(2,1)}, u32[]{:S(2)}) copy-start(bf16[256,256]{1,0:T(8,128)(2,1)} %own_ref.1) | copy-start | bytes 393220
  4.9 1.7 %copy-start = (bf16[512,1024]{1,0:T(8,128)(2,1)S(1)}, bf16[512,1024]{1,0:T(8,128)(2,1)}, u32[]{:S(2)}) copy-start(bf16[512,1024]{1,0:T(8,128)(2,1)} %out_w_ref.1) | copy-start | bytes 3145732
  4.9 1.7 %copy-start.3 = (bf16[256,1024]{1,0:T(8,128)(2,1)S(1)}, bf16[256,1024]{1,0:T(8,128)(2,1)}, u32[]{:S(2)}) copy-start(bf16[256,1024]{1,0:T(8,128)(2,1)} %residual_ref.1) | copy-start | bytes 1572868
  4.9 1.7 %copy-start.4 = (bf16[1024,256]{1,0:T(8,128)(2,1)S(1)}, bf16[1024,256]{1,0:T(8,128)(2,1)}, u32[]{:S(2)}) copy-start(bf16[1024,256]{1,0:T(8,128)(2,1)} %kv_w_ref.1) | copy-start | bytes 1572868
  6.6 8.2 %copy-start.1 = (bf16[1024,512]{1,0:T(8,128)(2,1)S(1)}, bf16[1024,512]{1,0:T(8,128)(2,1)}, u32[]{:S(2)}) copy-start(bf16[1024,512]{1,0:T(8,128)(2,1)} %refs_3_.1) | copy-start | bytes 3145732
  8.7 6.0 %copy-start.8 = (s32[1,4]{1,0:T(1,128)S(1)}, s32[1,4]{1,0:T(1,128)}, u32[]{:S(2)}) copy-start(s32[1,4]{1,0:T(1,128)} %refs_1_.1) | copy-start | bytes 52
  8.7 6.0 %collective-permute-start.5 = (bf16[256,256]{1,0:T(8,128)(2,1)S(1)}, bf16[256,256]{1,0:T(8,128)(2,1)S(1)}, u32[]{:S(2)}, u32[]{:S(2)}) collective-permute-start(bf16[256,256]{1,0:T(8,128)(2,1)S(1)} %get-tuple-element.20.refs_4_), channel_id=1, source_target_pairs={{0,1},{1,0},{2,3},{3,2},{4,5},{5,4},{6,7},{7,6},{8,9},{9,8},{10,11... | collective-permute-start | bytes 393224 | tf_op jit(solution)/shard_map/ppermute | solution.py:413
  9.0 10.5 %collective-permute-start.2 = (bf16[256,256]{1,0:T(8,128)(2,1)S(1)}, bf16[256,256]{1,0:T(8,128)(2,1)S(1)}, u32[]{:S(2)}, u32[]{:S(2)}) collective-permute-start(bf16[256,256]{1,0:T(8,128)(2,1)S(1)} %get-tuple-element.20.refs_4_), channel_id=1, source_target_pairs={{0,8},{1,9},{2,10},{3,11},{4,12},{5,13},{6,14},{7,15},{8,0},{9,1},... | collective-permute-start | bytes 393224 | tf_op jit(solution)/shard_map/ppermute | solution.py:413
  12.8 6.8 %collective-permute-start.3 = (bf16[256,256]{1,0:T(8,128)(2,1)S(1)}, bf16[256,256]{1,0:T(8,128)(2,1)S(1)}, u32[]{:S(2)}, u32[]{:S(2)}) collective-permute-start(bf16[256,256]{1,0:T(8,128)(2,1)S(1)} %get-tuple-element.20.refs_4_), channel_id=1, source_target_pairs={{0,4},{1,5},{2,6},{3,7},{4,0},{5,1},{6,2},{7,3},{8,12},{9,13},{10,... | collective-permute-start | bytes 393224 | tf_op jit(solution)/shard_map/ppermute | solution.py:413
  14.4 5.3 %collective-permute-start.4 = (bf16[256,256]{1,0:T(8,128)(2,1)S(1)}, bf16[256,256]{1,0:T(8,128)(2,1)S(1)}, u32[]{:S(2)}, u32[]{:S(2)}) collective-permute-start(bf16[256,256]{1,0:T(8,128)(2,1)S(1)} %get-tuple-element.20.refs_4_), channel_id=1, source_target_pairs={{0,2},{1,3},{2,0},{3,1},{4,6},{5,7},{6,4},{7,5},{8,10},{9,11},{10,... | collective-permute-start | bytes 393224 | tf_op jit(solution)/shard_map/ppermute | solution.py:413
  14.8 4.9 %copy-start.2 = (bf16[512,1024]{1,0:T(8,128)(2,1)S(1)}, bf16[512,1024]{1,0:T(8,128)(2,1)}, u32[]{:S(2)}) copy-start(bf16[512,1024]{1,0:T(8,128)(2,1)} %refs_9_.1) | copy-start | bytes 3145732

commit v7 on v6

--- a/solution.py
+++ b/solution.py
@@ -18,6 +18,7 @@
 STEP = 512
 LAST_STEP = 1024
 TOTALS = 16
+PIECE = 128
 
 
 def dot(a, b):
@@ -233,15 +234,25 @@
         )
 
     on_side(1, run)
-    hidden = (
-        dot_first(attended_ref[...], out_w_ref[...]) + residual_ref[...].astype(jnp.float32)
-    ).astype(jnp.bfloat16)
-    hidden_ref[...] = hidden
-    values = hidden.astype(jnp.float32)
-    scale = lax.rsqrt(jnp.mean(values * values, axis=-1, keepdims=True) + 1e-05)
-    normed = (values * scale).astype(jnp.bfloat16)
-    normed_ref[...] = normed
-    kv_ref[...] = dot(normed, kv_w_ref[...]).astype(jnp.bfloat16)
+    def project(here):
+        hidden_ref[here, :] = (
+            dot_first(attended_ref[:, here], out_w_ref[...])
+            + residual_ref[here, :].astype(jnp.float32)
+        ).astype(jnp.bfloat16)
+
+    def norm(here):
+        values = hidden_ref[here, :].astype(jnp.float32)
+        scale = lax.rsqrt(jnp.mean(values * values, axis=-1, keepdims=True) + 1e-05)
+        normed = (values * scale).astype(jnp.bfloat16)
+        normed_ref[here, :] = normed
+        kv_ref[here, :] = dot(normed, kv_w_ref[...]).astype(jnp.bfloat16)
+
+    pieces = [pl.ds(row, PIECE) for row in range(0, rows, PIECE)]
+    for n, here in enumerate(pieces):
+        project(here)
+        if n:
+            norm(pieces[n - 1])
+    norm(pieces[-1])
 
 
 def all_seen(head, part, scores):

time: 23.2 us -> 22.9 us (0.987)
  Pallas kernels: 9.12 us -> 8.83 us
    pallas_call x4, Pallas kernels: 9.12 us -> 8.83 us  [call(): pl.pallas_call(kernel, out_shape=out_shape, in_specs=in_specs, out_specs=...]
where the time goes in v7:
time: 22.9 us; the launch traced here: 22.8 us
  starting transfers between devices  9.06 us (40%)
  Pallas kernels  8.83 us (39%)
  waiting for transfers between devices  2.92 us (13%)
  local copies, waits for them, and re-layouts  1.89 us (8%)
    pallas_call x4, Pallas kernels, call(): pl.pallas_call(kernel, out_shape=out_shape, in_specs=in_specs, out_specs=...  8.83 us
    ppermute x4, starting transfers between devices, shards(): others[level] = lax.ppermute(keyvals, 'seq', route)  6.03 us
    ppermute x2, starting transfers between devices, exchange_edges(): return lax.ppermute(block, ('groups', 'seq'), route)  3.03 us
    ppermute x4, waiting for transfers between devices, shards(): others[level] = lax.ppermute(keyvals, 'seq', route)  2.91 us
    unnamed x18, local copies, waits for them, and re-layouts  1.89 us
  transfers between devices with their start and end apart: 6, of which 2 were waited for; matrix products, arithmetic and copies ran while one was open for 0% of the time, Pallas kernels for 16%

profile of v7, /device:TPU:0, one launch (start us, length us, event | category | flops | bytes accessed | tf_op | source)
XLA Modules:
  0.0 22.8 jit_solution(17958282953339459490)
XLA Ops:
  0.0 0.5 %collective-permute-start = (bf16[256,256]{1,0:T(8,128)(2,1)}, bf16[256,256]{1,0:T(8,128)(2,1)S(1)}, u32[]{:S(2)}, u32[]{:S(2)}) collective-permute-start(bf16[256,256]{1,0:T(8,128)(2,1)} %own_ref.1), channel_id=1, source_target_pairs={{0,1},{1,0},{2,3},{3,2},{4,5},{5,4},{6,7},{7,6},{8,9},{9,8},{10,11... | collective-permute-start | bytes 393224 | tf_op jit(solution)/shard_map/ppermute | solution.py:343
  0.5 2.6 %collective-permute-start.1 = (bf16[256,256]{1,0:T(8,128)(2,1)}, bf16[256,256]{1,0:T(8,128)(2,1)S(1)}, u32[]{:S(2)}, u32[]{:S(2)}) collective-permute-start(bf16[256,256]{1,0:T(8,128)(2,1)} %own_ref.1), channel_id=1, source_target_pairs={{0,16},{1,2},{2,1},{3,4},{4,3},{5,6},{6,5},{7,8},{8,7},{9,10},{10,... | collective-permute-start | bytes 393224 | tf_op jit(solution)/shard_map/ppermute | solution.py:343
  3.0 0.0 collective-permute-done.even_ref
  3.0 0.0 copy-done.7
  3.0 0.9 %copy-done.5 = bf16[256,512]{1,0:T(8,128)(2,1)S(1)} copy-done((bf16[256,512]{1,0:T(8,128)(2,1)S(1)}, bf16[256,512]{1,0:T(8,128)(2,1)}, u32[]{:S(2)}) %copy-start.5) | copy-done | bytes 262168
  4.0 0.9 %copy-done.6 = bf16[256,256]{1,0:T(8,128)(2,1)S(1)} copy-done((bf16[256,256]{1,0:T(8,128)(2,1)S(1)}, bf16[256,256]{1,0:T(8,128)(2,1)}, u32[]{:S(2)}) %copy-start.6) | copy-done | bytes 131096
  4.9 1.7 %own_window.1 = (s32[8,8,128]{2,1,0:T(8,128)S(1)}, bf16[8,256,128]{2,1,0:T(8,128)(2,1)S(1)}, f32[8,80,256]{2,1,0:T(8,128)S(1)}, f32[8,8,256]{2,1,0:T(8,128)S(1)}) custom-call(s32[1,8]{1,0:T(1,128)S(1)} %bitcast.1, bf16[256,512]{1,0:T(8,128)(2,1)S(1)} %copy-done.5, bf16[256,256]{1,0:T(8,128)(2,1)S(1)} %copy-done.6, ...), custom_call_target="tpu_custom_call" | custom-call | flops 4294967296 | bytes 2097152 | tf_op jit(solution)/shard_map/own_window/pallas_call | solution.py:377
  6.6 0.0 collective-permute-done.1.odd_ref
  6.6 0.0 copy-done
  6.6 0.0 copy-done.3
  6.6 0.0 copy-start.1
  6.6 1.8 %halo_window.1 = (bf16[256,1024]{1,0:T(8,128)(2,1)S(1)}, bf16[256,1024]{1,0:T(8,128)(2,1)S(1)}, bf16[256,256]{1,0:T(8,128)(2,1)S(1)}) custom-call(s32[8,8,128]{2,1,0:T(8,128)S(1)} %get-tuple-element.16.extents_ref, bf16[8,256,128]{2,1,0:T(8,128)(2,1)S(1)} %get-tuple-element.17.q_ref, bf16[256,256]{1,0:T(8,128)(2,1)S(1)} %collective-permute-done.1.odd_ref, ...), custom_call_target="tpu_custom_call" | custom-call | flops 5368709120 | bytes 2097152 | tf_op jit(solution)/shard_map/halo_window/pallas_call | solution.py:377
  8.4 0.0 copy-start.8
  8.4 0.3 %collective-permute-start.5 = (bf16[256,256]{1,0:T(8,128)(2,1)S(1)}, bf16[256,256]{1,0:T(8,128)(2,1)S(1)}, u32[]{:S(2)}, u32[]{:S(2)}) collective-permute-start(bf16[256,256]{1,0:T(8,128)(2,1)S(1)} %get-tuple-element.20.refs_4_), channel_id=1, source_target_pairs={{0,1},{1,0},{2,3},{3,2},{4,5},{5,4},{6,7},{7,6},{8,9},{9,8},{10,11... | collective-permute-start | bytes 393224 | tf_op jit(solution)/shard_map/ppermute | solution.py:424
  8.7 3.8 %collective-permute-start.2 = (bf16[256,256]{1,0:T(8,128)(2,1)S(1)}, bf16[256,256]{1,0:T(8,128)(2,1)S(1)}, u32[]{:S(2)}, u32[]{:S(2)}) collective-permute-start(bf16[256,256]{1,0:T(8,128)(2,1)S(1)} %get-tuple-element.20.refs_4_), channel_id=1, source_target_pairs={{0,8},{1,9},{2,10},{3,11},{4,12},{5,13},{6,14},{7,15},{8,0},{9,1},... | collective-permute-start | bytes 393224 | tf_op jit(solution)/shard_map/ppermute | solution.py:424
  12.5 1.6 %collective-permute-start.3 = (bf16[256,256]{1,0:T(8,128)(2,1)S(1)}, bf16[256,256]{1,0:T(8,128)(2,1)S(1)}, u32[]{:S(2)}, u32[]{:S(2)}) collective-permute-start(bf16[256,256]{1,0:T(8,128)(2,1)S(1)} %get-tuple-element.20.refs_4_), channel_id=1, source_target_pairs={{0,4},{1,5},{2,6},{3,7},{4,0},{5,1},{6,2},{7,3},{8,12},{9,13},{10,... | collective-permute-start | bytes 393224 | tf_op jit(solution)/shard_map/ppermute | solution.py:424
  14.1 0.3 %collective-permute-start.4 = (bf16[256,256]{1,0:T(8,128)(2,1)S(1)}, bf16[256,256]{1,0:T(8,128)(2,1)S(1)}, u32[]{:S(2)}, u32[]{:S(2)}) collective-permute-start(bf16[256,256]{1,0:T(8,128)(2,1)S(1)} %get-tuple-element.20.refs_4_), channel_id=1, source_target_pairs={{0,2},{1,3},{2,0},{3,1},{4,6},{5,7},{6,4},{7,5},{8,10},{9,11},{10,... | collective-permute-start | bytes 393224 | tf_op jit(solution)/shard_map/ppermute | solution.py:424
  14.5 0.0 collective-permute-done.5.refs_0_
  14.5 0.0 copy-start.2
  14.5 2.0 %own_butterfly.1 = (bf16[8,256,128]{2,1,0:T(8,128)(2,1)S(1)}, f32[8,80,256]{2,1,0:T(8,128)S(1)}, f32[8,8,256]{2,1,0:T(8,128)S(1)}, bf16[4,16,128]{2,1,0:T(8,128)(2,1)S(1)}) custom-call(bf16[256,256]{1,0:T(8,128)(2,1)S(1)} %collective-permute-done.5.refs_0_, s32[1,4]{1,0:T(1,128)S(1)} %copy-done.8, bf16[256,1024]{1,0:T(8,128)(2,1)S(1)} %get-tuple-element.21.refs_2_, ...), custom_call_target="tpu_custom_call" | custom-call | flops 6442450944 | bytes 2097152 | tf_op jit(solution)/shard_map/own_butterfly/pallas_call | solution.py:377
  16.5 2.7 %collective-permute-done.2.refs_0_ = bf16[256,256]{1,0:T(8,128)(2,1)S(1)} collective-permute-done((bf16[256,256]{1,0:T(8,128)(2,1)S(1)}, bf16[256,256]{1,0:T(8,128)(2,1)S(1)}, u32[]{:S(2)}, u32[]{:S(2)}) %collective-permute-start.2) | collective-permute-done | bytes 131104 | tf_op jit(solution)/shard_map/ppermute | solution.py:424
  19.2 0.2 collective-permute-done.3.refs_1_
  19.4 0.0 collective-permute-done.4.refs_2_
  19.4 3.4 %far_butterfly.1 = bf16[256,1024]{1,0:T(8,128)(2,1)} custom-call(bf16[256,256]{1,0:T(8,128)(2,1)S(1)} %collective-permute-done.2.refs_0_, bf16[256,256]{1,0:T(8,128)(2,1)S(1)} %collective-permute-done.3.refs_1_, bf16[256,256]{1,0:T(8,128)(2,1)S(1)} %collective-permute-done.4.refs_2_, bf16[4,16,128]{2,1,0:T(8,128)(2,1)S(1)} %get-tuple-element.22.refs_3_, ...), custom_call_target="tpu_custom_call" | custom-call | flops 8589934592 | bytes 2097152 | tf_op jit(solution)/shard_map/far_butterfly/pallas_call | solution.py:377
  (10 shorter events, 0.0 us)
Async XLA Ops:
  0.0 3.0 %copy-start.7 = (s32[8]{0:T(128)S(1)}, s32[8]{0:T(128)}, u32[]{:S(2)}) copy-start(s32[8]{0:T(128)} %param.12) | copy-start | bytes 100
  0.0 3.0 %collective-permute-start = (bf16[256,256]{1,0:T(8,128)(2,1)}, bf16[256,256]{1,0:T(8,128)(2,1)S(1)}, u32[]{:S(2)}, u32[]{:S(2)}) collective-permute-start(bf16[256,256]{1,0:T(8,128)(2,1)} %own_ref.1), channel_id=1, source_target_pairs={{0,1},{1,0},{2,3},{3,2},{4,5},{5,4},{6,7},{7,6},{8,9},{9,8},{10,11... | collective-permute-start | bytes 393224 | tf_op jit(solution)/shard_map/ppermute | solution.py:343
  0.5 6.1 %collective-permute-start.1 = (bf16[256,256]{1,0:T(8,128)(2,1)}, bf16[256,256]{1,0:T(8,128)(2,1)S(1)}, u32[]{:S(2)}, u32[]{:S(2)}) collective-permute-start(bf16[256,256]{1,0:T(8,128)(2,1)} %own_ref.1), channel_id=1, source_target_pairs={{0,16},{1,2},{2,1},{3,4},{4,3},{5,6},{6,5},{7,8},{8,7},{9,10},{10,... | collective-permute-start | bytes 393224 | tf_op jit(solution)/shard_map/ppermute | solution.py:343
  3.0 1.0 %copy-start.5 = (bf16[256,512]{1,0:T(8,128)(2,1)S(1)}, bf16[256,512]{1,0:T(8,128)(2,1)}, u32[]{:S(2)}) copy-start(bf16[256,512]{1,0:T(8,128)(2,1)} %queries_ref.1) | copy-start | bytes 786436
  4.0 0.9 %copy-start.6 = (bf16[256,256]{1,0:T(8,128)(2,1)S(1)}, bf16[256,256]{1,0:T(8,128)(2,1)}, u32[]{:S(2)}) copy-start(bf16[256,256]{1,0:T(8,128)(2,1)} %own_ref.1) | copy-start | bytes 393220
  4.9 1.7 %copy-start = (bf16[512,1024]{1,0:T(8,128)(2,1)S(1)}, bf16[512,1024]{1,0:T(8,128)(2,1)}, u32[]{:S(2)}) copy-start(bf16[512,1024]{1,0:T(8,128)(2,1)} %out_w_ref.1) | copy-start | bytes 3145732
  4.9 1.7 %copy-start.3 = (bf16[256,1024]{1,0:T(8,128)(2,1)S(1)}, bf16[256,1024]{1,0:T(8,128)(2,1)}, u32[]{:S(2)}) copy-start(bf16[256,1024]{1,0:T(8,128)(2,1)} %residual_ref.1) | copy-start | bytes 1572868
  4.9 1.7 %copy-start.4 = (bf16[1024,256]{1,0:T(8,128)(2,1)S(1)}, bf16[1024,256]{1,0:T(8,128)(2,1)}, u32[]{:S(2)}) copy-start(bf16[1024,256]{1,0:T(8,128)(2,1)} %kv_w_ref.1) | copy-start | bytes 1572868
  6.6 7.9 %copy-start.1 = (bf16[1024,512]{1,0:T(8,128)(2,1)S(1)}, bf16[1024,512]{1,0:T(8,128)(2,1)}, u32[]{:S(2)}) copy-start(bf16[1024,512]{1,0:T(8,128)(2,1)} %refs_3_.1) | copy-start | bytes 3145732
  8.4 6.0 %copy-start.8 = (s32[1,4]{1,0:T(1,128)S(1)}, s32[1,4]{1,0:T(1,128)}, u32[]{:S(2)}) copy-start(s32[1,4]{1,0:T(1,128)} %refs_1_.1) | copy-start | bytes 52
  8.4 6.0 %collective-permute-start.5 = (bf16[256,256]{1,0:T(8,128)(2,1)S(1)}, bf16[256,256]{1,0:T(8,128)(2,1)S(1)}, u32[]{:S(2)}, u32[]{:S(2)}) collective-permute-start(bf16[256,256]{1,0:T(8,128)(2,1)S(1)} %get-tuple-element.20.refs_4_), channel_id=1, source_target_pairs={{0,1},{1,0},{2,3},{3,2},{4,5},{5,4},{6,7},{7,6},{8,9},{9,8},{10,11... | collective-permute-start | bytes 393224 | tf_op jit(solution)/shard_map/ppermute | solution.py:424
  8.7 10.5 %collective-permute-start.2 = (bf16[256,256]{1,0:T(8,128)(2,1)S(1)}, bf16[256,256]{1,0:T(8,128)(2,1)S(1)}, u32[]{:S(2)}, u32[]{:S(2)}) collective-permute-start(bf16[256,256]{1,0:T(8,128)(2,1)S(1)} %get-tuple-element.20.refs_4_), channel_id=1, source_target_pairs={{0,8},{1,9},{2,10},{3,11},{4,12},{5,13},{6,14},{7,15},{8,0},{9,1},... | collective-permute-start | bytes 393224 | tf_op jit(solution)/shard_map/ppermute | solution.py:424
  12.5 6.8 %collective-permute-start.3 = (bf16[256,256]{1,0:T(8,128)(2,1)S(1)}, bf16[256,256]{1,0:T(8,128)(2,1)S(1)}, u32[]{:S(2)}, u32[]{:S(2)}) collective-permute-start(bf16[256,256]{1,0:T(8,128)(2,1)S(1)} %get-tuple-element.20.refs_4_), channel_id=1, source_target_pairs={{0,4},{1,5},{2,6},{3,7},{4,0},{5,1},{6,2},{7,3},{8,12},{9,13},{10,... | collective-permute-start | bytes 393224 | tf_op jit(solution)/shard_map/ppermute | solution.py:424
  14.1 5.3 %collective-permute-start.4 = (bf16[256,256]{1,0:T(8,128)(2,1)S(1)}, bf16[256,256]{1,0:T(8,128)(2,1)S(1)}, u32[]{:S(2)}, u32[]{:S(2)}) collective-permute-start(bf16[256,256]{1,0:T(8,128)(2,1)S(1)} %get-tuple-element.20.refs_4_), channel_id=1, source_target_pairs={{0,2},{1,3},{2,0},{3,1},{4,6},{5,7},{6,4},{7,5},{8,10},{9,11},{10,... | collective-permute-start | bytes 393224 | tf_op jit(solution)/shard_map/ppermute | solution.py:424
  14.5 4.9 %copy-start.2 = (bf16[512,1024]{1,0:T(8,128)(2,1)S(1)}, bf16[512,1024]{1,0:T(8,128)(2,1)}, u32[]{:S(2)}) copy-start(bf16[512,1024]{1,0:T(8,128)(2,1)} %refs_9_.1) | copy-start | bytes 3145732

commit v8 on v7

--- a/solution.py
+++ b/solution.py
@@ -16,7 +16,6 @@
 VMEM_LIMIT = 20 * 2**20
 ROWS = 256
 STEP = 512
-LAST_STEP = 1024
 TOTALS = 16
 PIECE = 128
 
@@ -67,13 +66,13 @@
         values_ref[g, HEAD_SIZE:, pl.ds(first, rows)] = one if shown is None else one * shown
 
 
-def attend(q_ref, key_refs, values_ref, parts, mask, prior, sink, columns=STEP):
+def attend(q_ref, key_refs, values_ref, parts, mask, prior, sink):
     heads = q_ref.shape[0]
     kv_heads = values_ref.shape[0]
     group = heads // kv_heads
     steps = []
     for part, (row, rows, key, span) in enumerate(parts):
-        many = max(columns // rows, 1)
+        many = max(STEP // rows, 1)
         for head in range(0, heads, group):
             for h in range(head, head + group, many):
                 steps.append((part, list(range(h, min(h + many, head + group)))))
@@ -90,7 +89,7 @@
             at += ref.shape[0]
         return jnp.concatenate(scores, axis=0)
 
-    def mix(part, mine, scores):
+    def soften(part, mine, scores):
         row, rows, key, span = parts[part]
         here = pl.ds(row, rows)
         weights, tops, scales = [], [], []
@@ -103,21 +102,23 @@
                 scales.append(jnp.exp2((old - top) * SCALE))
             tops.append(top)
             weights.append(jnp.exp2((some - top) * SCALE).astype(jnp.bfloat16))
-        sums = dot(
-            values_ref[mine[0] // group, :, pl.ds(key, span)], jnp.concatenate(weights, axis=1)
-        )
+        return jnp.concatenate(weights, axis=1), tops, scales
+
+    def mix(part, mine, weights, tops, scales):
+        row, rows, key, span = parts[part]
+        here = pl.ds(row, rows)
+        sums = dot(values_ref[mine[0] // group, :, pl.ds(key, span)], weights)
         for n, h in enumerate(mine):
             one = sums[:, n * rows : (n + 1) * rows]
             if prior is not None:
                 one = one + prior[0][h, :, here] * scales[n]
             sink(h, here, one, tops[n])
 
-    scores = score(*steps[0])
+    scores = [score(*step) for step in steps[:2]]
     for n, step in enumerate(steps):
-        ahead = score(*steps[n + 1]) if n + 1 < len(steps) else None
-        mix(*step, scores)
-        scores = ahead
-
+        if n + 2 < len(steps):
+            scores.append(score(*steps[n + 2]))
+        mix(*step, *soften(*step, scores[n]))
 
 def keep_state(sums_ref, tops_ref):
     def sink(head, here, sums, top):
@@ -319,7 +320,6 @@
         all_seen,
         (sums_ref, tops_ref),
         sink,
-        LAST_STEP,
     )
     if last:
         out_ref[...] = (

time: 22.9 us -> 22.9 us (level)
  no operation moved by 1% of the time
where the time goes in v8:
time: 22.9 us; the launch traced here: 22.7 us
  starting transfers between devices  8.93 us (39%)
  Pallas kernels  8.86 us (39%)
  waiting for transfers between devices  2.94 us (13%)
  local copies, waits for them, and re-layouts  1.89 us (8%)
    pallas_call x4, Pallas kernels, call(): pl.pallas_call(kernel, out_shape=out_shape, in_specs=in_specs, out_specs=...  8.86 us
    ppermute x4, starting transfers between devices, shards(): others[level] = lax.ppermute(keyvals, 'seq', route)  5.9 us
    ppermute x2, starting transfers between devices, exchange_edges(): return lax.ppermute(block, ('groups', 'seq'), route)  3.03 us
    ppermute x4, waiting for transfers between devices, shards(): others[level] = lax.ppermute(keyvals, 'seq', route)  2.93 us
    unnamed x18, local copies, waits for them, and re-layouts  1.89 us
  transfers between devices with their start and end apart: 6, of which 2 were waited for; matrix products, arithmetic and copies ran while one was open for 0% of the time, Pallas kernels for 16%

profile of v8, /device:TPU:0, one launch (start us, length us, event | category | flops | bytes accessed | tf_op | source)
XLA Modules:
  0.0 22.7 jit_solution(18031131730757542918)
XLA Ops:
  0.0 0.5 %collective-permute-start = (bf16[256,256]{1,0:T(8,128)(2,1)}, bf16[256,256]{1,0:T(8,128)(2,1)S(1)}, u32[]{:S(2)}, u32[]{:S(2)}) collective-permute-start(bf16[256,256]{1,0:T(8,128)(2,1)} %own_ref.1), channel_id=1, source_target_pairs={{0,1},{1,0},{2,3},{3,2},{4,5},{5,4},{6,7},{7,6},{8,9},{9,8},{10,11... | collective-permute-start | bytes 393224 | tf_op jit(solution)/shard_map/ppermute | solution.py:343
  0.5 2.6 %collective-permute-start.1 = (bf16[256,256]{1,0:T(8,128)(2,1)}, bf16[256,256]{1,0:T(8,128)(2,1)S(1)}, u32[]{:S(2)}, u32[]{:S(2)}) collective-permute-start(bf16[256,256]{1,0:T(8,128)(2,1)} %own_ref.1), channel_id=1, source_target_pairs={{0,16},{1,2},{2,1},{3,4},{4,3},{5,6},{6,5},{7,8},{8,7},{9,10},{10,... | collective-permute-start | bytes 393224 | tf_op jit(solution)/shard_map/ppermute | solution.py:343
  3.0 0.0 collective-permute-done.even_ref
  3.0 0.0 copy-done.7
  3.0 0.9 %copy-done.5 = bf16[256,512]{1,0:T(8,128)(2,1)S(1)} copy-done((bf16[256,512]{1,0:T(8,128)(2,1)S(1)}, bf16[256,512]{1,0:T(8,128)(2,1)}, u32[]{:S(2)}) %copy-start.5) | copy-done | bytes 262168
  4.0 0.9 %copy-done.6 = bf16[256,256]{1,0:T(8,128)(2,1)S(1)} copy-done((bf16[256,256]{1,0:T(8,128)(2,1)S(1)}, bf16[256,256]{1,0:T(8,128)(2,1)}, u32[]{:S(2)}) %copy-start.6) | copy-done | bytes 131096
  4.9 1.7 %own_window.1 = (s32[8,8,128]{2,1,0:T(8,128)S(1)}, bf16[8,256,128]{2,1,0:T(8,128)(2,1)S(1)}, f32[8,80,256]{2,1,0:T(8,128)S(1)}, f32[8,8,256]{2,1,0:T(8,128)S(1)}) custom-call(s32[1,8]{1,0:T(1,128)S(1)} %bitcast.1, bf16[256,512]{1,0:T(8,128)(2,1)S(1)} %copy-done.5, bf16[256,256]{1,0:T(8,128)(2,1)S(1)} %copy-done.6, ...), custom_call_target="tpu_custom_call" | custom-call | flops 4294967296 | bytes 2097152 | tf_op jit(solution)/shard_map/own_window/pallas_call | solution.py:377
  6.6 0.0 collective-permute-done.1.odd_ref
  6.6 0.0 copy-done
  6.7 0.0 copy-start.1
  6.7 1.8 %halo_window.1 = (bf16[256,1024]{1,0:T(8,128)(2,1)S(1)}, bf16[256,1024]{1,0:T(8,128)(2,1)S(1)}, bf16[256,256]{1,0:T(8,128)(2,1)S(1)}) custom-call(s32[8,8,128]{2,1,0:T(8,128)S(1)} %get-tuple-element.16.extents_ref, bf16[8,256,128]{2,1,0:T(8,128)(2,1)S(1)} %get-tuple-element.17.q_ref, bf16[256,256]{1,0:T(8,128)(2,1)S(1)} %collective-permute-done.1.odd_ref, ...), custom_call_target="tpu_custom_call" | custom-call | flops 5368709120 | bytes 2097152 | tf_op jit(solution)/shard_map/halo_window/pallas_call | solution.py:377
  8.5 0.0 copy-start.8
  8.5 0.2 collective-permute-start.5
  8.6 3.8 %collective-permute-start.2 = (bf16[256,256]{1,0:T(8,128)(2,1)S(1)}, bf16[256,256]{1,0:T(8,128)(2,1)S(1)}, u32[]{:S(2)}, u32[]{:S(2)}) collective-permute-start(bf16[256,256]{1,0:T(8,128)(2,1)S(1)} %get-tuple-element.20.refs_4_), channel_id=1, source_target_pairs={{0,8},{1,9},{2,10},{3,11},{4,12},{5,13},{6,14},{7,15},{8,0},{9,1},... | collective-permute-start | bytes 393224 | tf_op jit(solution)/shard_map/ppermute | solution.py:424
  12.4 1.6 %collective-permute-start.3 = (bf16[256,256]{1,0:T(8,128)(2,1)S(1)}, bf16[256,256]{1,0:T(8,128)(2,1)S(1)}, u32[]{:S(2)}, u32[]{:S(2)}) collective-permute-start(bf16[256,256]{1,0:T(8,128)(2,1)S(1)} %get-tuple-element.20.refs_4_), channel_id=1, source_target_pairs={{0,4},{1,5},{2,6},{3,7},{4,0},{5,1},{6,2},{7,3},{8,12},{9,13},{10,... | collective-permute-start | bytes 393224 | tf_op jit(solution)/shard_map/ppermute | solution.py:424
  14.0 0.3 %collective-permute-start.4 = (bf16[256,256]{1,0:T(8,128)(2,1)S(1)}, bf16[256,256]{1,0:T(8,128)(2,1)S(1)}, u32[]{:S(2)}, u32[]{:S(2)}) collective-permute-start(bf16[256,256]{1,0:T(8,128)(2,1)S(1)} %get-tuple-element.20.refs_4_), channel_id=1, source_target_pairs={{0,2},{1,3},{2,0},{3,1},{4,6},{5,7},{6,4},{7,5},{8,10},{9,11},{10,... | collective-permute-start | bytes 393224 | tf_op jit(solution)/shard_map/ppermute | solution.py:424
  14.4 0.0 collective-permute-done.5.refs_0_
  14.4 0.0 copy-done.8
  14.4 0.0 copy-start.2
  14.4 2.0 %own_butterfly.1 = (bf16[8,256,128]{2,1,0:T(8,128)(2,1)S(1)}, f32[8,80,256]{2,1,0:T(8,128)S(1)}, f32[8,8,256]{2,1,0:T(8,128)S(1)}, bf16[4,16,128]{2,1,0:T(8,128)(2,1)S(1)}) custom-call(bf16[256,256]{1,0:T(8,128)(2,1)S(1)} %collective-permute-done.5.refs_0_, s32[1,4]{1,0:T(1,128)S(1)} %copy-done.8, bf16[256,1024]{1,0:T(8,128)(2,1)S(1)} %get-tuple-element.21.refs_2_, ...), custom_call_target="tpu_custom_call" | custom-call | flops 6442450944 | bytes 2097152 | tf_op jit(solution)/shard_map/own_butterfly/pallas_call | solution.py:377
  16.4 2.7 %collective-permute-done.2.refs_0_ = bf16[256,256]{1,0:T(8,128)(2,1)S(1)} collective-permute-done((bf16[256,256]{1,0:T(8,128)(2,1)S(1)}, bf16[256,256]{1,0:T(8,128)(2,1)S(1)}, u32[]{:S(2)}, u32[]{:S(2)}) %collective-permute-start.2) | collective-permute-done | bytes 131104 | tf_op jit(solution)/shard_map/ppermute | solution.py:424
  19.1 0.2 collective-permute-done.3.refs_1_
  19.3 0.0 collective-permute-done.4.refs_2_
  19.3 3.4 %far_butterfly.1 = bf16[256,1024]{1,0:T(8,128)(2,1)} custom-call(bf16[256,256]{1,0:T(8,128)(2,1)S(1)} %collective-permute-done.2.refs_0_, bf16[256,256]{1,0:T(8,128)(2,1)S(1)} %collective-permute-done.3.refs_1_, bf16[256,256]{1,0:T(8,128)(2,1)S(1)} %collective-permute-done.4.refs_2_, bf16[4,16,128]{2,1,0:T(8,128)(2,1)S(1)} %get-tuple-element.22.refs_3_, ...), custom_call_target="tpu_custom_call" | custom-call | flops 8589934592 | bytes 2097152 | tf_op jit(solution)/shard_map/far_butterfly/pallas_call | solution.py:377
  (10 shorter events, 0.0 us)
Async XLA Ops:
  0.0 3.0 %copy-start.7 = (s32[8]{0:T(128)S(1)}, s32[8]{0:T(128)}, u32[]{:S(2)}) copy-start(s32[8]{0:T(128)} %param.12) | copy-start | bytes 100
  0.0 3.0 %collective-permute-start = (bf16[256,256]{1,0:T(8,128)(2,1)}, bf16[256,256]{1,0:T(8,128)(2,1)S(1)}, u32[]{:S(2)}, u32[]{:S(2)}) collective-permute-start(bf16[256,256]{1,0:T(8,128)(2,1)} %own_ref.1), channel_id=1, source_target_pairs={{0,1},{1,0},{2,3},{3,2},{4,5},{5,4},{6,7},{7,6},{8,9},{9,8},{10,11... | collective-permute-start | bytes 393224 | tf_op jit(solution)/shard_map/ppermute | solution.py:343
  0.5 6.2 %collective-permute-start.1 = (bf16[256,256]{1,0:T(8,128)(2,1)}, bf16[256,256]{1,0:T(8,128)(2,1)S(1)}, u32[]{:S(2)}, u32[]{:S(2)}) collective-permute-start(bf16[256,256]{1,0:T(8,128)(2,1)} %own_ref.1), channel_id=1, source_target_pairs={{0,16},{1,2},{2,1},{3,4},{4,3},{5,6},{6,5},{7,8},{8,7},{9,10},{10,... | collective-permute-start | bytes 393224 | tf_op jit(solution)/shard_map/ppermute | solution.py:343
  3.0 1.0 %copy-start.5 = (bf16[256,512]{1,0:T(8,128)(2,1)S(1)}, bf16[256,512]{1,0:T(8,128)(2,1)}, u32[]{:S(2)}) copy-start(bf16[256,512]{1,0:T(8,128)(2,1)} %queries_ref.1) | copy-start | bytes 786436
  4.0 0.9 %copy-start.6 = (bf16[256,256]{1,0:T(8,128)(2,1)S(1)}, bf16[256,256]{1,0:T(8,128)(2,1)}, u32[]{:S(2)}) copy-start(bf16[256,256]{1,0:T(8,128)(2,1)} %own_ref.1) | copy-start | bytes 393220
  4.9 1.8 %copy-start = (bf16[512,1024]{1,0:T(8,128)(2,1)S(1)}, bf16[512,1024]{1,0:T(8,128)(2,1)}, u32[]{:S(2)}) copy-start(bf16[512,1024]{1,0:T(8,128)(2,1)} %out_w_ref.1) | copy-start | bytes 3145732
  4.9 1.8 %copy-start.3 = (bf16[256,1024]{1,0:T(8,128)(2,1)S(1)}, bf16[256,1024]{1,0:T(8,128)(2,1)}, u32[]{:S(2)}) copy-start(bf16[256,1024]{1,0:T(8,128)(2,1)} %residual_ref.1) | copy-start | bytes 1572868
  4.9 1.8 %copy-start.4 = (bf16[1024,256]{1,0:T(8,128)(2,1)S(1)}, bf16[1024,256]{1,0:T(8,128)(2,1)}, u32[]{:S(2)}) copy-start(bf16[1024,256]{1,0:T(8,128)(2,1)} %kv_w_ref.1) | copy-start | bytes 1572868
  6.7 7.7 %copy-start.1 = (bf16[1024,512]{1,0:T(8,128)(2,1)S(1)}, bf16[1024,512]{1,0:T(8,128)(2,1)}, u32[]{:S(2)}) copy-start(bf16[1024,512]{1,0:T(8,128)(2,1)} %refs_3_.1) | copy-start | bytes 3145732
  8.5 5.9 %copy-start.8 = (s32[1,4]{1,0:T(1,128)S(1)}, s32[1,4]{1,0:T(1,128)}, u32[]{:S(2)}) copy-start(s32[1,4]{1,0:T(1,128)} %refs_1_.1) | copy-start | bytes 52
  8.5 5.9 %collective-permute-start.5 = (bf16[256,256]{1,0:T(8,128)(2,1)S(1)}, bf16[256,256]{1,0:T(8,128)(2,1)S(1)}, u32[]{:S(2)}, u32[]{:S(2)}) collective-permute-start(bf16[256,256]{1,0:T(8,128)(2,1)S(1)} %get-tuple-element.20.refs_4_), channel_id=1, source_target_pairs={{0,1},{1,0},{2,3},{3,2},{4,5},{5,4},{6,7},{7,6},{8,9},{9,8},{10,11... | collective-permute-start | bytes 393224 | tf_op jit(solution)/shard_map/ppermute | solution.py:424
  8.6 10.5 %collective-permute-start.2 = (bf16[256,256]{1,0:T(8,128)(2,1)S(1)}, bf16[256,256]{1,0:T(8,128)(2,1)S(1)}, u32[]{:S(2)}, u32[]{:S(2)}) collective-permute-start(bf16[256,256]{1,0:T(8,128)(2,1)S(1)} %get-tuple-element.20.refs_4_), channel_id=1, source_target_pairs={{0,8},{1,9},{2,10},{3,11},{4,12},{5,13},{6,14},{7,15},{8,0},{9,1},... | collective-permute-start | bytes 393224 | tf_op jit(solution)/shard_map/ppermute | solution.py:424
  12.4 6.8 %collective-permute-start.3 = (bf16[256,256]{1,0:T(8,128)(2,1)S(1)}, bf16[256,256]{1,0:T(8,128)(2,1)S(1)}, u32[]{:S(2)}, u32[]{:S(2)}) collective-permute-start(bf16[256,256]{1,0:T(8,128)(2,1)S(1)} %get-tuple-element.20.refs_4_), channel_id=1, source_target_pairs={{0,4},{1,5},{2,6},{3,7},{4,0},{5,1},{6,2},{7,3},{8,12},{9,13},{10,... | collective-permute-start | bytes 393224 | tf_op jit(solution)/shard_map/ppermute | solution.py:424
  14.0 5.3 %collective-permute-start.4 = (bf16[256,256]{1,0:T(8,128)(2,1)S(1)}, bf16[256,256]{1,0:T(8,128)(2,1)S(1)}, u32[]{:S(2)}, u32[]{:S(2)}) collective-permute-start(bf16[256,256]{1,0:T(8,128)(2,1)S(1)} %get-tuple-element.20.refs_4_), channel_id=1, source_target_pairs={{0,2},{1,3},{2,0},{3,1},{4,6},{5,7},{6,4},{7,5},{8,10},{9,11},{10,... | collective-permute-start | bytes 393224 | tf_op jit(solution)/shard_map/ppermute | solution.py:424
  14.4 4.9 %copy-start.2 = (bf16[512,1024]{1,0:T(8,128)(2,1)S(1)}, bf16[512,1024]{1,0:T(8,128)(2,1)}, u32[]{:S(2)}) copy-start(bf16[512,1024]{1,0:T(8,128)(2,1)} %refs_9_.1) | copy-start | bytes 3145732

commit v9 on v8

--- a/solution.py
+++ b/solution.py
@@ -114,11 +114,22 @@
                 one = one + prior[0][h, :, here] * scales[n]
             sink(h, here, one, tops[n])
 
-    scores = [score(*step) for step in steps[:2]]
+    if len(parts) == 1:
+        scores = [score(*step) for step in steps[:2]]
+        for n, step in enumerate(steps):
+            if n + 2 < len(steps):
+                scores.append(score(*steps[n + 2]))
+            mix(*step, *soften(*step, scores[n]))
+        return
+    scores, weights = [score(*step) for step in steps[:2]], []
     for n, step in enumerate(steps):
+        weights.append(soften(*step, scores[n]))
         if n + 2 < len(steps):
             scores.append(score(*steps[n + 2]))
-        mix(*step, *soften(*step, scores[n]))
+        if n:
+            mix(*steps[n - 1], *weights[n - 1])
+    mix(*steps[-1], *weights[-1])
+
 
 def keep_state(sums_ref, tops_ref):
     def sink(head, here, sums, top):

time: 22.9 us -> 22.8 us (level)
  no operation moved by 1% of the time
where the time goes in v9:
time: 22.8 us; the launch traced here: 22.7 us
  starting transfers between devices  8.99 us (39%)
  Pallas kernels  8.73 us (38%)
  waiting for transfers between devices  2.97 us (13%)
  local copies, waits for them, and re-layouts  1.89 us (8%)
    pallas_call x4, Pallas kernels, call(): pl.pallas_call(kernel, out_shape=out_shape, in_specs=in_specs, out_specs=...  8.73 us
    ppermute x4, starting transfers between devices, shards(): others[level] = lax.ppermute(keyvals, 'seq', route)  5.96 us
    ppermute x2, starting transfers between devices, exchange_edges(): return lax.ppermute(block, ('groups', 'seq'), route)  3.03 us
    ppermute x4, waiting for transfers between devices, shards(): others[level] = lax.ppermute(keyvals, 'seq', route)  2.97 us
    unnamed x18, local copies, waits for them, and re-layouts  1.89 us
  transfers between devices with their start and end apart: 6, of which 2 were waited for; matrix products, arithmetic and copies ran while one was open for 0% of the time, Pallas kernels for 16%

profile of v9, /device:TPU:0, one launch (start us, length us, event | category | flops | bytes accessed | tf_op | source)
XLA Modules:
  0.0 22.7 jit_solution(15988942986848429775)
XLA Ops:
  0.0 0.5 %collective-permute-start = (bf16[256,256]{1,0:T(8,128)(2,1)}, bf16[256,256]{1,0:T(8,128)(2,1)S(1)}, u32[]{:S(2)}, u32[]{:S(2)}) collective-permute-start(bf16[256,256]{1,0:T(8,128)(2,1)} %own_ref.1), channel_id=1, source_target_pairs={{0,1},{1,0},{2,3},{3,2},{4,5},{5,4},{6,7},{7,6},{8,9},{9,8},{10,11... | collective-permute-start | bytes 393224 | tf_op jit(solution)/shard_map/ppermute | solution.py:354
  0.5 2.6 %collective-permute-start.1 = (bf16[256,256]{1,0:T(8,128)(2,1)}, bf16[256,256]{1,0:T(8,128)(2,1)S(1)}, u32[]{:S(2)}, u32[]{:S(2)}) collective-permute-start(bf16[256,256]{1,0:T(8,128)(2,1)} %own_ref.1), channel_id=1, source_target_pairs={{0,16},{1,2},{2,1},{3,4},{4,3},{5,6},{6,5},{7,8},{8,7},{9,10},{10,... | collective-permute-start | bytes 393224 | tf_op jit(solution)/shard_map/ppermute | solution.py:354
  3.0 0.0 collective-permute-done.even_ref
  3.0 0.0 copy-done.7
  3.0 0.9 %copy-done.5 = bf16[256,512]{1,0:T(8,128)(2,1)S(1)} copy-done((bf16[256,512]{1,0:T(8,128)(2,1)S(1)}, bf16[256,512]{1,0:T(8,128)(2,1)}, u32[]{:S(2)}) %copy-start.5) | copy-done | bytes 262168
  4.0 0.9 %copy-done.6 = bf16[256,256]{1,0:T(8,128)(2,1)S(1)} copy-done((bf16[256,256]{1,0:T(8,128)(2,1)S(1)}, bf16[256,256]{1,0:T(8,128)(2,1)}, u32[]{:S(2)}) %copy-start.6) | copy-done | bytes 131096
  4.9 1.6 %own_window.1 = (s32[8,8,128]{2,1,0:T(8,128)S(1)}, bf16[8,256,128]{2,1,0:T(8,128)(2,1)S(1)}, f32[8,80,256]{2,1,0:T(8,128)S(1)}, f32[8,8,256]{2,1,0:T(8,128)S(1)}) custom-call(s32[1,8]{1,0:T(1,128)S(1)} %bitcast.1, bf16[256,512]{1,0:T(8,128)(2,1)S(1)} %copy-done.5, bf16[256,256]{1,0:T(8,128)(2,1)S(1)} %copy-done.6, ...), custom_call_target="tpu_custom_call" | custom-call | flops 4294967296 | bytes 2097152 | tf_op jit(solution)/shard_map/own_window/pallas_call | solution.py:388
  6.5 0.0 collective-permute-done.1.odd_ref
  6.6 0.0 copy-done
  6.6 0.0 copy-done.3
  6.6 0.0 copy-start.1
  6.6 1.7 %halo_window.1 = (bf16[256,1024]{1,0:T(8,128)(2,1)S(1)}, bf16[256,1024]{1,0:T(8,128)(2,1)S(1)}, bf16[256,256]{1,0:T(8,128)(2,1)S(1)}) custom-call(s32[8,8,128]{2,1,0:T(8,128)S(1)} %get-tuple-element.16.extents_ref, bf16[8,256,128]{2,1,0:T(8,128)(2,1)S(1)} %get-tuple-element.17.q_ref, bf16[256,256]{1,0:T(8,128)(2,1)S(1)} %collective-permute-done.1.odd_ref, ...), custom_call_target="tpu_custom_call" | custom-call | flops 5368709120 | bytes 2097152 | tf_op jit(solution)/shard_map/halo_window/pallas_call | solution.py:388
  8.3 0.0 copy-start.8
  8.3 0.2 collective-permute-start.5
  8.6 3.9 %collective-permute-start.2 = (bf16[256,256]{1,0:T(8,128)(2,1)S(1)}, bf16[256,256]{1,0:T(8,128)(2,1)S(1)}, u32[]{:S(2)}, u32[]{:S(2)}) collective-permute-start(bf16[256,256]{1,0:T(8,128)(2,1)S(1)} %get-tuple-element.20.refs_4_), channel_id=1, source_target_pairs={{0,8},{1,9},{2,10},{3,11},{4,12},{5,13},{6,14},{7,15},{8,0},{9,1},... | collective-permute-start | bytes 393224 | tf_op jit(solution)/shard_map/ppermute | solution.py:435
  12.4 1.6 %collective-permute-start.3 = (bf16[256,256]{1,0:T(8,128)(2,1)S(1)}, bf16[256,256]{1,0:T(8,128)(2,1)S(1)}, u32[]{:S(2)}, u32[]{:S(2)}) collective-permute-start(bf16[256,256]{1,0:T(8,128)(2,1)S(1)} %get-tuple-element.20.refs_4_), channel_id=1, source_target_pairs={{0,4},{1,5},{2,6},{3,7},{4,0},{5,1},{6,2},{7,3},{8,12},{9,13},{10,... | collective-permute-start | bytes 393224 | tf_op jit(solution)/shard_map/ppermute | solution.py:435
  14.0 0.3 %collective-permute-start.4 = (bf16[256,256]{1,0:T(8,128)(2,1)S(1)}, bf16[256,256]{1,0:T(8,128)(2,1)S(1)}, u32[]{:S(2)}, u32[]{:S(2)}) collective-permute-start(bf16[256,256]{1,0:T(8,128)(2,1)S(1)} %get-tuple-element.20.refs_4_), channel_id=1, source_target_pairs={{0,2},{1,3},{2,0},{3,1},{4,6},{5,7},{6,4},{7,5},{8,10},{9,11},{10,... | collective-permute-start | bytes 393224 | tf_op jit(solution)/shard_map/ppermute | solution.py:435
  14.3 0.0 collective-permute-done.5.refs_0_
  14.3 0.0 copy-start.2
  14.3 2.0 %own_butterfly.1 = (bf16[8,256,128]{2,1,0:T(8,128)(2,1)S(1)}, f32[8,80,256]{2,1,0:T(8,128)S(1)}, f32[8,8,256]{2,1,0:T(8,128)S(1)}, bf16[4,16,128]{2,1,0:T(8,128)(2,1)S(1)}) custom-call(bf16[256,256]{1,0:T(8,128)(2,1)S(1)} %collective-permute-done.5.refs_0_, s32[1,4]{1,0:T(1,128)S(1)} %copy-done.8, bf16[256,1024]{1,0:T(8,128)(2,1)S(1)} %get-tuple-element.21.refs_2_, ...), custom_call_target="tpu_custom_call" | custom-call | flops 6442450944 | bytes 2097152 | tf_op jit(solution)/shard_map/own_butterfly/pallas_call | solution.py:388
  16.3 2.8 %collective-permute-done.2.refs_0_ = bf16[256,256]{1,0:T(8,128)(2,1)S(1)} collective-permute-done((bf16[256,256]{1,0:T(8,128)(2,1)S(1)}, bf16[256,256]{1,0:T(8,128)(2,1)S(1)}, u32[]{:S(2)}, u32[]{:S(2)}) %collective-permute-start.2) | collective-permute-done | bytes 131104 | tf_op jit(solution)/shard_map/ppermute | solution.py:435
  19.1 0.2 collective-permute-done.3.refs_1_
  19.3 0.0 collective-permute-done.4.refs_2_
  19.3 3.4 %far_butterfly.1 = bf16[256,1024]{1,0:T(8,128)(2,1)} custom-call(bf16[256,256]{1,0:T(8,128)(2,1)S(1)} %collective-permute-done.2.refs_0_, bf16[256,256]{1,0:T(8,128)(2,1)S(1)} %collective-permute-done.3.refs_1_, bf16[256,256]{1,0:T(8,128)(2,1)S(1)} %collective-permute-done.4.refs_2_, bf16[4,16,128]{2,1,0:T(8,128)(2,1)S(1)} %get-tuple-element.22.refs_3_, ...), custom_call_target="tpu_custom_call" | custom-call | flops 8589934592 | bytes 2097152 | tf_op jit(solution)/shard_map/far_butterfly/pallas_call | solution.py:388
  (10 shorter events, 0.0 us)
Async XLA Ops:
  0.0 3.0 %copy-start.7 = (s32[8]{0:T(128)S(1)}, s32[8]{0:T(128)}, u32[]{:S(2)}) copy-start(s32[8]{0:T(128)} %param.12) | copy-start | bytes 100
  0.0 3.0 %collective-permute-start = (bf16[256,256]{1,0:T(8,128)(2,1)}, bf16[256,256]{1,0:T(8,128)(2,1)S(1)}, u32[]{:S(2)}, u32[]{:S(2)}) collective-permute-start(bf16[256,256]{1,0:T(8,128)(2,1)} %own_ref.1), channel_id=1, source_target_pairs={{0,1},{1,0},{2,3},{3,2},{4,5},{5,4},{6,7},{7,6},{8,9},{9,8},{10,11... | collective-permute-start | bytes 393224 | tf_op jit(solution)/shard_map/ppermute | solution.py:354
  0.5 6.1 %collective-permute-start.1 = (bf16[256,256]{1,0:T(8,128)(2,1)}, bf16[256,256]{1,0:T(8,128)(2,1)S(1)}, u32[]{:S(2)}, u32[]{:S(2)}) collective-permute-start(bf16[256,256]{1,0:T(8,128)(2,1)} %own_ref.1), channel_id=1, source_target_pairs={{0,16},{1,2},{2,1},{3,4},{4,3},{5,6},{6,5},{7,8},{8,7},{9,10},{10,... | collective-permute-start | bytes 393224 | tf_op jit(solution)/shard_map/ppermute | solution.py:354
  3.0 1.0 %copy-start.5 = (bf16[256,512]{1,0:T(8,128)(2,1)S(1)}, bf16[256,512]{1,0:T(8,128)(2,1)}, u32[]{:S(2)}) copy-start(bf16[256,512]{1,0:T(8,128)(2,1)} %queries_ref.1) | copy-start | bytes 786436
  4.0 0.9 %copy-start.6 = (bf16[256,256]{1,0:T(8,128)(2,1)S(1)}, bf16[256,256]{1,0:T(8,128)(2,1)}, u32[]{:S(2)}) copy-start(bf16[256,256]{1,0:T(8,128)(2,1)} %own_ref.1) | copy-start | bytes 393220
  4.9 1.7 %copy-start = (bf16[512,1024]{1,0:T(8,128)(2,1)S(1)}, bf16[512,1024]{1,0:T(8,128)(2,1)}, u32[]{:S(2)}) copy-start(bf16[512,1024]{1,0:T(8,128)(2,1)} %out_w_ref.1) | copy-start | bytes 3145732
  4.9 1.7 %copy-start.3 = (bf16[256,1024]{1,0:T(8,128)(2,1)S(1)}, bf16[256,1024]{1,0:T(8,128)(2,1)}, u32[]{:S(2)}) copy-start(bf16[256,1024]{1,0:T(8,128)(2,1)} %residual_ref.1) | copy-start | bytes 1572868
  4.9 1.7 %copy-start.4 = (bf16[1024,256]{1,0:T(8,128)(2,1)S(1)}, bf16[1024,256]{1,0:T(8,128)(2,1)}, u32[]{:S(2)}) copy-start(bf16[1024,256]{1,0:T(8,128)(2,1)} %kv_w_ref.1) | copy-start | bytes 1572868
  6.6 7.7 %copy-start.1 = (bf16[1024,512]{1,0:T(8,128)(2,1)S(1)}, bf16[1024,512]{1,0:T(8,128)(2,1)}, u32[]{:S(2)}) copy-start(bf16[1024,512]{1,0:T(8,128)(2,1)} %refs_3_.1) | copy-start | bytes 3145732
  8.3 6.0 %copy-start.8 = (s32[1,4]{1,0:T(1,128)S(1)}, s32[1,4]{1,0:T(1,128)}, u32[]{:S(2)}) copy-start(s32[1,4]{1,0:T(1,128)} %refs_1_.1) | copy-start | bytes 52
  8.3 6.0 %collective-permute-start.5 = (bf16[256,256]{1,0:T(8,128)(2,1)S(1)}, bf16[256,256]{1,0:T(8,128)(2,1)S(1)}, u32[]{:S(2)}, u32[]{:S(2)}) collective-permute-start(bf16[256,256]{1,0:T(8,128)(2,1)S(1)} %get-tuple-element.20.refs_4_), channel_id=1, source_target_pairs={{0,1},{1,0},{2,3},{3,2},{4,5},{5,4},{6,7},{7,6},{8,9},{9,8},{10,11... | collective-permute-start | bytes 393224 | tf_op jit(solution)/shard_map/ppermute | solution.py:435
  8.6 10.5 %collective-permute-start.2 = (bf16[256,256]{1,0:T(8,128)(2,1)S(1)}, bf16[256,256]{1,0:T(8,128)(2,1)S(1)}, u32[]{:S(2)}, u32[]{:S(2)}) collective-permute-start(bf16[256,256]{1,0:T(8,128)(2,1)S(1)} %get-tuple-element.20.refs_4_), channel_id=1, source_target_pairs={{0,8},{1,9},{2,10},{3,11},{4,12},{5,13},{6,14},{7,15},{8,0},{9,1},... | collective-permute-start | bytes 393224 | tf_op jit(solution)/shard_map/ppermute | solution.py:435
  12.4 6.8 %collective-permute-start.3 = (bf16[256,256]{1,0:T(8,128)(2,1)S(1)}, bf16[256,256]{1,0:T(8,128)(2,1)S(1)}, u32[]{:S(2)}, u32[]{:S(2)}) collective-permute-start(bf16[256,256]{1,0:T(8,128)(2,1)S(1)} %get-tuple-element.20.refs_4_), channel_id=1, source_target_pairs={{0,4},{1,5},{2,6},{3,7},{4,0},{5,1},{6,2},{7,3},{8,12},{9,13},{10,... | collective-permute-start | bytes 393224 | tf_op jit(solution)/shard_map/ppermute | solution.py:435
  14.0 5.3 %collective-permute-start.4 = (bf16[256,256]{1,0:T(8,128)(2,1)S(1)}, bf16[256,256]{1,0:T(8,128)(2,1)S(1)}, u32[]{:S(2)}, u32[]{:S(2)}) collective-permute-start(bf16[256,256]{1,0:T(8,128)(2,1)S(1)} %get-tuple-element.20.refs_4_), channel_id=1, source_target_pairs={{0,2},{1,3},{2,0},{3,1},{4,6},{5,7},{6,4},{7,5},{8,10},{9,11},{10,... | collective-permute-start | bytes 393224 | tf_op jit(solution)/shard_map/ppermute | solution.py:435
  14.3 5.0 %copy-start.2 = (bf16[512,1024]{1,0:T(8,128)(2,1)S(1)}, bf16[512,1024]{1,0:T(8,128)(2,1)}, u32[]{:S(2)}) copy-start(bf16[512,1024]{1,0:T(8,128)(2,1)} %refs_9_.1) | copy-start | bytes 3145732
